TPU v7x, 256 devices: a whole 4x4x8 slice. The times are simulated.
256 devices in a mesh: row: 8 (over x, core), col: 8 (over y, z_hi), band: 4 (over z_lo).
Axes of the slice: x: 4, y: 4, z: 8 (z_hi: 2, z_lo: 4; z = z_hi * 4 + z_lo), core: 2. Of those that a mesh axis runs over, the one named last changes fastest.
Arguments:
- frames: bfloat16 [512, 128, 2, 1024], P(('row', 'col'), 'band'), may hold values from -6 to 6
- tail_frames: bfloat16 [512, 15, 2, 1024], P(('row', 'col')), may hold values from -6 to 6
- prototype: float32 [16, 1024], replicated, may hold values from -1.5 to 1.5
Outputs:
- visibility: float32 [512, 8, 64, 2, 1024], P('row', 'col', None, None, 'band')
All inputs are finite; a program needn't handle non-finite values.
Results may differ from a plain program's by a relative error of at most 0.0059.
Values may be sent and summed in bfloat16 or wider, within the bound.
No kernel may reach another device: no remote copies, remote signals or barrier semaphores. Data moves between devices by JAX's collectives and lax.ppermute only.
A program may use at most 128 MiB of HBM per device.

v0:
```python
import math

import jax
import jax.numpy as jnp
from jax import lax
from jax.sharding import PartitionSpec as P


def from_behind(value, axis, steps):
    count = lax.axis_size(axis)
    initial, last = (max(0, -steps), min(count, count - steps))
    return lax.ppermute(value, axis, [(source, source + steps) for source in range(initial, last)])


def dft_table(n_chan, output_part):
    sample = jnp.arange(n_chan, dtype=jnp.int32)[:, None]
    channel = jnp.arange(n_chan, dtype=jnp.int32)[None, :]
    theta = 2.0 * math.pi / n_chan * (sample * channel % n_chan).astype(jnp.float32)
    cosine = jnp.cos(theta)
    sine = jnp.sin(theta)
    if output_part == 0:
        return jnp.concatenate([cosine, sine], 0).astype(jnp.bfloat16)
    return jnp.concatenate([-sine, cosine], 0).astype(jnp.bfloat16)


def polyphase(extended, coeffs, count):
    summed = jnp.zeros(extended.shape[:1] + (count,) + extended.shape[2:], jnp.float32)
    for tap in range(coeffs.shape[0]):
        summed = summed + coeffs[tap][None, None, None, :] * extended[:, tap : tap + count].astype(
            jnp.float32
        )
    return summed.astype(jnp.bfloat16)


def transform(filtered, n_chan, norm_scale):
    halves = [
        jnp.dot(filtered, dft_table(n_chan, part), preferred_element_type=jnp.float32)
        for part in range(2)
    ]
    return (jnp.concatenate(halves, 1) * norm_scale).astype(jnp.bfloat16)


def shards(frames, tail_frames, prototype):
    n_chan = frames.shape[3]
    group_inputs = frames.shape[0]
    taps = prototype.shape[0]
    bands = lax.axis_size("band")
    norm_scale = 1.0 / math.sqrt(n_chan)
    leading = frames[:, : taps - 1]
    following = from_behind(leading, "band", -1)
    is_last = lax.axis_index("band") == bands - 1
    following = jnp.where(is_last, tail_frames, following)
    extended = jnp.concatenate([frames, following], 1)
    local_spec = frames.shape[1]
    filtered = polyphase(extended, prototype, local_spec).reshape(
        group_inputs * local_spec, 2 * n_chan
    )
    spectra = transform(filtered, n_chan, norm_scale).reshape(group_inputs, local_spec, 2, n_chan)
    turned = lax.all_to_all(spectra, "band", split_axis=3, concat_axis=1, tiled=True)
    first_block = lax.all_gather(turned, "col", axis=0, tiled=True)
    spectra_count = turned.shape[1]
    outer = jnp.einsum(
        "ascn,bsdn->abcdn",
        first_block,
        lax.all_gather(turned, "row", axis=0, tiled=True),
        preferred_element_type=jnp.float32,
    )
    real_part = outer[:, :, 0, 0] + outer[:, :, 1, 1]
    imag_part = outer[:, :, 1, 0] - outer[:, :, 0, 1]
    return (jnp.stack([real_part, imag_part], 2) * (1.0 / spectra_count))[:, None]


def solution(mesh):
    placed = (P(("row", "col"), "band", None, None), P(("row", "col"), None, None, None), P())
    return jax.shard_map(
        shards,
        mesh=mesh,
        in_specs=placed,
        out_specs=P("row", "col", None, None, "band"),
        check_vma=False,
    )
```

profile of v0, /device:TPU:2, one launch (start us, length us, event | category | flops | bytes accessed | tf_op | source)
XLA Modules:
  0.0 445.7 jit_solution(10079292080039003588)
XLA Ops:
  6.5 0.0 copy-start.2
  6.5 0.0 all-gather.3.cloned.1.call-start
  6.5 1.4 slice.110
  7.9 1.3 collective-permute-start
  9.2 15.7 %fusion.21 = bf16[1024,1024]{1,0:T(8,128)(2,1)S(1)} fusion(), kind=kLoop, calls=%fused_computation.30 | loop fusion | flops 15728640 | bytes 2097152 | tf_op jit(solution)/shard_map/convert.3
  24.9 0.0 copy-done.2
  25.0 0.0 copy-start.1
  25.0 0.0 copy-start
  25.0 17.0 %negate_convert_fusion = (bf16[1024,1024]{1,0:T(8,128)(2,1)S(1)}, bf16[1024,1024]{1,0:T(8,128)(2,1)S(1)}) fusion(), kind=kLoop, calls=%fused_computation.22 | loop fusion | flops 17825792 | bytes 4194304 | tf_op jit(solution)/shard_map/convert
  42.1 0.0 collective-permute-done
  42.1 0.0 copy-done.1
  42.1 0.5 broadcast_select_fusion
  42.6 0.0 copy-done
  42.6 18.8 %add_convert_fusion = bf16[8,32,2,1024]{3,2,1,0:T(2,128)(2,1)S(1)} fusion(bf16[8,32,2,1024]{3,2,1,0:T(2,128)(2,1)S(1)} %copy-done, bf16[8,15,2,1024]{3,2,1,0:T(2,128)(2,1)S(1)} %broadcast_select_fusion, f32[1024]{0:T(1024)S(1)} %bitcast.65, f32[1024]{0:T(1024)S(1)} %bitcast.66, f32[1024]{0:T(1024)S(1)} %bitcast.52, f32[1024]{0:T(1024)S(1)} %bitcast.53, ...), kind=kLoop, calls=%fused_computation.31 | loop fusion | flops 33030144 | bytes 2654208 | tf_op jit(solution)/shard_map/convert_element_type | solution.py:32
  61.4 0.3 copy.39
  61.7 1.2 fusion.8
  63.0 1.2 fusion.12
  64.2 0.2 fusion.19
  64.4 0.8 convert_element_type.89
  65.2 7.7 %copy.28 = bf16[8,32,2,1024]{1,2,0,3:T(2,128)(2,1)} copy(bf16[8,32,2,1024]{3,2,1,0:T(2,128)(2,1)S(1)} %convert_element_type.89) | data formatting | bytes 2097152 | tf_op jit(solution)/shard_map/convert_element_type | solution.py:40
  72.9 5.6 %reshape.106 = bf16[4,2,65536]{2,1,0:T(2,128)(2,1)S(1)} reshape(bf16[1024,8,2,32]{3,2,1,0:T(2,128)(2,1)} %bitcast.44) | data formatting | bytes 2097152
  78.5 31.9 %all_to_all.18 = bf16[4,2,65536]{2,1,0:T(2,128)(2,1)S(1)} all-to-all(bf16[4,2,65536]{2,1,0:T(2,128)(2,1)S(1)} %reshape.106), channel_id=1, replica_groups=mesh['row'=8,'col'=8,'band'=4] {'band'}, dimensions={0} | all-to-all | bytes 2097152 | tf_op jit(solution)/shard_map/all_to_all | solution.py:59
  110.4 3.5 reshape.107
  113.8 9.8 %copy.38 = bf16[8,32,2,4,256]{4,3,1,2,0:T(4,128)(2,1)S(1)} copy(bf16[8,32,2,4,256]{1,2,0,4,3:T(2,128)(2,1)} %bitcast.45) | data formatting | bytes 2097152 | tf_op jit(solution)/shard_map/all_to_all | solution.py:59
  123.6 0.2 copy.30
  123.8 1.8 copy.31
  125.6 0.0 all-gather.3.cloned.1.call-update
  125.6 0.2 all-gather.5.cloned.1.call-start
  125.9 0.5 all-gather.5.cloned.1.call-update
  126.4 57.0 %all-gather.3.cloned.1.call-done = bf16[64,128,2,256]{1,0,2,3:T(8,128)(2,1)} async-done(((bf16[8,128,2,256]{1,0,2,3:T(8,128)(2,1)}), bf16[64,128,2,256]{1,0,2,3:T(8,128)(2,1)}) %all-gather.3.cloned.1.call-update) | async-done | bytes 8388624 | tf_op jit(solution)/shard_map/all_gather | solution.py:65
  183.4 186.3 %all-gather.5.cloned.1.call-done = bf16[64,128,2,256]{1,0,2,3:T(8,128)(2,1)} async-done(((bf16[8,128,2,256]{1,0,2,3:T(8,128)(2,1)}), bf16[64,128,2,256]{1,0,2,3:T(8,128)(2,1)}) %all-gather.5.cloned.1.call-update) | async-done | bytes 8388624 | tf_op jit(solution)/shard_map/all_gather | solution.py:60
  369.7 18.8 %fusion = f32[256,64,2,64,2]{3,1,4,2,0:T(8,128)} fusion(bf16[64,128,2,256]{1,0,2,3:T(8,128)(2,1)} %all-gather.5.cloned.1.call-done, bf16[64,128,2,256]{1,0,2,3:T(8,128)(2,1)} %all-gather.3.cloned.1.call-done), kind=kOutput, calls=%fused_computation.1 | convolution fusion | flops 1073741824 | bytes 33554432 | tf_op jit(solution)/shard_map/ascn,bsdn->abcdn/dot_general | solution.py:62
  388.5 29.4 %copy.33 = f32[256,64,2,64,2]{0,1,3,2,4:T(8,128)} copy(f32[256,64,2,64,2]{3,1,4,2,0:T(8,128)} %fusion) | data formatting | bytes 33554432 | tf_op jit(solution)/shard_map/ascn,bsdn->abcdn/dot_general | solution.py:62
  417.9 10.2 %fusion.7 = (f32[64,1,64,1,256]{4,2,3,1,0:T(8,128)S(1)}, f32[64,1,64,1,256]{4,2,3,1,0:T(8,128)}) fusion(f32[64,64,2,2,256]{4,1,0,3,2:T(8,128)} %bitcast.43), kind=kLoop, calls=%fused_computation.13 | loop fusion | flops 2097152 | bytes 25165824 | tf_op jit(solution)/shard_map/stack | solution.py:70
  428.1 3.1 maximum_multiply_fusion
  431.3 7.6 %copy.35 = f32[64,1,64,2,256]{4,3,2,1,0:T(2,128)} copy(f32[64,1,64,2,256]{4,2,3,1,0:T(8,128)S(1)} %maximum_multiply_fusion) | data formatting | bytes 16777216 | tf_op jit(solution)/shard_map/mul | solution.py:70
  (1 shorter events, 0.0 us)
Async XLA Ops:
  6.5 18.4 %copy-start.2 = (f32[16,1024]{1,0:T(8,128)S(1)}, f32[16,1024]{1,0:T(8,128)}, u32[]{:S(2)}) copy-start(f32[16,1024]{1,0:T(8,128)} %param.5) | copy-start | bytes 196612
  6.5 176.9 %all-gather.3.cloned.1.call-start = ((), (), s32[]{:S(2)}) async-start(), calls=%async_computation.1 | async-start | bytes 9437184 | tf_op jit(solution)/shard_map/all_gather | solution.py:65
  7.9 34.1 %collective-permute-start = (bf16[8,15,2,1024]{3,2,1,0:T(2,128)(2,1)S(1)}, bf16[8,15,2,1024]{3,2,1,0:T(2,128)(2,1)S(1)}, u32[]{:S(2)}, u32[]{:S(2)}) collective-permute-start(bf16[8,15,2,1024]{3,2,1,0:T(2,128)(2,1)S(1)} %slice.110), channel_id=1, source_target_pairs={{1,0},{2,1},{3,2},{5,4},{6,5},{7,6},{9,8},{10,9},{11,10},{13,12},{... | collective-permute-start | bytes 1474568 | tf_op jit(solution)/shard_map/ppermute | solution.py:12
  25.0 17.1 %copy-start.1 = (bf16[8,15,2,1024]{3,2,1,0:T(2,128)(2,1)S(1)}, bf16[8,15,2,1024]{3,2,1,0:T(2,128)(2,1)}, u32[]{:S(2)}) copy-start(bf16[8,15,2,1024]{3,2,1,0:T(2,128)(2,1)} %param.4) | copy-start | bytes 1474564
  25.0 17.6 %copy-start = (bf16[8,32,2,1024]{3,2,1,0:T(2,128)(2,1)S(1)}, bf16[8,32,2,1024]{3,2,1,0:T(2,128)(2,1)}, u32[]{:S(2)}) copy-start(bf16[8,32,2,1024]{3,2,1,0:T(2,128)(2,1)} %param.3) | copy-start | bytes 3145732
  125.6 244.1 %all-gather.5.cloned.1.call-start = ((), (), s32[]{:S(2)}) async-start(), calls=%async_computation.2 | async-start | bytes 9437184 | tf_op jit(solution)/shard_map/all_gather | solution.py:60
Sparse Core Ops, SparseCore 0:
  125.8 57.5 all-gather.2
  185.9 183.8 all-gather.4
where the time goes:
time: 447 us; the launch traced here: 446 us
  waiting for transfers between devices  244 us (55%)
  local copies, waits for them, and re-layouts  68.1 us (15%)
  other arithmetic  65.5 us (15%)
  blocking collectives  31.9 us (7%)
  matrix products  21.3 us (5%)
  between operations  13.6 us (3%)
    all_gather x1, waiting for transfers between devices, shards(): first_block = lax.all_gather(turned, 'col', axis=0, tiled=True)  186 us
    all_gather x1, waiting for transfers between devices, shards(): lax.all_gather(turned, 'row', axis=0, tiled=True)  57 us
    another operation x2, other arithmetic  32.7 us
    all_to_all x1, blocking collectives, shards(): lax.all_to_all(spectra, 'band', split_axis=3, concat_axis=1, tiled=True)  31.9 us
    dot_general x1, local copies, waits for them, and re-layouts, shards(): jnp.einsum('ascn,bsdn->abcdn', first_block, lax.all_gather(turned, 'row',...  29.4 us
    convert_element_type x1, other arithmetic, polyphase(): return summed.astype(jnp.bfloat16)  18.8 us
    dot_general x1, matrix products, shards(): jnp.einsum('ascn,bsdn->abcdn', first_block, lax.all_gather(turned, 'row',...  18.8 us
    all_to_all x3, local copies, waits for them, and re-layouts, shards(): lax.all_to_all(spectra, 'band', split_axis=3, concat_axis=1, tiled=True)  11.8 us
  transfers between devices with their start and end apart: 3, of which 2 were waited for; matrix products, arithmetic and copies ran while one was open for 7% of the time, Pallas kernels for 0%

commit v1 on v0

v1 whole, which is shorter than its diff:
```python
import functools
import math

import jax
import jax.numpy as jnp
import numpy as np
from jax import lax
from jax.experimental import pallas as pl
from jax.experimental.pallas import tpu as pltpu
from jax.sharding import Mesh
from jax.sharding import PartitionSpec as P

LANES = 128
TAPS = 16
HALF = 16
INPUTS = 8
BANDS = 4
CHAN = 1024
VMEM_LIMIT = 48 * 1024 * 1024


def dft_table():
    sample = np.arange(CHAN, dtype=np.int64)[:, None]
    channel = np.arange(CHAN, dtype=np.int64)[None, :]
    theta = np.float32(2.0 * math.pi / CHAN) * (sample * channel % CHAN).astype(np.float32)
    parts = []
    for trig in (np.cos, np.sin):
        full = trig(theta.astype(np.float64)).astype(np.float32)
        parts.append(full.reshape(CHAN, BANDS, 2, LANES))
    table = np.stack(parts)
    table = table.transpose(3, 1, 0, 2, 4).reshape(2, CHAN, 2 * BANDS * LANES)
    return jnp.asarray(table, dtype=jnp.bfloat16)


def filter_transform_kernel(late, *refs):
    if late:
        flag_ref, first_ref, recv_ref, tail_ref, coeff_ref, table_ref, out0, out1, sums, lhs = refs
    else:
        first_ref, coeff_ref, table_ref, out0, out1, sums, lhs = refs
    tiles = CHAN // LANES

    def frame(a, t):
        if t < HALF:
            return first_ref[a, t].astype(jnp.float32)
        if not late:
            return first_ref[a, t].astype(jnp.float32)
        t -= HALF
        last = flag_ref[0] == 1
        return jnp.where(last, tail_ref[a, t], recv_ref[a, t]).astype(jnp.float32)

    def one_input(a, carry):
        acc = [None] * HALF
        for t in range(HALF + TAPS - 1):
            value = frame(a, t)
            for s in range(max(0, t - TAPS + 1), min(HALF, t + 1)):
                term = coeff_ref[t - s] * value
                acc[s] = term if acc[s] is None else acc[s] + term
        for s in range(HALF):
            sums[pl.ds(s * 16, 16), :] = acc[s]
        for k in range(tiles):
            for c in range(2):
                rows = sums[pl.ds(2 * k + c, HALF, 16), :]
                start = pl.multiple_of((a * 2 + c) * HALF, HALF)
                lhs[pl.ds(start, HALF), k * LANES : (k + 1) * LANES] = rows.astype(jnp.bfloat16)
        return carry

    lax.fori_loop(0, INPUTS, one_input, 0)
    scale = 1.0 / math.sqrt(CHAN)
    width = BANDS * LANES
    for half, out in enumerate((out0, out1)):
        both = jnp.dot(lhs[...], table_ref[half], preferred_element_type=jnp.float32)
        both = both.reshape(INPUTS, 2, HALF, 2 * width)
        real = (both[:, 0, :, :width] + both[:, 1, :, width:]) * scale
        imag = (both[:, 1, :, :width] - both[:, 0, :, width:]) * scale
        for band in range(BANDS):
            cols = slice(band * LANES, (band + 1) * LANES)
            for part, value in enumerate((real, imag)):
                value = value[:, :, cols].astype(jnp.bfloat16)
                out[band, :, part] = value
                out[band + BANDS, :, part] = value


def filter_transform(late, coeff, table, first, recv=None, tail=None, flag=None):
    block = jax.ShapeDtypeStruct((2 * BANDS, INPUTS, 2, HALF, LANES), jnp.bfloat16)
    vmem = pl.BlockSpec(memory_space=pltpu.VMEM)
    if late:
        args = (flag, first, recv, tail, coeff, table)
        in_specs = [pl.BlockSpec(memory_space=pltpu.SMEM)]
        in_specs += [pl.BlockSpec((INPUTS, HALF, 16, LANES), lambda i: (0, 1, 0, 0))]
        in_specs += [vmem] * 4
    else:
        args = (first, coeff, table)
        in_specs = [vmem] * 3
    return pl.pallas_call(
        functools.partial(filter_transform_kernel, late),
        out_shape=(block, block),
        grid=(1,),
        in_specs=in_specs,
        out_specs=(vmem, vmem),
        scratch_shapes=[
            pltpu.VMEM((HALF * 16, LANES), jnp.float32),
            pltpu.VMEM((INPUTS * 2 * HALF, CHAN), jnp.bfloat16),
        ],
        compiler_params=pltpu.CompilerParams(vmem_limit_bytes=VMEM_LIMIT),
        cost_estimate=pl.CostEstimate(
            flops=2 * 2 * 256 * CHAN * CHAN, bytes_accessed=8 << 20, transcendentals=0
        ),
        name="filter_transform",
    )(*args)


def turn_kernel(group_ref, recv_ref, out_ref, own_ref, rows):
    for high in range(2):
        for a in range(INPUTS):
            pieces = [recv_ref[high * BANDS + low, a, c] for c in range(2) for low in range(BANDS)]
            block = jnp.concatenate(pieces, 0).astype(jnp.float32)
            rows[pl.ds(high * INPUTS + a, LANES, 16), :] = block.T
    start = pl.multiple_of(group_ref[0] * INPUTS, INPUTS)

    def one(n, carry):
        base = pl.multiple_of(n * 16, 16)
        out_ref[n] = rows[pl.ds(base, 16), :].astype(jnp.bfloat16)
        mine = pl.multiple_of(base + start, 8)
        own_ref[n] = rows[pl.ds(mine, INPUTS), :].astype(jnp.bfloat16)
        return carry

    lax.fori_loop(0, LANES, one, 0, unroll=8)


def turn(group, recv):
    vmem = pl.BlockSpec(memory_space=pltpu.VMEM)
    return pl.pallas_call(
        turn_kernel,
        out_shape=(
            jax.ShapeDtypeStruct((LANES, 2 * INPUTS, LANES), jnp.bfloat16),
            jax.ShapeDtypeStruct((LANES, INPUTS, LANES), jnp.bfloat16),
        ),
        in_specs=[pl.BlockSpec(memory_space=pltpu.SMEM), vmem],
        out_specs=(vmem, vmem),
        scratch_shapes=[pltpu.VMEM((LANES * 16, LANES), jnp.float32)],
        compiler_params=pltpu.CompilerParams(vmem_limit_bytes=VMEM_LIMIT),
        cost_estimate=pl.CostEstimate(flops=1 << 20, bytes_accessed=2 << 20, transcendentals=0),
        name="turn",
    )(group, recv)


ROWS = 64
N_PIECE = 11


def correlate_kernel(half, spectra, place_ref, *refs):
    early, late = refs[:N_PIECE], refs[N_PIECE : 2 * N_PIECE]
    out_ref, outer, mixed = refs[-3:]
    step = pl.program_id(0)
    sign = jnp.where(lax.broadcasted_iota(jnp.int32, (ROWS, LANES), 1) < LANES // 2, -1.0, 1.0)

    first_core = place_ref[9] == 0

    def multiply(second, n):
        m = n + second * (LANES // 2)
        left, right = [], []
        for own, below, above, far0, far1, own8, sib8, got, got2, swap, swap2 in (early, late):
            far = far1 if second else far0
            left.append(jnp.concatenate([own[m], above[m], far[n], below[m]], 0))
            pieces = [own8[m], sib8[m], got[0, m], got[1, m], swap[0, m], swap[1, m]]
            came, other = (swap2, got2) if second else (got2, swap2)
            for i in (1, 0) if second else (0, 1):
                pieces.append(jnp.where(first_core, came[i, n], other[i, n]))
            right.append(jnp.concatenate([p.astype(jnp.float32) for p in pieces], 0))
        lhs = jnp.concatenate(left, 1)
        turned = [pltpu.roll(r, LANES // 2, 1) * sign for r in right]
        rhs = jnp.concatenate([jnp.concatenate(right, 1), jnp.concatenate(turned, 1)], 0)
        value = lax.dot_general(
            lhs,
            rhs.astype(jnp.bfloat16),
            (((1,), (1,)), ((), ())),
            preferred_element_type=jnp.float32,
        )
        outer[pl.ds(pl.multiple_of(m * ROWS, ROWS), ROWS), :] = value

    @pl.when(step == 0)
    def _():
        for second in range(2):

            def one(n, carry):
                multiply(second, n)
                return carry

            lax.fori_loop(0, LANES // 2, one, 0, unroll=4)

    my_y = place_ref[0]
    slot = lax.rem(step - my_y + 4, 4)

    def write(i, carry):
        column = slot * 16 + i
        block = outer[pl.ds(column, LANES, ROWS), :].T * (1.0 / spectra)
        for r in range(8):
            target = place_ref[1 + r] * 16
            for part in range(2):
                mixed[pl.ds(target + part, 8, 2), :] = block[part * 64 + r * 8 : part * 64 + r * 8 + 8]
        out_ref[i, 0] = mixed[...].reshape(ROWS, 2, LANES)
        return carry

    lax.fori_loop(0, 16, write, 0, unroll=2)


def correlate(half, spectra, place, early, late, previous):
    vmem = pl.BlockSpec(memory_space=pltpu.VMEM)
    smem = pl.BlockSpec(memory_space=pltpu.SMEM)
    extra, aliases = (), {}
    kernel = functools.partial(correlate_kernel, half, spectra)
    if previous is not None:
        extra, aliases = (previous,), {1 + 2 * N_PIECE: 0}

        def kernel(*refs):
            refs = refs[: 1 + 2 * N_PIECE] + refs[2 + 2 * N_PIECE :]
            correlate_kernel(half, spectra, *refs)

    return pl.pallas_call(
        kernel,
        out_shape=jax.ShapeDtypeStruct((64, 1, 64, 2, 256), jnp.float32),
        grid=(4,),
        in_specs=[smem] + [vmem] * (2 * N_PIECE) + [pl.BlockSpec(memory_space=pl.ANY)] * len(extra),
        out_specs=pl.BlockSpec((16, 1, 64, 2, LANES), lambda i: (i, 0, 0, 0, half)),
        scratch_shapes=[
            pltpu.VMEM((LANES * ROWS, LANES), jnp.float32),
            pltpu.VMEM((LANES, LANES), jnp.float32),
        ],
        input_output_aliases=aliases,
        compiler_params=pltpu.CompilerParams(vmem_limit_bytes=VMEM_LIMIT),
        cost_estimate=pl.CostEstimate(
            flops=2 * 64 * 128 * 256 * 128, bytes_accessed=12 << 20, transcendentals=0
        ),
        name="correlate",
    )(place, *early, *late, *extra)


def ring(value, axis, step):
    count = lax.axis_size(axis)
    return lax.ppermute(value, axis, [(i, (i + step) % count) for i in range(count)])


def spread(own, own8):
    x_size = 4
    below = ring(own, "y", 1)
    above = ring(own, "y", -1)
    sib8 = ring(own8, "core", 1)
    pair = jnp.stack([own8, sib8])
    swing = []
    for x in range(x_size):
        swing.append((2 * x, 2 * ((x + 1) % x_size)))
        swing.append((2 * x + 1, 2 * ((x - 1) % x_size) + 1))
    got = lax.ppermute(pair, ("x", "core"), swing)
    core = lax.axis_index("core")
    part = lax.dynamic_slice_in_dim(got, core * 64, 64, 1)
    got2 = lax.ppermute(part, ("x", "core"), swing)
    far0 = ring(below[:64], "y", 1)
    far1 = ring(above[64:], "y", -1)
    swap = ring(got, "core", 1)
    swap2 = ring(got2, "core", 1)
    return own, below, above, far0, far1, own8, sib8, got, got2, swap, swap2


def shards(frames, tail_frames, prototype):
    spectra = 128
    coeff = jnp.repeat(prototype.reshape(TAPS, CHAN // LANES, LANES), 2, axis=1)
    table = dft_table()

    def words(value):
        shape = value.shape[:2]
        value = value.reshape(shape + (2, CHAN // LANES, LANES)).transpose(0, 1, 3, 2, 4)
        return value.reshape(shape + (16, LANES))

    mine, tail = words(frames), words(tail_frames)
    bands = lax.axis_size("zl")
    following = lax.ppermute(mine[:, : TAPS - 1], "zl", [(b + 1, b) for b in range(bands - 1)])
    is_last = (lax.axis_index("zl") == bands - 1).astype(jnp.int32).reshape(1)
    group = lax.axis_index("zh").reshape(1)
    my_x, my_core = lax.axis_index("x"), lax.axis_index("core")
    toward = 1 - 2 * my_core
    near = lax.rem(my_x - toward + 4, 4)
    other = lax.rem(my_x + toward + 4, 4)
    far = lax.rem(my_x + 2, 4)
    rest = 1 - my_core
    order = [
        2 * my_x + my_core,
        2 * my_x + rest,
        2 * near + my_core,
        2 * near + rest,
        2 * other + rest,
        2 * other + my_core,
    ]
    place = jnp.stack([lax.axis_index("y"), *order, 2 * far, 2 * far + 1, my_core]).astype(jnp.int32)

    early = filter_transform(False, coeff, table, mine)
    late = filter_transform(True, coeff, table, mine, following, tail, is_last)
    out = None
    for half in range(2):
        pieces = []
        for source in (early, late):
            recv = lax.all_to_all(source[half], ("zh", "zl"), 0, 0, tiled=True)
            own, own8 = turn(group, recv)
            pieces.append(spread(own, own8))
        out = correlate(half, spectra, place, *pieces, out)
    return out


def solution(mesh):
    fine = Mesh(mesh.devices.reshape(4, 2, 4, 2, 4), ("x", "core", "y", "zh", "zl"))
    row_col = ("x", "core", "y", "zh")
    placed = (P(row_col, "zl", None, None), P(row_col, None, None, None), P())
    return jax.shard_map(
        shards,
        mesh=fine,
        in_specs=placed,
        out_specs=P(("x", "core"), ("y", "zh"), None, None, "zl"),
        check_vma=False,
    )
```

time: 447 us -> 242 us (0.54)
  waiting for transfers between devices: 244 us -> 62 us
  other arithmetic: 65.5 us -> 3.56 us
  Pallas kernels: 0 us -> 51.6 us
  starting transfers between devices: 1.52 us -> 39.1 us
  local copies, waits for them, and re-layouts: 68.1 us -> 33.6 us
  matrix products: 21.3 us -> 0 us
  blocking collectives: 31.9 us -> 47.1 us
  between operations: 13.6 us -> 0.33 us
    all_gather x2 -> x0, waiting for transfers between devices: 243 us -> none  [the longest x1 186 us: shards(): first_block = lax.all_gather(turned, 'col', axis=0, tiled=True)]
    ppermute x1 -> x37, waiting for transfers between devices: 0.01 us -> 62 us  [the longest x28 36.4 us: ring(): lax.ppermute(value, axis, [(i, (i + step) % count) for i in range(count)])]
    pallas_call x0 -> x8, Pallas kernels: none -> 51.6 us  [the longest x2 36.1 us: correlate(): pl.pallas_call(kernel, out_shape=jax.ShapeDtypeStruct((64, 1, 64, 2, 256)...]
    another operation x3 -> x4, other arithmetic: 42.9 us -> 3.56 us  [spread(): pair = jnp.stack([own8, sib8])]
    ppermute x1 -> x37, starting transfers between devices: 1.29 us -> 32.1 us  [the longest x28 20.2 us: ring(): lax.ppermute(value, axis, [(i, (i + step) % count) for i in range(count)])]
    dot_general x1 -> x0, local copies, waits for them, and re-layouts: 29.4 us -> none  [shards(): jnp.einsum('ascn,bsdn->abcdn', first_block, lax.all_gather(turned, 'row',...]
    dot_general x3 -> x0, matrix products: 21.3 us -> none  [the longest x1 18.8 us: shards(): jnp.einsum('ascn,bsdn->abcdn', first_block, lax.all_gather(turned, 'row',...]
    convert_element_type x2 -> x0, other arithmetic: 19 us -> none  [the longest x1 18.8 us: polyphase(): return summed.astype(jnp.bfloat16)]
  transfers between devices with their start and end apart: 3 -> 39, of which waited for: 2 -> 14; matrix products, arithmetic and copies ran while one was open for 7% -> 6% of each run, Pallas kernels for 0% -> 12%
where the time goes in v1:
time: 242 us; the launch traced here: 237 us
  waiting for transfers between devices  62 us (26%)
  Pallas kernels  51.6 us (21%)
  blocking collectives  47.1 us (19%)
  starting transfers between devices  39.1 us (16%)
  local copies, waits for them, and re-layouts  33.6 us (14%)
  other arithmetic  3.56 us (1%)
    all_to_all x2, blocking collectives, shards(): recv = lax.all_to_all(source[half], ('zh', 'zl'), 0, 0, tiled=True)  47.1 us
    ppermute x28, waiting for transfers between devices, ring(): lax.ppermute(value, axis, [(i, (i + step) % count) for i in range(count)])  36.4 us
    pallas_call x2, Pallas kernels, correlate(): pl.pallas_call(kernel, out_shape=jax.ShapeDtypeStruct((64, 1, 64, 2, 256)...  36.1 us
    unnamed x81, local copies, waits for them, and re-layouts  23.1 us
    ppermute x28, starting transfers between devices, ring(): lax.ppermute(value, axis, [(i, (i + step) % count) for i in range(count)])  20.2 us
    ppermute x1, waiting for transfers between devices, shards(): lax.ppermute(mine[:, :TAPS - 1], 'zl', [(b + 1, b) for b in range(bands -...  19.4 us
    pallas_call x2, Pallas kernels, filter_transform(): pl.pallas_call(functools.partial(filter_transform_kernel, late), out_shap...  11.1 us
    all_to_all x2, starting transfers between devices, shards(): recv = lax.all_to_all(source[half], ('zh', 'zl'), 0, 0, tiled=True)  6.99 us
  transfers between devices with their start and end apart: 39, of which 14 were waited for; matrix products, arithmetic and copies ran while one was open for 6% of the time, Pallas kernels for 12%

profile of v1, /device:TPU:2, one launch (start us, length us, event | category | flops | bytes accessed | tf_op | source)
XLA Modules:
  0.0 237.4 jit_solution(5167991790501903440)
XLA Ops:
  0.9 1.2 copy-done
  2.1 5.3 %filter_transform.2 = (bf16[8,8,2,16,128]{4,3,2,1,0:T(8,128)(2,1)}, bf16[8,8,2,16,128]{4,3,2,1,0:T(8,128)(2,1)S(1)}) custom-call(bf16[8,32,16,128]{3,2,1,0:T(8,128)(2,1)S(1)} %bitcast.34, f32[16,16,128]{2,1,0:T(8,128)S(1)} %bitcast.36, bf16[2,1024,1024]{2,1,0:T(8,128)(2,1)} %constant.42.clone.refs_2_.refs_5_), custom_call_target="tpu_custom_call" | custom-call | flops 1073741824 | bytes 8388608 | tf_op jit(solution)/shard_map/filter_transform/pallas_call | solution.py:94
  7.4 25.7 %all_to_all.20.recv_ref = bf16[8,8,2,16,128]{4,3,2,1,0:T(8,128)(2,1)S(1)} all-to-all(bf16[8,8,2,16,128]{4,3,2,1,0:T(8,128)(2,1)S(1)} %get-tuple-element.17), channel_id=1, replica_groups=mesh['x'=4,'core'=2,'y'=4,'zh'=2,'zl'=4] {'zh','zl'}, dimensions={0} | all-to-all | bytes 1048576 | tf_op jit(solution)/shard_map/all_to_all | solution.py:301
  33.1 3.5 %all-to-all-start.2 = ((bf16[8,8,2,16,128]{4,3,2,1,0:T(8,128)(2,1)}), bf16[8,8,2,16,128]{4,3,2,1,0:T(8,128)(2,1)S(1)}, u32[]{:S(2)}, u32[]{:S(2)}) async-start(bf16[8,8,2,16,128]{4,3,2,1,0:T(8,128)(2,1)} %get-tuple-element.23), calls=%async_computation.2 | async-start | bytes 1048576 | tf_op jit(solution)/shard_map/all_to_all | solution.py:301
  36.6 1.9 slice.38
  38.5 1.3 collective-permute-start.9
  39.8 19.4 %collective-permute-done.9.refs_2_ = bf16[8,15,16,128]{3,2,1,0:T(8,128)(2,1)S(1)} collective-permute-done((bf16[8,15,16,128]{3,2,1,0:T(8,128)(2,1)}, bf16[8,15,16,128]{3,2,1,0:T(8,128)(2,1)S(1)}, u32[]{:S(2)}, u32[]{:S(2)}) %collective-permute-start.9) | collective-permute-done | bytes 491552 | tf_op jit(solution)/shard_map/ppermute | solution.py:276
  60.0 1.0 copy-done.17
  61.0 5.8 %filter_transform.3 = (bf16[8,8,2,16,128]{4,3,2,1,0:T(8,128)(2,1)S(1)}, bf16[8,8,2,16,128]{4,3,2,1,0:T(8,128)(2,1)}) custom-call(s32[1]{0:T(128)} %bitcast.17.refs_0_, bf16[8,32,16,128]{3,2,1,0:T(8,128)(2,1)S(1)} %bitcast.35, bf16[8,15,16,128]{3,2,1,0:T(8,128)(2,1)S(1)} %copy-done.17, bf16[8,15,16,128]{3,2,1,0:T(8,128)(2,1)S(1)} %bitcast.46, ...), custom_call_target="tpu_custom_call" | custom-call | flops 1073741824 | bytes 8388608 | tf_op jit(solution)/shard_map/filter_transform/pallas_call | solution.py:94
  66.8 21.4 %all_to_all.21.recv_ref = bf16[8,8,2,16,128]{4,3,2,1,0:T(8,128)(2,1)S(1)} all-to-all(bf16[8,8,2,16,128]{4,3,2,1,0:T(8,128)(2,1)S(1)} %get-tuple-element.26), channel_id=1, replica_groups=mesh['x'=4,'core'=2,'y'=4,'zh'=2,'zl'=4] {'zh','zl'}, dimensions={0} | all-to-all | bytes 1048576 | tf_op jit(solution)/shard_map/all_to_all | solution.py:301
  88.2 3.5 %all-to-all-start.1 = ((bf16[8,8,2,16,128]{4,3,2,1,0:T(8,128)(2,1)}), bf16[8,8,2,16,128]{4,3,2,1,0:T(8,128)(2,1)S(1)}, u32[]{:S(2)}, u32[]{:S(2)}) async-start(bf16[8,8,2,16,128]{4,3,2,1,0:T(8,128)(2,1)} %get-tuple-element.20), calls=%async_computation.1 | async-start | bytes 1048576 | tf_op jit(solution)/shard_map/all_to_all | solution.py:301
  91.7 1.3 turn.4
  93.0 3.0 %collective-permute-start.1 = (bf16[128,16,128]{2,1,0:T(8,128)(2,1)}, bf16[128,16,128]{2,1,0:T(8,128)(2,1)S(1)}, u32[]{:S(2)}, u32[]{:S(2)}) collective-permute-start(bf16[128,16,128]{2,1,0:T(8,128)(2,1)} %get-tuple-element.18.refs_1_), channel_id=1, source_target_pairs={{0,24},{8,0},{16,8},{24,16},{1,25},{9,1},{17,9},{25,17},{2,26},{10... | collective-permute-start | bytes 1572872 | tf_op jit(solution)/shard_map/ppermute | solution.py:240
  96.1 1.3 turn.6
  97.9 3.0 %collective-permute-start.20 = (bf16[128,16,128]{2,1,0:T(8,128)(2,1)}, bf16[128,16,128]{2,1,0:T(8,128)(2,1)}, u32[]{:S(2)}, u32[]{:S(2)}) collective-permute-start(bf16[128,16,128]{2,1,0:T(8,128)(2,1)} %get-tuple-element.24.refs_0_), channel_id=1, source_target_pairs={{0,24},{8,0},{16,8},{24,16},{1,25},{9,1},{17,9},{25,17},{2,26},{10... | collective-permute-start | bytes 1572872 | tf_op jit(solution)/shard_map/ppermute | solution.py:240
  101.7 1.5 collective-permute-start.5
  104.0 2.7 %collective-permute-done.1.refs_3_ = bf16[128,16,128]{2,1,0:T(8,128)(2,1)S(1)} collective-permute-done((bf16[128,16,128]{2,1,0:T(8,128)(2,1)}, bf16[128,16,128]{2,1,0:T(8,128)(2,1)S(1)}, u32[]{:S(2)}, u32[]{:S(2)}) %collective-permute-start.1) | collective-permute-done | bytes 524320 | tf_op jit(solution)/shard_map/ppermute | solution.py:240
  106.7 1.5 collective-permute-start.24
  110.2 1.3 turn.5
  112.2 3.2 %collective-permute-done.20.refs_2_ = bf16[128,16,128]{2,1,0:T(8,128)(2,1)} collective-permute-done((bf16[128,16,128]{2,1,0:T(8,128)(2,1)}, bf16[128,16,128]{2,1,0:T(8,128)(2,1)}, u32[]{:S(2)}, u32[]{:S(2)}) %collective-permute-start.20) | collective-permute-done | bytes 524320 | tf_op jit(solution)/shard_map/ppermute | solution.py:240
  115.4 7.7 %collective-permute-done.19.refs_1_ = bf16[128,16,128]{2,1,0:T(8,128)(2,1)} collective-permute-done((bf16[128,16,128]{2,1,0:T(8,128)(2,1)}, bf16[128,16,128]{2,1,0:T(8,128)(2,1)}, u32[]{:S(2)}, u32[]{:S(2)}) %collective-permute-start.19) | collective-permute-done | bytes 524320 | tf_op jit(solution)/shard_map/ppermute | solution.py:240
  123.2 2.1 collective-permute-start.2
  125.3 1.0 slice.42
  126.3 1.3 collective-permute-start.22
  128.7 2.0 collective-permute-start.10
  130.7 1.7 collective-permute-done.3.refs_5_
  133.8 3.2 %collective-permute-start.29 = (bf16[128,16,128]{2,1,0:T(8,128)(2,1)}, bf16[128,16,128]{2,1,0:T(8,128)(2,1)}, u32[]{:S(2)}, u32[]{:S(2)}) collective-permute-start(bf16[128,16,128]{2,1,0:T(8,128)(2,1)} %copy-done.12), channel_id=1, source_target_pairs={{0,24},{8,0},{16,8},{24,16},{1,25},{9,1},{17,9},{25,17},{2,26},{10... | collective-permute-start | bytes 1572872 | tf_op jit(solution)/shard_map/ppermute | solution.py:240
  137.0 1.0 collective-permute-done.22.refs_4_
  138.7 1.8 pad_maximum_fusion.3
  140.5 10.1 %collective-permute-done.21.refs_3_ = bf16[64,16,128]{2,1,0:T(8,128)(2,1)S(1)} collective-permute-done((bf16[64,16,128]{2,1,0:T(8,128)(2,1)S(1)}, bf16[64,16,128]{2,1,0:T(8,128)(2,1)S(1)}, u32[]{:S(2)}, u32[]{:S(2)}) %collective-permute-start.21) | collective-permute-done | bytes 262176 | tf_op jit(solution)/shard_map/ppermute | solution.py:240
  151.4 1.5 collective-permute-start.33
  152.9 1.3 collective-permute-start.15
  154.8 4.5 %collective-permute-done.29.refs_13_ = bf16[128,16,128]{2,1,0:T(8,128)(2,1)} collective-permute-done((bf16[128,16,128]{2,1,0:T(8,128)(2,1)}, bf16[128,16,128]{2,1,0:T(8,128)(2,1)}, u32[]{:S(2)}, u32[]{:S(2)}) %collective-permute-start.29) | collective-permute-done | bytes 524320 | tf_op jit(solution)/shard_map/ppermute | solution.py:240
  159.3 1.5 collective-permute-start.25
  161.7 1.0 slice.44
  162.7 1.6 collective-permute-start.13
  164.3 5.0 %collective-permute-done.6.refs_9_ = bf16[2,64,8,128]{3,2,1,0:T(8,128)(2,1)} collective-permute-done((bf16[2,64,8,128]{3,2,1,0:T(8,128)(2,1)S(1)}, bf16[2,64,8,128]{3,2,1,0:T(8,128)(2,1)}, u32[]{:S(2)}, u32[]{:S(2)}) %collective-permute-start.6) | collective-permute-done | bytes 262176 | tf_op jit(solution)/shard_map/ppermute | solution.py:256
  169.4 1.0 slice.43
  170.4 1.0 constant_dynamic-slice_fusion
  172.0 1.4 collective-permute-start.30
  173.4 1.5 collective-permute-start.34
  176.4 1.0 constant_dynamic-slice_fusion.2
  177.3 4.1 %collective-permute-done.30.refs_14_ = bf16[64,16,128]{2,1,0:T(8,128)(2,1)S(1)} collective-permute-done((bf16[64,16,128]{2,1,0:T(8,128)(2,1)S(1)}, bf16[64,16,128]{2,1,0:T(8,128)(2,1)S(1)}, u32[]{:S(2)}, u32[]{:S(2)}) %collective-permute-start.30) | collective-permute-done | bytes 262176 | tf_op jit(solution)/shard_map/ppermute | solution.py:240
  182.1 1.5 collective-permute-start.16
  186.3 1.7 slice.39
  192.5 1.0 copy-done.14
  201.2 18.0 %correlate.2.refs_23_ = f32[64,1,64,2,256]{4,3,2,1,0:T(2,128)} custom-call(s32[10]{0:T(128)S(1)} %stack.79.place_ref.refs_0_, bf16[128,16,128]{2,1,0:T(8,128)(2,1)} %get-tuple-element.24.refs_0_, bf16[128,16,128]{2,1,0:T(8,128)(2,1)} %collective-permute-done.19.refs_1_, bf16[128,16,128]{2,1,0:T(8,128)(2,1)} %collective-permute-done.20.refs_2_, ...), custom_call_target="tpu_custom_call" | custom-call | flops 536870912 | bytes 12582912 | tf_op jit(solution)/shard_map/correlate/pallas_call | solution.py:219
  219.2 18.2 %correlate.3 = f32[64,1,64,2,256]{4,3,2,1,0:T(2,128)} custom-call(s32[10]{0:T(128)S(1)} %stack.79.place_ref.refs_0_, bf16[128,16,128]{2,1,0:T(8,128)(2,1)} %get-tuple-element.18.refs_1_, bf16[128,16,128]{2,1,0:T(8,128)(2,1)S(1)} %collective-permute-done.refs_2_, ...), custom_call_target="tpu_custom_call", output_to_operand_aliasing={{}: (23, {})} | custom-call | flops 536870912 | bytes 12582912 | tf_op jit(solution)/shard_map/correlate/pallas_call | solution.py:219
  (140 shorter events, 30.0 us)
Async XLA Ops:
  2.1 57.8 %copy-start.1 = (bf16[8,32,2,1024]{3,2,1,0:T(2,128)(2,1)S(1)}, bf16[8,32,2,1024]{3,2,1,0:T(2,128)(2,1)}, u32[]{:S(2)}) copy-start(bf16[8,32,2,1024]{3,2,1,0:T(2,128)(2,1)} %param.4) | copy-start | bytes 3145732
  2.1 57.8 %copy-start.15 = (bf16[8,15,2,1024]{3,2,1,0:T(2,128)(2,1)S(1)}, bf16[8,15,2,1024]{3,2,1,0:T(2,128)(2,1)}, u32[]{:S(2)}) copy-start(bf16[8,15,2,1024]{3,2,1,0:T(2,128)(2,1)} %param.5) | copy-start | bytes 1474564
  33.1 33.7 %all-to-all-start.2 = ((bf16[8,8,2,16,128]{4,3,2,1,0:T(8,128)(2,1)}), bf16[8,8,2,16,128]{4,3,2,1,0:T(8,128)(2,1)S(1)}, u32[]{:S(2)}, u32[]{:S(2)}) async-start(bf16[8,8,2,16,128]{4,3,2,1,0:T(8,128)(2,1)} %get-tuple-element.23), calls=%async_computation.2 | async-start | bytes 1048576 | tf_op jit(solution)/shard_map/all_to_all | solution.py:301
  38.5 20.7 %collective-permute-start.9 = (bf16[8,15,16,128]{3,2,1,0:T(8,128)(2,1)}, bf16[8,15,16,128]{3,2,1,0:T(8,128)(2,1)S(1)}, u32[]{:S(2)}, u32[]{:S(2)}) collective-permute-start(bf16[8,15,16,128]{3,2,1,0:T(8,128)(2,1)} %slice.38), channel_id=1, source_target_pairs={{1,0},{2,1},{3,2},{5,4},{6,5},{7,6},{9,8},{10,9},{11,10},{13,12},{... | collective-permute-start | bytes 1474568 | tf_op jit(solution)/shard_map/ppermute | solution.py:276
  88.2 22.0 %all-to-all-start.1 = ((bf16[8,8,2,16,128]{4,3,2,1,0:T(8,128)(2,1)}), bf16[8,8,2,16,128]{4,3,2,1,0:T(8,128)(2,1)S(1)}, u32[]{:S(2)}, u32[]{:S(2)}) async-start(bf16[8,8,2,16,128]{4,3,2,1,0:T(8,128)(2,1)} %get-tuple-element.20), calls=%async_computation.1 | async-start | bytes 1048576 | tf_op jit(solution)/shard_map/all_to_all | solution.py:301
  93.0 13.7 %collective-permute-start.1 = (bf16[128,16,128]{2,1,0:T(8,128)(2,1)}, bf16[128,16,128]{2,1,0:T(8,128)(2,1)S(1)}, u32[]{:S(2)}, u32[]{:S(2)}) collective-permute-start(bf16[128,16,128]{2,1,0:T(8,128)(2,1)} %get-tuple-element.18.refs_1_), channel_id=1, source_target_pairs={{0,24},{8,0},{16,8},{24,16},{1,25},{9,1},{17,9},{25,17},{2,26},{10... | collective-permute-start | bytes 1572872 | tf_op jit(solution)/shard_map/ppermute | solution.py:240
  96.1 4.8 %collective-permute-start.4 = (bf16[128,8,128]{2,1,0:T(8,128)(2,1)S(1)}, bf16[128,8,128]{2,1,0:T(8,128)(2,1)S(1)}, u32[]{:S(2)}, u32[]{:S(2)}) collective-permute-start(bf16[128,8,128]{2,1,0:T(8,128)(2,1)S(1)} %get-tuple-element.19.refs_6_), channel_id=1, source_target_pairs={{0,32},{32,0},{1,33},{33,1},{2,34},{34,2},{3,35},{35,3},{4,36},{36... | collective-permute-start | bytes 786440 | tf_op jit(solution)/shard_map/ppermute | solution.py:240
  96.1 16.1 %collective-permute-start = (bf16[128,16,128]{2,1,0:T(8,128)(2,1)}, bf16[128,16,128]{2,1,0:T(8,128)(2,1)S(1)}, u32[]{:S(2)}, u32[]{:S(2)}) collective-permute-start(bf16[128,16,128]{2,1,0:T(8,128)(2,1)} %get-tuple-element.18.refs_1_), channel_id=1, source_target_pairs={{0,8},{8,16},{16,24},{24,0},{1,9},{9,17},{17,25},{25,1},{2,10},{10... | collective-permute-start | bytes 1572872 | tf_op jit(solution)/shard_map/ppermute | solution.py:240
  97.4 4.3 %collective-permute-start.23 = (bf16[128,8,128]{2,1,0:T(8,128)(2,1)S(1)}, bf16[128,8,128]{2,1,0:T(8,128)(2,1)S(1)}, u32[]{:S(2)}, u32[]{:S(2)}) collective-permute-start(bf16[128,8,128]{2,1,0:T(8,128)(2,1)S(1)} %get-tuple-element.25.refs_5_), channel_id=1, source_target_pairs={{0,32},{32,0},{1,33},{33,1},{2,34},{34,2},{3,35},{35,3},{4,36},{36... | collective-permute-start | bytes 786440 | tf_op jit(solution)/shard_map/ppermute | solution.py:240
  97.9 17.5 %collective-permute-start.20 = (bf16[128,16,128]{2,1,0:T(8,128)(2,1)}, bf16[128,16,128]{2,1,0:T(8,128)(2,1)}, u32[]{:S(2)}, u32[]{:S(2)}) collective-permute-start(bf16[128,16,128]{2,1,0:T(8,128)(2,1)} %get-tuple-element.24.refs_0_), channel_id=1, source_target_pairs={{0,24},{8,0},{16,8},{24,16},{1,25},{9,1},{17,9},{25,17},{2,26},{10... | collective-permute-start | bytes 1572872 | tf_op jit(solution)/shard_map/ppermute | solution.py:240
  100.8 22.3 %collective-permute-start.19 = (bf16[128,16,128]{2,1,0:T(8,128)(2,1)}, bf16[128,16,128]{2,1,0:T(8,128)(2,1)}, u32[]{:S(2)}, u32[]{:S(2)}) collective-permute-start(bf16[128,16,128]{2,1,0:T(8,128)(2,1)} %get-tuple-element.24.refs_0_), channel_id=1, source_target_pairs={{0,8},{8,16},{16,24},{24,0},{1,9},{9,17},{17,25},{25,1},{2,10},{10... | collective-permute-start | bytes 1572872 | tf_op jit(solution)/shard_map/ppermute | solution.py:240
  101.7 25.9 %collective-permute-start.5 = (bf16[2,128,8,128]{3,2,1,0:T(8,128)(2,1)}, bf16[2,128,8,128]{3,2,1,0:T(8,128)(2,1)S(1)}, u32[]{:S(2)}, u32[]{:S(2)}) collective-permute-start(bf16[2,128,8,128]{3,2,1,0:T(8,128)(2,1)} %pad_maximum_fusion), channel_id=1, source_target_pairs={{0,64},{32,224},{64,128},{96,32},{128,192},{160,96},{192,0},{224,1... | collective-permute-start | bytes 1572872 | tf_op jit(solution)/shard_map/ppermute | solution.py:253
  106.7 21.9 %collective-permute-start.24 = (bf16[2,128,8,128]{3,2,1,0:T(8,128)(2,1)}, bf16[2,128,8,128]{3,2,1,0:T(8,128)(2,1)S(1)}, u32[]{:S(2)}, u32[]{:S(2)}) collective-permute-start(bf16[2,128,8,128]{3,2,1,0:T(8,128)(2,1)} %pad_maximum_fusion.2), channel_id=1, source_target_pairs={{0,64},{32,224},{64,128},{96,32},{128,192},{160,96},{192,0},{224,1... | collective-permute-start | bytes 1572872 | tf_op jit(solution)/shard_map/ppermute | solution.py:253
  110.2 80.4 %copy-start.5 = (bf16[128,8,128]{2,1,0:T(8,128)(2,1)S(1)}, bf16[128,8,128]{2,1,0:T(8,128)(2,1)}, u32[]{:S(2)}) copy-start(bf16[128,8,128]{2,1,0:T(8,128)(2,1)} %copy-done.4) | copy-start | bytes 786436
  111.5 79.1 %copy-start.7 = (bf16[128,8,128]{2,1,0:T(8,128)(2,1)S(1)}, bf16[128,8,128]{2,1,0:T(8,128)(2,1)}, u32[]{:S(2)}) copy-start(bf16[128,8,128]{2,1,0:T(8,128)(2,1)} %copy-done.6) | copy-start | bytes 786436
  112.2 11.0 %collective-permute-start.14 = (bf16[128,8,128]{2,1,0:T(8,128)(2,1)S(1)}, bf16[128,8,128]{2,1,0:T(8,128)(2,1)S(1)}, u32[]{:S(2)}, u32[]{:S(2)}) collective-permute-start(bf16[128,8,128]{2,1,0:T(8,128)(2,1)S(1)} %get-tuple-element.22.refs_17_), channel_id=1, source_target_pairs={{0,32},{32,0},{1,33},{33,1},{2,34},{34,2},{3,35},{35,3},{4,36},{36... | collective-permute-start | bytes 786440 | tf_op jit(solution)/shard_map/ppermute | solution.py:240
  115.4 10.9 %collective-permute-start.32 = (bf16[128,8,128]{2,1,0:T(8,128)(2,1)}, bf16[128,8,128]{2,1,0:T(8,128)(2,1)S(1)}, u32[]{:S(2)}, u32[]{:S(2)}) collective-permute-start(bf16[128,8,128]{2,1,0:T(8,128)(2,1)} %copy-done.8), channel_id=1, source_target_pairs={{0,32},{32,0},{1,33},{33,1},{2,34},{34,2},{3,35},{35,3},{4,36},{36... | collective-permute-start | bytes 786440 | tf_op jit(solution)/shard_map/ppermute | solution.py:240
  123.2 9.2 %collective-permute-start.3 = (bf16[64,16,128]{2,1,0:T(8,128)(2,1)S(1)}, bf16[64,16,128]{2,1,0:T(8,128)(2,1)S(1)}, u32[]{:S(2)}, u32[]{:S(2)}) collective-permute-start(bf16[64,16,128]{2,1,0:T(8,128)(2,1)S(1)} %slice.37), channel_id=1, source_target_pairs={{0,24},{8,0},{16,8},{24,16},{1,25},{9,1},{17,9},{25,17},{2,26},{10... | collective-permute-start | bytes 786440 | tf_op jit(solution)/shard_map/ppermute | solution.py:240
  123.2 9.9 %collective-permute-start.2 = (bf16[64,16,128]{2,1,0:T(8,128)(2,1)S(1)}, bf16[64,16,128]{2,1,0:T(8,128)(2,1)S(1)}, u32[]{:S(2)}, u32[]{:S(2)}) collective-permute-start(bf16[64,16,128]{2,1,0:T(8,128)(2,1)S(1)} %slice.36), channel_id=1, source_target_pairs={{0,8},{8,16},{16,24},{24,0},{1,9},{9,17},{17,25},{25,1},{2,10},{10... | collective-permute-start | bytes 786440 | tf_op jit(solution)/shard_map/ppermute | solution.py:240
  126.3 11.7 %collective-permute-start.22 = (bf16[64,16,128]{2,1,0:T(8,128)(2,1)S(1)}, bf16[64,16,128]{2,1,0:T(8,128)(2,1)S(1)}, u32[]{:S(2)}, u32[]{:S(2)}) collective-permute-start(bf16[64,16,128]{2,1,0:T(8,128)(2,1)S(1)} %slice.42), channel_id=1, source_target_pairs={{0,24},{8,0},{16,8},{24,16},{1,25},{9,1},{17,9},{25,17},{2,26},{10... | collective-permute-start | bytes 786440 | tf_op jit(solution)/shard_map/ppermute | solution.py:240
  127.6 25.3 %collective-permute-start.11 = (bf16[128,16,128]{2,1,0:T(8,128)(2,1)}, bf16[128,16,128]{2,1,0:T(8,128)(2,1)}, u32[]{:S(2)}, u32[]{:S(2)}) collective-permute-start(bf16[128,16,128]{2,1,0:T(8,128)(2,1)} %get-tuple-element.21.refs_12_), channel_id=1, source_target_pairs={{0,24},{8,0},{16,8},{24,16},{1,25},{9,1},{17,9},{25,17},{2,26},{10... | collective-permute-start | bytes 1572872 | tf_op jit(solution)/shard_map/ppermute | solution.py:240
  128.7 25.5 %collective-permute-start.10 = (bf16[128,16,128]{2,1,0:T(8,128)(2,1)}, bf16[128,16,128]{2,1,0:T(8,128)(2,1)}, u32[]{:S(2)}, u32[]{:S(2)}) collective-permute-start(bf16[128,16,128]{2,1,0:T(8,128)(2,1)} %get-tuple-element.21.refs_12_), channel_id=1, source_target_pairs={{0,8},{8,16},{16,24},{24,0},{1,9},{9,17},{17,25},{25,1},{2,10},{10... | collective-permute-start | bytes 1572872 | tf_op jit(solution)/shard_map/ppermute | solution.py:240
  133.1 17.6 %collective-permute-start.21 = (bf16[64,16,128]{2,1,0:T(8,128)(2,1)S(1)}, bf16[64,16,128]{2,1,0:T(8,128)(2,1)S(1)}, u32[]{:S(2)}, u32[]{:S(2)}) collective-permute-start(bf16[64,16,128]{2,1,0:T(8,128)(2,1)S(1)} %slice.41), channel_id=1, source_target_pairs={{0,8},{8,16},{16,24},{24,0},{1,9},{9,17},{17,25},{25,1},{2,10},{10... | collective-permute-start | bytes 786440 | tf_op jit(solution)/shard_map/ppermute | solution.py:240
  133.8 25.5 %collective-permute-start.29 = (bf16[128,16,128]{2,1,0:T(8,128)(2,1)}, bf16[128,16,128]{2,1,0:T(8,128)(2,1)}, u32[]{:S(2)}, u32[]{:S(2)}) collective-permute-start(bf16[128,16,128]{2,1,0:T(8,128)(2,1)} %copy-done.12), channel_id=1, source_target_pairs={{0,24},{8,0},{16,8},{24,16},{1,25},{9,1},{17,9},{25,17},{2,26},{10... | collective-permute-start | bytes 1572872 | tf_op jit(solution)/shard_map/ppermute | solution.py:240
  138.7 24.0 %collective-permute-start.28 = (bf16[128,16,128]{2,1,0:T(8,128)(2,1)}, bf16[128,16,128]{2,1,0:T(8,128)(2,1)}, u32[]{:S(2)}, u32[]{:S(2)}) collective-permute-start(bf16[128,16,128]{2,1,0:T(8,128)(2,1)} %copy-done.12), channel_id=1, source_target_pairs={{0,8},{8,16},{16,24},{24,0},{1,9},{9,17},{17,25},{25,1},{2,10},{10... | collective-permute-start | bytes 1572872 | tf_op jit(solution)/shard_map/ppermute | solution.py:240
  151.4 18.1 %collective-permute-start.33 = (bf16[2,128,8,128]{3,2,1,0:T(8,128)(2,1)}, bf16[2,128,8,128]{3,2,1,0:T(8,128)(2,1)}, u32[]{:S(2)}, u32[]{:S(2)}) collective-permute-start(bf16[2,128,8,128]{3,2,1,0:T(8,128)(2,1)} %pad_maximum_fusion.3), channel_id=1, source_target_pairs={{0,64},{32,224},{64,128},{96,32},{128,192},{160,96},{192,0},{224,1... | collective-permute-start | bytes 1572872 | tf_op jit(solution)/shard_map/ppermute | solution.py:253
  152.9 20.5 %collective-permute-start.15 = (bf16[2,128,8,128]{3,2,1,0:T(8,128)(2,1)S(1)}, bf16[2,128,8,128]{3,2,1,0:T(8,128)(2,1)}, u32[]{:S(2)}, u32[]{:S(2)}) collective-permute-start(bf16[2,128,8,128]{3,2,1,0:T(8,128)(2,1)S(1)} %pad_maximum_fusion.1), channel_id=1, source_target_pairs={{0,64},{32,224},{64,128},{96,32},{128,192},{160,96},{192,0},{224,1... | collective-permute-start | bytes 1572872 | tf_op jit(solution)/shard_map/ppermute | solution.py:253
  154.2 15.1 %collective-permute-start.6 = (bf16[2,64,8,128]{3,2,1,0:T(8,128)(2,1)S(1)}, bf16[2,64,8,128]{3,2,1,0:T(8,128)(2,1)}, u32[]{:S(2)}, u32[]{:S(2)}) collective-permute-start(bf16[2,64,8,128]{3,2,1,0:T(8,128)(2,1)S(1)} %constant_dynamic-slice_fusion.3), channel_id=1, source_target_pairs={{0,64},{32,224},{64,128},{96,32},{128,192},{160,96},{192,0},{224,1... | collective-permute-start | bytes 786440 | tf_op jit(solution)/shard_map/ppermute | solution.py:256
  159.3 12.7 %collective-permute-start.25 = (bf16[2,64,8,128]{3,2,1,0:T(8,128)(2,1)S(1)}, bf16[2,64,8,128]{3,2,1,0:T(8,128)(2,1)S(1)}, u32[]{:S(2)}, u32[]{:S(2)}) collective-permute-start(bf16[2,64,8,128]{3,2,1,0:T(8,128)(2,1)S(1)} %constant_dynamic-slice_fusion.1), channel_id=1, source_target_pairs={{0,64},{32,224},{64,128},{96,32},{128,192},{160,96},{192,0},{224,1... | collective-permute-start | bytes 786440 | tf_op jit(solution)/shard_map/ppermute | solution.py:256
  162.7 12.1 %collective-permute-start.13 = (bf16[64,16,128]{2,1,0:T(8,128)(2,1)S(1)}, bf16[64,16,128]{2,1,0:T(8,128)(2,1)S(1)}, u32[]{:S(2)}, u32[]{:S(2)}) collective-permute-start(bf16[64,16,128]{2,1,0:T(8,128)(2,1)S(1)} %slice.40), channel_id=1, source_target_pairs={{0,24},{8,0},{16,8},{24,16},{1,25},{9,1},{17,9},{25,17},{2,26},{10... | collective-permute-start | bytes 786440 | tf_op jit(solution)/shard_map/ppermute | solution.py:240
  169.3 6.4 %collective-permute-start.31 = (bf16[64,16,128]{2,1,0:T(8,128)(2,1)S(1)}, bf16[64,16,128]{2,1,0:T(8,128)(2,1)S(1)}, u32[]{:S(2)}, u32[]{:S(2)}) collective-permute-start(bf16[64,16,128]{2,1,0:T(8,128)(2,1)S(1)} %slice.44), channel_id=1, source_target_pairs={{0,24},{8,0},{16,8},{24,16},{1,25},{9,1},{17,9},{25,17},{2,26},{10... | collective-permute-start | bytes 786440 | tf_op jit(solution)/shard_map/ppermute | solution.py:240
  169.4 16.1 %collective-permute-start.26 = (bf16[2,128,8,128]{3,2,1,0:T(8,128)(2,1)S(1)}, bf16[2,128,8,128]{3,2,1,0:T(8,128)(2,1)S(1)}, u32[]{:S(2)}, u32[]{:S(2)}) collective-permute-start(bf16[2,128,8,128]{3,2,1,0:T(8,128)(2,1)S(1)} %collective-permute-done.24.refs_7_), channel_id=1, source_target_pairs={{0,32},{32,0},{1,33},{33,1},{2,34},{34,2},{3,35},{35,3},{4,36},{36... | collective-permute-start | bytes 1572872 | tf_op jit(solution)/shard_map/ppermute | solution.py:240
  172.0 14.3 %copy-start.28 = (bf16[2,64,8,128]{3,2,1,0:T(8,128)(2,1)}, bf16[2,64,8,128]{3,2,1,0:T(8,128)(2,1)S(1)}, u32[]{:S(2)}) copy-start(bf16[2,64,8,128]{3,2,1,0:T(8,128)(2,1)S(1)} %collective-permute-done.25.refs_8_) | copy-start | bytes 786436
  172.0 9.4 %collective-permute-start.30 = (bf16[64,16,128]{2,1,0:T(8,128)(2,1)S(1)}, bf16[64,16,128]{2,1,0:T(8,128)(2,1)S(1)}, u32[]{:S(2)}, u32[]{:S(2)}) collective-permute-start(bf16[64,16,128]{2,1,0:T(8,128)(2,1)S(1)} %slice.43), channel_id=1, source_target_pairs={{0,8},{8,16},{16,24},{24,0},{1,9},{9,17},{17,25},{25,1},{2,10},{10... | collective-permute-start | bytes 786440 | tf_op jit(solution)/shard_map/ppermute | solution.py:240
  173.4 10.2 %collective-permute-start.34 = (bf16[2,64,8,128]{3,2,1,0:T(8,128)(2,1)S(1)}, bf16[2,64,8,128]{3,2,1,0:T(8,128)(2,1)S(1)}, u32[]{:S(2)}, u32[]{:S(2)}) collective-permute-start(bf16[2,64,8,128]{3,2,1,0:T(8,128)(2,1)S(1)} %constant_dynamic-slice_fusion), channel_id=1, source_target_pairs={{0,64},{32,224},{64,128},{96,32},{128,192},{160,96},{192,0},{224,1... | collective-permute-start | bytes 786440 | tf_op jit(solution)/shard_map/ppermute | solution.py:256
  174.8 9.4 %collective-permute-start.27 = (bf16[2,64,8,128]{3,2,1,0:T(8,128)(2,1)S(1)}, bf16[2,64,8,128]{3,2,1,0:T(8,128)(2,1)S(1)}, u32[]{:S(2)}, u32[]{:S(2)}) collective-permute-start(bf16[2,64,8,128]{3,2,1,0:T(8,128)(2,1)S(1)} %collective-permute-done.25.refs_8_), channel_id=1, source_target_pairs={{0,32},{32,0},{1,33},{33,1},{2,34},{34,2},{3,35},{35,3},{4,36},{36... | collective-permute-start | bytes 786440 | tf_op jit(solution)/shard_map/ppermute | solution.py:240
  176.4 13.6 %collective-permute-start.35 = (bf16[2,128,8,128]{3,2,1,0:T(8,128)(2,1)}, bf16[2,128,8,128]{3,2,1,0:T(8,128)(2,1)}, u32[]{:S(2)}, u32[]{:S(2)}) collective-permute-start(bf16[2,128,8,128]{3,2,1,0:T(8,128)(2,1)} %collective-permute-done.33.refs_18_), channel_id=1, source_target_pairs={{0,32},{32,0},{1,33},{33,1},{2,34},{34,2},{3,35},{35,3},{4,36},{36... | collective-permute-start | bytes 1572872 | tf_op jit(solution)/shard_map/ppermute | solution.py:240
  182.1 6.5 %collective-permute-start.16 = (bf16[2,64,8,128]{3,2,1,0:T(8,128)(2,1)S(1)}, bf16[2,64,8,128]{3,2,1,0:T(8,128)(2,1)}, u32[]{:S(2)}, u32[]{:S(2)}) collective-permute-start(bf16[2,64,8,128]{3,2,1,0:T(8,128)(2,1)S(1)} %constant_dynamic-slice_fusion.2), channel_id=1, source_target_pairs={{0,64},{32,224},{64,128},{96,32},{128,192},{160,96},{192,0},{224,1... | collective-permute-start | bytes 786440 | tf_op jit(solution)/shard_map/ppermute | solution.py:256
  183.6 5.7 %collective-permute-start.36 = (bf16[2,64,8,128]{3,2,1,0:T(8,128)(2,1)S(1)}, bf16[2,64,8,128]{3,2,1,0:T(8,128)(2,1)S(1)}, u32[]{:S(2)}, u32[]{:S(2)}) collective-permute-start(bf16[2,64,8,128]{3,2,1,0:T(8,128)(2,1)S(1)} %collective-permute-done.34.refs_19_), channel_id=1, source_target_pairs={{0,32},{32,0},{1,33},{33,1},{2,34},{34,2},{3,35},{35,3},{4,36},{36... | collective-permute-start | bytes 786440 | tf_op jit(solution)/shard_map/ppermute | solution.py:240
  185.0 34.2 %collective-permute-start.7 = (bf16[2,128,8,128]{3,2,1,0:T(8,128)(2,1)S(1)}, bf16[2,128,8,128]{3,2,1,0:T(8,128)(2,1)}, u32[]{:S(2)}, u32[]{:S(2)}) collective-permute-start(bf16[2,128,8,128]{3,2,1,0:T(8,128)(2,1)S(1)} %collective-permute-done.5.refs_8_), channel_id=1, source_target_pairs={{0,32},{32,0},{1,33},{33,1},{2,34},{34,2},{3,35},{35,3},{4,36},{36... | collective-permute-start | bytes 1572872 | tf_op jit(solution)/shard_map/ppermute | solution.py:240
  186.3 32.9 %collective-permute-start.17 = (bf16[2,128,8,128]{3,2,1,0:T(8,128)(2,1)}, bf16[2,128,8,128]{3,2,1,0:T(8,128)(2,1)}, u32[]{:S(2)}, u32[]{:S(2)}) collective-permute-start(bf16[2,128,8,128]{3,2,1,0:T(8,128)(2,1)} %collective-permute-done.15.refs_19_), channel_id=1, source_target_pairs={{0,32},{32,0},{1,33},{33,1},{2,34},{34,2},{3,35},{35,3},{4,36},{36... | collective-permute-start | bytes 1572872 | tf_op jit(solution)/shard_map/ppermute | solution.py:240
  188.6 30.6 %collective-permute-start.12 = (bf16[64,16,128]{2,1,0:T(8,128)(2,1)}, bf16[64,16,128]{2,1,0:T(8,128)(2,1)}, u32[]{:S(2)}, u32[]{:S(2)}) collective-permute-start(bf16[64,16,128]{2,1,0:T(8,128)(2,1)} %slice.39), channel_id=1, source_target_pairs={{0,8},{8,16},{16,24},{24,0},{1,9},{9,17},{17,25},{25,1},{2,10},{10... | collective-permute-start | bytes 786440 | tf_op jit(solution)/shard_map/ppermute | solution.py:240
  190.0 29.2 %collective-permute-start.8 = (bf16[2,64,8,128]{3,2,1,0:T(8,128)(2,1)}, bf16[2,64,8,128]{3,2,1,0:T(8,128)(2,1)}, u32[]{:S(2)}, u32[]{:S(2)}) collective-permute-start(bf16[2,64,8,128]{3,2,1,0:T(8,128)(2,1)} %collective-permute-done.6.refs_9_), channel_id=1, source_target_pairs={{0,32},{32,0},{1,33},{33,1},{2,34},{34,2},{3,35},{35,3},{4,36},{36... | collective-permute-start | bytes 786440 | tf_op jit(solution)/shard_map/ppermute | solution.py:240
  190.0 29.2 %collective-permute-start.18 = (bf16[2,64,8,128]{3,2,1,0:T(8,128)(2,1)}, bf16[2,64,8,128]{3,2,1,0:T(8,128)(2,1)}, u32[]{:S(2)}, u32[]{:S(2)}) collective-permute-start(bf16[2,64,8,128]{3,2,1,0:T(8,128)(2,1)} %collective-permute-done.16.refs_20_), channel_id=1, source_target_pairs={{0,32},{32,0},{1,33},{33,1},{2,34},{34,2},{3,35},{35,3},{4,36},{36... | collective-permute-start | bytes 786440 | tf_op jit(solution)/shard_map/ppermute | solution.py:240
  201.2 18.0 %copy-start.3 = (bf16[128,8,128]{2,1,0:T(8,128)(2,1)S(1)}, bf16[128,8,128]{2,1,0:T(8,128)(2,1)}, u32[]{:S(2)}) copy-start(bf16[128,8,128]{2,1,0:T(8,128)(2,1)} %copy-done.2) | copy-start | bytes 786436
  201.2 18.0 %copy-start.19 = (bf16[64,16,128]{2,1,0:T(8,128)(2,1)S(1)}, bf16[64,16,128]{2,1,0:T(8,128)(2,1)}, u32[]{:S(2)}) copy-start(bf16[64,16,128]{2,1,0:T(8,128)(2,1)} %copy-done.18) | copy-start | bytes 786436
  201.2 18.0 %copy-start.21 = (bf16[64,16,128]{2,1,0:T(8,128)(2,1)S(1)}, bf16[64,16,128]{2,1,0:T(8,128)(2,1)}, u32[]{:S(2)}) copy-start(bf16[64,16,128]{2,1,0:T(8,128)(2,1)} %copy-done.20) | copy-start | bytes 786436
  201.2 18.1 %copy-start.27 = (bf16[64,16,128]{2,1,0:T(8,128)(2,1)S(1)}, bf16[64,16,128]{2,1,0:T(8,128)(2,1)}, u32[]{:S(2)}) copy-start(bf16[64,16,128]{2,1,0:T(8,128)(2,1)} %copy-done.26) | copy-start | bytes 786436
  (31 other events, 65.8 us)

commit v2 on v0

v2 whole, which is shorter than its diff:
```python
import functools
import math

import jax
import jax.numpy as jnp
import numpy as np
from jax import lax
from jax.experimental import pallas as pl
from jax.experimental.pallas import tpu as pltpu
from jax.sharding import Mesh
from jax.sharding import PartitionSpec as P

LANES = 128
TAPS = 16
HALF = 16
INPUTS = 8
BANDS = 4
CHAN = 1024
VMEM_LIMIT = 60 * 1024 * 1024
PAIRS = 64


def dft_table():
    sample = np.arange(CHAN, dtype=np.int64)[:, None]
    channel = np.arange(CHAN, dtype=np.int64)[None, :]
    theta = np.float32(2.0 * math.pi / CHAN) * (sample * channel % CHAN).astype(np.float32)
    parts = []
    for trig in (np.cos, np.sin):
        full = trig(theta.astype(np.float64)).astype(np.float32)
        parts.append(full.reshape(CHAN, BANDS, CHAN // BANDS))
    table = np.stack(parts, 2).transpose(1, 0, 2, 3)
    return jnp.asarray(table.reshape(BANDS, CHAN, 2 * CHAN // BANDS), dtype=jnp.bfloat16)


def filter_transform_kernel(late, *refs):
    place_ref, refs = refs[0], refs[1:]
    n_frames = 3 if late else 1
    sources, (proto_ref, table_ref), refs = refs[:n_frames], refs[n_frames : n_frames + 2], refs[n_frames + 2 :]
    held, (table, coeff, sums, lhs, sems, table_sem) = refs[-6 - n_frames : -6], refs[-6:]
    outs = refs[: -6 - n_frames]
    band = place_ref[0]

    def copies(a):
        found = []
        for i, (source, buffer) in enumerate(zip(sources, held)):
            part = source.at[a, HALF:] if late and i == 0 else source.at[a]
            found.append(pltpu.make_async_copy(part, buffer.at[a], sems.at[i, a]))
        return found

    for a in range(INPUTS):
        for copy in copies(a):
            copy.start()

    def table_copy(k):
        return pltpu.make_async_copy(table_ref.at[k], table.at[k], table_sem.at[k])

    for k in range(BANDS):
        table_copy(k).start()
    for k in range(CHAN // LANES):
        for c in range(2):
            coeff[pl.ds(2 * k + c, TAPS, 16), :] = proto_ref[:, k * LANES : (k + 1) * LANES]

    def frame(a, t):
        if t < HALF or not late:
            return held[0][a, t].astype(jnp.float32)
        t -= HALF
        return jnp.where(band == BANDS - 1, held[2][a, t], held[1][a, t]).astype(jnp.float32)

    def one_input(a, carry):
        for copy in copies(a):
            copy.wait()
        acc = [None] * HALF
        for t in range(HALF + TAPS - 1):
            value = frame(a, t)
            for s in range(max(0, t - TAPS + 1), min(HALF, t + 1)):
                term = coeff[(t - s) * 16 : (t - s + 1) * 16, :] * value
                acc[s] = term if acc[s] is None else acc[s] + term
        for s in range(HALF):
            sums[pl.ds(s * 16, 16), :] = acc[s]
        for k in range(CHAN // LANES):
            for c in range(2):
                rows = sums[pl.ds(2 * k + c, HALF, 16), :]
                start = pl.multiple_of((a * 2 + c) * HALF, HALF)
                lhs[pl.ds(start, HALF), k * LANES : (k + 1) * LANES] = rows.astype(jnp.bfloat16)
        return carry

    lax.fori_loop(0, INPUTS, one_input, 0)
    scale = 1.0 / math.sqrt(CHAN)
    width = CHAN // BANDS
    for k in range(BANDS):
        table_copy(k).wait()
        both = jnp.dot(lhs[...], table[k], preferred_element_type=jnp.float32)
        both = both.reshape(INPUTS, 2, HALF, 2 * width)
        real = (both[:, 0, :, :width] + both[:, 1, :, width:]) * scale
        imag = (both[:, 1, :, :width] - both[:, 0, :, width:]) * scale
        for part, value in enumerate((real, imag)):
            value = value.astype(jnp.bfloat16)
            for z in range(2):
                outs[0][z * BANDS + k, :, part] = value


def filter_transform(late, place, prototype, table, *frames):
    vmem = pl.BlockSpec(memory_space=pltpu.VMEM)
    hbm = pl.BlockSpec(memory_space=pl.ANY)
    shapes = [(2 * BANDS, INPUTS, 2, HALF, 2 * LANES)]
    held = [(INPUTS, HALF, 16, LANES)] + [(INPUTS, TAPS - 1, 16, LANES)] * 2
    held = held if late else [(INPUTS, 2 * HALF, 16, LANES)]
    (blocks,) = pl.pallas_call(
        functools.partial(filter_transform_kernel, late),
        out_shape=[jax.ShapeDtypeStruct(shape, jnp.bfloat16) for shape in shapes],
        in_specs=[pl.BlockSpec(memory_space=pltpu.SMEM)] + [hbm] * len(frames) + [vmem, hbm],
        out_specs=[vmem] * len(shapes),
        scratch_shapes=[pltpu.VMEM(shape, jnp.bfloat16) for shape in held]
        + [
            pltpu.VMEM((BANDS, CHAN, 4 * LANES), jnp.bfloat16),
            pltpu.VMEM((TAPS * 16, LANES), jnp.float32),
            pltpu.VMEM((HALF * 16, LANES), jnp.float32),
            pltpu.VMEM((INPUTS * 2 * HALF, CHAN), jnp.bfloat16),
            pltpu.SemaphoreType.DMA((len(held), INPUTS)),
            pltpu.SemaphoreType.DMA((BANDS,)),
        ],
        compiler_params=pltpu.CompilerParams(vmem_limit_bytes=VMEM_LIMIT),
        cost_estimate=pl.CostEstimate(
            flops=FAR if late else 1 << 31, bytes_accessed=8 << 20, transcendentals=0
        ),
        name="filter_transform",
    )(place, *frames, prototype, table)
    return blocks


def turn_kernel(place_ref, recv_ref, *refs):
    outs, own_ref, rows = refs[-4:-2], refs[-2], refs[-1]
    for z in range(2):
        for a in range(INPUTS):
            for g in range(2):
                cols = slice(g * LANES, (g + 1) * LANES)
                pieces = [recv_ref[z * BANDS + k, a, c, :, cols] for c in range(2) for k in range(BANDS)]
                block = jnp.concatenate(pieces, 0).astype(jnp.float32).T
                for h in range(2):
                    start = (g * 2 + z) * PAIRS * 16 + h * INPUTS + a
                    rows[pl.ds(start, PAIRS, 16), :] = block[h * PAIRS : (h + 1) * PAIRS]
    for g in range(2):
        for z in range(2):

            def one(n, carry):
                base = pl.multiple_of(((g * 2 + z) * PAIRS + n) * 16, 16)
                outs[g][z, n] = rows[pl.ds(base, 16), :].astype(jnp.bfloat16)
                return carry

            lax.fori_loop(0, PAIRS, one, 0, unroll=16)
        own_ref[g] = outs[g][place_ref[2]]


def turn(place, recv, *tokens):
    vmem = pl.BlockSpec(memory_space=pltpu.VMEM)
    shapes = [(2, PAIRS, 16, LANES)] * 3
    return pl.pallas_call(
        turn_kernel,
        out_shape=[jax.ShapeDtypeStruct(shape, jnp.bfloat16) for shape in shapes],
        in_specs=[pl.BlockSpec(memory_space=pltpu.SMEM), vmem]
        + [pl.BlockSpec(memory_space=pl.ANY)] * len(tokens),
        out_specs=[vmem] * len(shapes),
        scratch_shapes=[pltpu.VMEM((4 * PAIRS * 16, LANES), jnp.float32)],
        compiler_params=pltpu.CompilerParams(vmem_limit_bytes=32 << 20),
        cost_estimate=pl.CostEstimate(flops=1 << 20, bytes_accessed=4 << 20, transcendentals=0),
        name="turn",
    )(place, recv, *tokens)


STEPS = 2
FAR = 1 << 37


def correlate_kernel(spectra, shape, place_ref, *refs):
    sources, (out_ref, outer, mixed) = refs[: len(shape)], refs[-3:]
    step = pl.program_id(0)
    count = PAIRS // STEPS
    lane = lax.broadcasted_iota(jnp.int32, (1, LANES), 1)
    sign = jnp.where(lane < LANES // 2, -1.0, 1.0)
    first = (lane % 16) < 8

    def multiply(n, carry):
        found = {}
        for ref, (kind, late, blocks) in zip(sources, shape):
            for i in range(blocks):
                at = place_ref[3 + i] if blocks == 8 else i
                value = ref[at, 0, n] if len(ref.shape) == 5 else ref[at, n]
                found.setdefault((kind, late), []).append(value)
        lhs, plain = (
            [jnp.concatenate(found[kind, late], 0) for late in range(2)] for kind in range(2)
        )
        lhs = jnp.concatenate(lhs, 1)
        turned = [
            (pltpu.roll(p.astype(jnp.float32), LANES // 2, 1) * sign).astype(jnp.bfloat16)
            for p in plain
        ]
        rhs = jnp.concatenate([jnp.concatenate(plain, 1), jnp.concatenate(turned, 1)], 0)
        value = lax.dot_general(
            lhs, rhs, (((1,), (1,)), ((), ())), preferred_element_type=jnp.float32
        )
        value = value.reshape(8, 2, 8, 2 * LANES)
        base = (step * count + n) * 64
        for part in range(2):
            cols = slice(part * LANES, (part + 1) * LANES)
            kept = jnp.where(first[None], value[:, 0, :, cols], value[:, 1, :, cols])
            outer[part, pl.ds(pl.multiple_of(base, 64), 64), :] = kept.reshape(64, LANES)
        return carry

    @pl.when(step < STEPS)
    def _():
        lax.fori_loop(0, count, multiply, 0, unroll=16)

    low = lane < LANES // 2

    def write(i, carry):
        place = lax.rem(step - STEPS - place_ref[1] + 4, 4) * 16
        for part in range(2):
            cols = [outer[part, pl.ds(place + z * 8 + i, PAIRS, 64), :] for z in range(2)]
            block = jnp.concatenate(cols, 0).T * (1.0 / spectra)
            for r in range(8):
                start = place_ref[3 + r] * 16 + part
                one = block[r * 16 : r * 16 + 8]
                two = block[r * 16 + 8 : r * 16 + 16]
                near = jnp.where(low, one, pltpu.roll(two, PAIRS, 1))
                other = jnp.where(low, pltpu.roll(one, PAIRS, 1), two)
                mixed[0, pl.ds(start, 8, 2), :] = near
                mixed[1, pl.ds(start, 8, 2), :] = other
        for z in range(2):
            out_ref[i + z * 8, 0] = mixed[z].reshape(64, 2, LANES)
        return carry

    @pl.when(step >= STEPS)
    def _():
        lax.fori_loop(0, 8, write, 0, unroll=4)


def correlate(half, spectra, place, lefts, rights, previous):
    count = PAIRS // STEPS
    arrays, shape = [], []
    for kind, both in enumerate((lefts, rights)):
        for late, values in enumerate(both):
            for value in values:
                arrays.append(value)
                shape.append((kind, late, value.shape[0]))
    specs = []
    for value in arrays:
        lead = value.shape[:-3]
        at = (0, half if lead[-1] == 2 else 0) if len(lead) == 2 else (0,)
        size = (lead[0],) + (1,) * (len(lead) - 1)

        def index(i, at=at):
            return (*at, jnp.minimum(i, STEPS - 1), 0, 0)

        specs.append(pl.BlockSpec((*size, count, 16, LANES), index))
    n_in = 1 + len(arrays)
    extra, aliases = (), {}
    kernel = functools.partial(correlate_kernel, spectra, shape)
    if previous is not None:
        extra, aliases = (previous,), {n_in: 0}

        def kernel(*refs):
            correlate_kernel(spectra, shape, *refs[:n_in], *refs[n_in + 1 :])

    return pl.pallas_call(
        kernel,
        out_shape=jax.ShapeDtypeStruct((64, 1, 64, 2, 256), jnp.float32),
        grid=(STEPS + 4,),
        in_specs=[pl.BlockSpec(memory_space=pltpu.SMEM)]
        + specs
        + [pl.BlockSpec(memory_space=pl.ANY)] * len(extra),
        out_specs=pl.BlockSpec(
            (16, 1, 64, 2, LANES), lambda i: (jnp.maximum(i - STEPS, 0), 0, 0, 0, half)
        ),
        scratch_shapes=[
            pltpu.VMEM((2, PAIRS * 64, LANES), jnp.float32),
            pltpu.VMEM((2, LANES, LANES), jnp.float32),
        ],
        input_output_aliases=aliases,
        compiler_params=pltpu.CompilerParams(vmem_limit_bytes=VMEM_LIMIT),
        cost_estimate=pl.CostEstimate(
            flops=2 * 64 * 128 * 256 * 128, bytes_accessed=12 << 20, transcendentals=0
        ),
        name="correlate",
    )(place, *arrays, *extra)


def hold_kernel(*refs):
    refs[-1][...] = jnp.zeros_like(refs[-1])


def hold(*values):
    return pl.pallas_call(
        hold_kernel,
        out_shape=jax.ShapeDtypeStruct((8, LANES), jnp.float32),
        in_specs=[pl.BlockSpec(memory_space=pl.ANY)] * len(values),
        out_specs=pl.BlockSpec(memory_space=pltpu.VMEM),
        compiler_params=pltpu.CompilerParams(vmem_limit_bytes=60 << 20),
        cost_estimate=pl.CostEstimate(flops=FAR, bytes_accessed=1 << 20, transcendentals=0),
        name="hold",
    )(*values)


def ring(value, axis, step):
    count = lax.axis_size(axis)
    return lax.ppermute(value, axis, [(i, (i + step) % count) for i in range(count)])


def along_y(value, step):
    below, above = ring(value, "y", 1), ring(value, "y", -1)
    return value, above, ring(below if step > 0 else above, "y", step), below


def across_x(own):
    found = []
    for step in range(4):
        same = ring(own, "x", -step) if step else own
        found += [same, ring(same, "core", 1)]
    return [value[None] for value in found]


def gather_x(own):
    return [lax.all_gather(own, ("x", "core"), axis=0)]


def shards(frames, tail_frames, prototype):
    spectra = 128
    table = dft_table()

    def words(value):
        shape = value.shape[:2]
        value = value.reshape(shape + (2, CHAN // LANES, LANES)).transpose(0, 1, 3, 2, 4)
        return value.reshape(shape + (16, LANES))

    mine, tail = words(frames), words(tail_frames)
    bands = lax.axis_size("zl")
    following = lax.ppermute(mine[:, : TAPS - 1], "zl", [(b + 1, b) for b in range(bands - 1)])
    place = [lax.axis_index(axis) for axis in ("zl", "y", "zh")]
    my_x, my_core = lax.axis_index("x"), lax.axis_index("core")
    order = []
    for step in range(4):
        there = lax.rem(my_x + step, 4) * 2
        order += [there + my_core, there + 1 - my_core]
    place = jnp.stack(place + order).astype(jnp.int32)

    early = filter_transform(False, place, prototype, table, mine)
    late = filter_transform(True, place, prototype, table, mine, following, tail)

    exchange = functools.partial(
        lax.all_to_all, axis_name=("zh", "zl"), split_axis=0, concat_axis=0, tiled=True
    )
    recv, late = lax.optimization_barrier((exchange(early), late))
    *halves, own = turn(place, recv)
    right0 = gather_x(own)
    first = [along_y(value, step) for value, step in zip(halves, (1, -1))]
    near = [value for _, above, _, below in first for value in (above, below)]
    tokens = hold(*near), hold(first[0][2], first[1][2])
    *halves, own = turn(place, exchange(late), *tokens)
    right1 = across_x(own)
    second = [along_y(value, step) for value, step in zip(halves, (1, -1))]
    out = None
    for half in range(2):
        out = correlate(half, spectra, place, (first[half], second[half]), (right0, right1), out)
    return out


def solution(mesh):
    fine = Mesh(mesh.devices.reshape(4, 2, 4, 2, 4), ("x", "core", "y", "zh", "zl"))
    row_col = ("x", "core", "y", "zh")
    placed = (P(row_col, "zl", None, None), P(row_col, None, None, None), P())
    return jax.shard_map(
        shards,
        mesh=fine,
        in_specs=placed,
        out_specs=P(("x", "core"), ("y", "zh"), None, None, "zl"),
        check_vma=False,
    )
```

time: 447 us -> 177 us (0.40)
  waiting for transfers between devices: 244 us -> 74.4 us
  other arithmetic: 65.5 us -> 0 us
  local copies, waits for them, and re-layouts: 68.1 us -> 7.24 us
  Pallas kernels: 0 us -> 45.4 us
  starting transfers between devices: 1.52 us -> 35.6 us
  blocking collectives: 31.9 us -> 0 us
  matrix products: 21.3 us -> 0 us
    all_gather x2 -> x1, waiting for transfers between devices: 243 us -> 0.01 us  [gather_x(): return [lax.all_gather(own, ('x', 'core'), axis=0)]]
    ppermute x1 -> x20, waiting for transfers between devices: 0.01 us -> 53.4 us  [the longest x19 53.4 us: ring(): lax.ppermute(value, axis, [(i, (i + step) % count) for i in range(count)])]
    pallas_call x0 -> x8, Pallas kernels: none -> 45.4 us  [the longest x2 25.2 us: correlate(): pl.pallas_call(kernel, out_shape=jax.ShapeDtypeStruct((64, 1, 64, 2, 256)...]
    another operation x3 -> x0, other arithmetic: 42.9 us -> none
    all_to_all x1 -> x0, blocking collectives: 31.9 us -> none  [shards(): lax.all_to_all(spectra, 'band', split_axis=3, concat_axis=1, tiled=True)]
    dot_general x1 -> x0, local copies, waits for them, and re-layouts: 29.4 us -> none  [shards(): jnp.einsum('ascn,bsdn->abcdn', first_block, lax.all_gather(turned, 'row',...]
    dot_general x3 -> x0, matrix products: 21.3 us -> none  [the longest x1 18.8 us: shards(): jnp.einsum('ascn,bsdn->abcdn', first_block, lax.all_gather(turned, 'row',...]
    ppermute x1 -> x20, starting transfers between devices: 1.29 us -> 21.7 us  [the longest x19 20.4 us: ring(): lax.ppermute(value, axis, [(i, (i + step) % count) for i in range(count)])]
  transfers between devices with their start and end apart: 3 -> 23, of which waited for: 2 -> 9; matrix products, arithmetic and copies ran while one was open for 7% -> 0% of each run, Pallas kernels for 0% -> 17%
where the time goes in v2:
time: 177 us; the launch traced here: 176 us
  waiting for transfers between devices  74.4 us (42%)
  Pallas kernels  45.4 us (26%)
  starting transfers between devices  35.6 us (20%)
  between operations  13.7 us (8%)
  local copies, waits for them, and re-layouts  7.24 us (4%)
    ppermute x19, waiting for transfers between devices, ring(): lax.ppermute(value, axis, [(i, (i + step) % count) for i in range(count)])  53.4 us
    pallas_call x2, Pallas kernels, correlate(): pl.pallas_call(kernel, out_shape=jax.ShapeDtypeStruct((64, 1, 64, 2, 256)...  25.2 us
    ppermute x19, starting transfers between devices, ring(): lax.ppermute(value, axis, [(i, (i + step) % count) for i in range(count)])  20.4 us
    all_to_all x1, waiting for transfers between devices, shards(): recv, late = lax.optimization_barrier((exchange(early), late))  20.2 us
    pallas_call x2, Pallas kernels, filter_transform(): pl.pallas_call(functools.partial(filter_transform_kernel, late), out_shap...  14.5 us
    all_to_all x1, starting transfers between devices, shards(): recv, late = lax.optimization_barrier((exchange(early), late))  9.66 us
    unnamed x46, local copies, waits for them, and re-layouts  5.51 us
    pallas_call x2, Pallas kernels, turn(): pl.pallas_call(turn_kernel, out_shape=[jax.ShapeDtypeStruct(shape, jnp.bf...  4.54 us
  transfers between devices with their start and end apart: 23, of which 9 were waited for; matrix products, arithmetic and copies ran while one was open for 0% of the time, Pallas kernels for 17%

profile of v2, /device:TPU:2, one launch (start us, length us, event | category | flops | bytes accessed | tf_op | source)
XLA Modules:
  0.0 176.3 jit_solution(5652041194514383302)
XLA Ops:
  6.5 1.1 slice.4
  7.6 1.3 collective-permute-start
  8.9 0.7 stack.47.refs_0_.place_ref
  9.6 7.1 %filter_transform.2 = bf16[8,8,2,16,256]{4,3,2,1,0:T(8,128)(2,1)} custom-call(s32[11]{0:T(128)} %stack.47.refs_0_.place_ref, bf16[8,32,16,128]{3,2,1,0:T(8,128)(2,1)} %bitcast.47, f32[16,1024]{1,0:T(8,128)} %refs_4_.1, bf16[4,1024,512]{2,1,0:T(8,128)(2,1)} %constant.38.clone.refs_3_.refs_5_), custom_call_target="tpu_custom_call" | custom-call | flops 2147483648 | bytes 8388608 | tf_op jit(solution)/shard_map/filter_transform/pallas_call | solution.py:108
  16.7 9.7 %all-to-all-start = ((bf16[8,8,2,16,256]{4,3,2,1,0:T(8,128)(2,1)}), bf16[8,8,2,16,256]{4,3,2,1,0:T(8,128)(2,1)S(1)}, u32[]{:S(2)}, u32[]{:S(2)}) async-start(bf16[8,8,2,16,256]{4,3,2,1,0:T(8,128)(2,1)} %filter_transform.2), calls=%async_computation | async-start | bytes 2097152 | tf_op jit(solution)/shard_map/all_to_all | solution.py:351
  26.4 0.0 collective-permute-done.refs_2_
  26.4 0.8 copy-done.22
  27.2 7.4 %filter_transform.3 = bf16[8,8,2,16,256]{4,3,2,1,0:T(8,128)(2,1)} custom-call(s32[11]{0:T(128)} %stack.47.refs_0_.place_ref, bf16[8,32,16,128]{3,2,1,0:T(8,128)(2,1)} %bitcast.48, bf16[8,15,16,128]{3,2,1,0:T(8,128)(2,1)} %copy-done.22, bf16[8,15,16,128]{3,2,1,0:T(8,128)(2,1)} %bitcast.49, f32[16,1024]{1,0:T(8,128)} %refs_4_.1, ...), custom_call_target="tpu_custom_call" | custom-call | flops 137438953472 | bytes 8388608 | tf_op jit(solution)/shard_map/filter_transform/pallas_call | solution.py:108
  34.6 20.2 %all-to-all-done.recv_ref = bf16[8,8,2,16,256]{4,3,2,1,0:T(8,128)(2,1)S(1)} async-done(((bf16[8,8,2,16,256]{4,3,2,1,0:T(8,128)(2,1)}), bf16[8,8,2,16,256]{4,3,2,1,0:T(8,128)(2,1)S(1)}, u32[]{:S(2)}, u32[]{:S(2)}) %all-to-all-start) | async-done | bytes 1048608 | tf_op jit(solution)/shard_map/all_to_all | solution.py:351
  54.8 2.3 %turn.2 = (bf16[2,64,16,128]{3,2,1,0:T(8,128)(2,1)S(1)}, bf16[2,64,16,128]{3,2,1,0:T(8,128)(2,1)S(1)}, bf16[2,64,16,128]{3,2,1,0:T(8,128)(2,1)}) custom-call(s32[11]{0:T(128)S(1)} %copy-done.5, bf16[8,8,2,16,256]{4,3,2,1,0:T(8,128)(2,1)S(1)} %all-to-all-done.recv_ref), custom_call_target="tpu_custom_call" | custom-call | flops 1048576 | bytes 4194304 | tf_op jit(solution)/shard_map/turn/pallas_call | solution.py:157
  57.1 3.0 %collective-permute-start.1 = (bf16[2,64,16,128]{3,2,1,0:T(8,128)(2,1)S(1)}, bf16[2,64,16,128]{3,2,1,0:T(8,128)(2,1)S(1)}, u32[]{:S(2)}, u32[]{:S(2)}) collective-permute-start(bf16[2,64,16,128]{3,2,1,0:T(8,128)(2,1)S(1)} %get-tuple-element.14.refs_1_), channel_id=1, source_target_pairs={{0,24},{8,0},{16,8},{24,16},{1,25},{9,1},{17,9},{25,17},{2,26},{10... | collective-permute-start | bytes 1572872 | tf_op jit(solution)/shard_map/ppermute | solution.py:305
  60.2 0.0 collective-permute-start.5
  60.2 0.6 collective-permute-start.3
  60.7 2.7 %collective-permute-start.4 = (bf16[2,64,16,128]{3,2,1,0:T(8,128)(2,1)S(1)}, bf16[2,64,16,128]{3,2,1,0:T(8,128)(2,1)S(1)}, u32[]{:S(2)}, u32[]{:S(2)}) collective-permute-start(bf16[2,64,16,128]{3,2,1,0:T(8,128)(2,1)S(1)} %get-tuple-element.16.refs_0_), channel_id=1, source_target_pairs={{0,24},{8,0},{16,8},{24,16},{1,25},{9,1},{17,9},{25,17},{2,26},{10... | collective-permute-start | bytes 1572872 | tf_op jit(solution)/shard_map/ppermute | solution.py:305
  63.4 4.2 %all-to-all-start.1 = ((bf16[8,8,2,16,256]{4,3,2,1,0:T(8,128)(2,1)}), bf16[8,8,2,16,256]{4,3,2,1,0:T(8,128)(2,1)}, u32[]{:S(2)}, u32[]{:S(2)}) async-start(bf16[8,8,2,16,256]{4,3,2,1,0:T(8,128)(2,1)} %filter_transform.3), calls=%async_computation.1 | async-start | bytes 2097152 | tf_op jit(solution)/shard_map/all_to_all | solution.py:357
  67.7 0.0 all-gather.3.cloned.1.call-start
  67.7 0.7 all-gather.3.cloned.1.call-update
  68.4 4.0 %collective-permute-done.1.refs_2_ = bf16[2,64,16,128]{3,2,1,0:T(8,128)(2,1)S(1)} collective-permute-done((bf16[2,64,16,128]{3,2,1,0:T(8,128)(2,1)S(1)}, bf16[2,64,16,128]{3,2,1,0:T(8,128)(2,1)S(1)}, u32[]{:S(2)}, u32[]{:S(2)}) %collective-permute-start.1) | collective-permute-done | bytes 524320 | tf_op jit(solution)/shard_map/ppermute | solution.py:305
  72.5 3.7 %collective-permute-start.2 = (bf16[2,64,16,128]{3,2,1,0:T(8,128)(2,1)S(1)}, bf16[2,64,16,128]{3,2,1,0:T(8,128)(2,1)S(1)}, u32[]{:S(2)}, u32[]{:S(2)}) collective-permute-start(bf16[2,64,16,128]{3,2,1,0:T(8,128)(2,1)S(1)} %collective-permute-done.1.refs_2_), channel_id=1, source_target_pairs={{0,24},{8,0},{16,8},{24,16},{1,25},{9,1},{17,9},{25,17},{2,26},{10... | collective-permute-start | bytes 1572872 | tf_op jit(solution)/shard_map/ppermute | solution.py:305
  76.2 0.0 collective-permute-done.5.refs_1_.refs_3_
  76.2 0.0 collective-permute-start.6
  76.2 11.2 %collective-permute-done.3.refs_3_.refs_4_ = bf16[2,64,16,128]{3,2,1,0:T(8,128)(2,1)S(1)} collective-permute-done((bf16[2,64,16,128]{3,2,1,0:T(8,128)(2,1)S(1)}, bf16[2,64,16,128]{3,2,1,0:T(8,128)(2,1)S(1)}, u32[]{:S(2)}, u32[]{:S(2)}) %collective-permute-start.3) | collective-permute-done | bytes 524320 | tf_op jit(solution)/shard_map/ppermute | solution.py:305
  87.5 0.8 copy-done.15
  88.3 0.8 copy-done.18
  89.1 0.6 hold.2.refs_0_
  89.7 4.3 %collective-permute-done.2.refs_1_.refs_3_ = bf16[2,64,16,128]{3,2,1,0:T(8,128)(2,1)S(1)} collective-permute-done((bf16[2,64,16,128]{3,2,1,0:T(8,128)(2,1)S(1)}, bf16[2,64,16,128]{3,2,1,0:T(8,128)(2,1)S(1)}, u32[]{:S(2)}, u32[]{:S(2)}) %collective-permute-start.2) | collective-permute-done | bytes 524320 | tf_op jit(solution)/shard_map/ppermute | solution.py:305
  94.0 3.5 %collective-permute-done.6.refs_0_.refs_2_ = bf16[2,64,16,128]{3,2,1,0:T(8,128)(2,1)} collective-permute-done((bf16[2,64,16,128]{3,2,1,0:T(8,128)(2,1)S(1)}, bf16[2,64,16,128]{3,2,1,0:T(8,128)(2,1)}, u32[]{:S(2)}, u32[]{:S(2)}) %collective-permute-start.6) | collective-permute-done | bytes 524320 | tf_op jit(solution)/shard_map/ppermute | solution.py:305
  97.5 0.6 hold.3.refs_1_
  98.1 0.7 copy-done.7
  98.8 2.2 %turn.3 = (bf16[2,64,16,128]{3,2,1,0:T(8,128)(2,1)S(1)}, bf16[2,64,16,128]{3,2,1,0:T(8,128)(2,1)S(1)}, bf16[2,64,16,128]{3,2,1,0:T(8,128)(2,1)S(1)}) custom-call(s32[11]{0:T(128)S(1)} %copy-done.5, bf16[8,8,2,16,256]{4,3,2,1,0:T(8,128)(2,1)} %all-to-all-done.1.recv_ref, f32[8,128]{1,0:T(8,128)S(1)} %copy-done.6, f32[8,128]{1,0:T(8,128)S(1)} %copy-done.7), custom_call_target="tpu_custom_call" | custom-call | flops 1048576 | bytes 4194304 | tf_op jit(solution)/shard_map/turn/pallas_call | solution.py:157
  101.1 1.1 collective-permute-start.7
  102.2 1.0 collective-permute-start.18
  103.2 2.2 %collective-permute-start.17 = (bf16[2,64,16,128]{3,2,1,0:T(8,128)(2,1)S(1)}, bf16[2,64,16,128]{3,2,1,0:T(8,128)(2,1)S(1)}, u32[]{:S(2)}, u32[]{:S(2)}) collective-permute-start(bf16[2,64,16,128]{3,2,1,0:T(8,128)(2,1)S(1)} %get-tuple-element.20.refs_4_), channel_id=1, source_target_pairs={{0,24},{8,0},{16,8},{24,16},{1,25},{9,1},{17,9},{25,17},{2,26},{10... | collective-permute-start | bytes 1572872 | tf_op jit(solution)/shard_map/ppermute | solution.py:305
  105.4 1.5 collective-permute-start.15
  106.9 1.1 collective-permute-start.13
  108.0 8.1 %collective-permute-done.7.refs_6_ = bf16[2,64,16,128]{3,2,1,0:T(8,128)(2,1)} collective-permute-done((bf16[2,64,16,128]{3,2,1,0:T(8,128)(2,1)S(1)}, bf16[2,64,16,128]{3,2,1,0:T(8,128)(2,1)}, u32[]{:S(2)}, u32[]{:S(2)}) %collective-permute-start.7) | collective-permute-done | bytes 524320 | tf_op jit(solution)/shard_map/ppermute | solution.py:305
  116.1 0.6 collective-permute-start.11
  116.7 8.3 %collective-permute-done.17.refs_5_ = bf16[2,64,16,128]{3,2,1,0:T(8,128)(2,1)S(1)} collective-permute-done((bf16[2,64,16,128]{3,2,1,0:T(8,128)(2,1)S(1)}, bf16[2,64,16,128]{3,2,1,0:T(8,128)(2,1)S(1)}, u32[]{:S(2)}, u32[]{:S(2)}) %collective-permute-start.17) | collective-permute-done | bytes 524320 | tf_op jit(solution)/shard_map/ppermute | solution.py:305
  125.1 0.8 copy-done.20
  125.9 0.5 collective-permute-start.14
  126.4 5.2 %collective-permute-done.11 = bf16[2,64,16,128]{3,2,1,0:T(8,128)(2,1)S(1)} collective-permute-done((bf16[2,64,16,128]{3,2,1,0:T(8,128)(2,1)S(1)}, bf16[2,64,16,128]{3,2,1,0:T(8,128)(2,1)S(1)}, u32[]{:S(2)}, u32[]{:S(2)}) %collective-permute-start.11) | collective-permute-done | bytes 524320 | tf_op jit(solution)/shard_map/ppermute | solution.py:305
  131.6 0.1 collective-permute-start.9
  131.7 8.6 %collective-permute-done.19.refs_6_ = bf16[2,64,16,128]{3,2,1,0:T(8,128)(2,1)S(1)} collective-permute-done((bf16[2,64,16,128]{3,2,1,0:T(8,128)(2,1)S(1)}, bf16[2,64,16,128]{3,2,1,0:T(8,128)(2,1)S(1)}, u32[]{:S(2)}, u32[]{:S(2)}) %collective-permute-start.19) | collective-permute-done | bytes 524320 | tf_op jit(solution)/shard_map/ppermute | solution.py:305
  140.3 2.3 %collective-permute-start.8 = (bf16[2,64,16,128]{3,2,1,0:T(8,128)(2,1)}, bf16[2,64,16,128]{3,2,1,0:T(8,128)(2,1)}, u32[]{:S(2)}, u32[]{:S(2)}) collective-permute-start(bf16[2,64,16,128]{3,2,1,0:T(8,128)(2,1)} %collective-permute-done.7.refs_6_), channel_id=1, source_target_pairs={{0,24},{8,0},{16,8},{24,16},{1,25},{9,1},{17,9},{25,17},{2,26},{10... | collective-permute-start | bytes 1572872 | tf_op jit(solution)/shard_map/ppermute | solution.py:305
  142.6 0.8 copy-done.12
  143.4 0.8 copy-done.13
  144.2 12.6 %correlate.2.refs_18_ = f32[64,1,64,2,256]{4,3,2,1,0:T(2,128)} custom-call(s32[11]{0:T(128)} %stack.47.refs_0_.place_ref, bf16[2,64,16,128]{3,2,1,0:T(8,128)(2,1)} %copy-done.3, bf16[2,64,16,128]{3,2,1,0:T(8,128)(2,1)} %copy-done.18, bf16[2,64,16,128]{3,2,1,0:T(8,128)(2,1)} %collective-permute-done.6.refs_0_.refs_2_, bf16[2,64,16,128]{3,2,1,0:T(8,128)(2,1)} %copy-done.17, ...), custom_call_target="tpu_custom_call" | custom-call | flops 536870912 | bytes 12582912 | tf_op jit(solution)/shard_map/correlate/pallas_call | solution.py:264
  156.9 12.6 %correlate.3 = f32[64,1,64,2,256]{4,3,2,1,0:T(2,128)} custom-call(s32[11]{0:T(128)} %stack.47.refs_0_.place_ref, bf16[2,64,16,128]{3,2,1,0:T(8,128)(2,1)} %copy-done.1, bf16[2,64,16,128]{3,2,1,0:T(8,128)(2,1)} %copy-done.14, bf16[2,64,16,128]{3,2,1,0:T(8,128)(2,1)} %copy-done.16, ...), custom_call_target="tpu_custom_call", output_to_operand_aliasing={{}: (18, {})} | custom-call | flops 536870912 | bytes 12582912 | tf_op jit(solution)/shard_map/correlate/pallas_call | solution.py:264
  (55 shorter events, 0.1 us)
Async XLA Ops:
  7.6 18.8 %collective-permute-start = (bf16[8,15,16,128]{3,2,1,0:T(8,128)(2,1)S(1)}, bf16[8,15,16,128]{3,2,1,0:T(8,128)(2,1)S(1)}, u32[]{:S(2)}, u32[]{:S(2)}) collective-permute-start(bf16[8,15,16,128]{3,2,1,0:T(8,128)(2,1)S(1)} %slice.4), channel_id=1, source_target_pairs={{1,0},{2,1},{3,2},{5,4},{6,5},{7,6},{9,8},{10,9},{11,10},{13,12},{... | collective-permute-start | bytes 1474568 | tf_op jit(solution)/shard_map/ppermute | solution.py:336
  16.7 38.1 %all-to-all-start = ((bf16[8,8,2,16,256]{4,3,2,1,0:T(8,128)(2,1)}), bf16[8,8,2,16,256]{4,3,2,1,0:T(8,128)(2,1)S(1)}, u32[]{:S(2)}, u32[]{:S(2)}) async-start(bf16[8,8,2,16,256]{4,3,2,1,0:T(8,128)(2,1)} %filter_transform.2), calls=%async_computation | async-start | bytes 2097152 | tf_op jit(solution)/shard_map/all_to_all | solution.py:351
  26.4 0.8 copy-start.22
  27.2 27.6 %copy-start.5 = (s32[11]{0:T(128)S(1)}, s32[11]{0:T(128)}, u32[]{:S(2)}) copy-start(s32[11]{0:T(128)} %stack.47.refs_0_.place_ref) | copy-start | bytes 136
  57.1 32.5 %copy-start.1 = (bf16[2,64,16,128]{3,2,1,0:T(8,128)(2,1)}, bf16[2,64,16,128]{3,2,1,0:T(8,128)(2,1)S(1)}, u32[]{:S(2)}) copy-start(bf16[2,64,16,128]{3,2,1,0:T(8,128)(2,1)S(1)} %get-tuple-element.14.refs_1_) | copy-start | bytes 1572868
  57.1 32.5 %copy-start.3 = (bf16[2,64,16,128]{3,2,1,0:T(8,128)(2,1)}, bf16[2,64,16,128]{3,2,1,0:T(8,128)(2,1)S(1)}, u32[]{:S(2)}) copy-start(bf16[2,64,16,128]{3,2,1,0:T(8,128)(2,1)S(1)} %get-tuple-element.16.refs_0_) | copy-start | bytes 1572868
  57.1 15.3 %collective-permute-start.1 = (bf16[2,64,16,128]{3,2,1,0:T(8,128)(2,1)S(1)}, bf16[2,64,16,128]{3,2,1,0:T(8,128)(2,1)S(1)}, u32[]{:S(2)}, u32[]{:S(2)}) collective-permute-start(bf16[2,64,16,128]{3,2,1,0:T(8,128)(2,1)S(1)} %get-tuple-element.14.refs_1_), channel_id=1, source_target_pairs={{0,24},{8,0},{16,8},{24,16},{1,25},{9,1},{17,9},{25,17},{2,26},{10... | collective-permute-start | bytes 1572872 | tf_op jit(solution)/shard_map/ppermute | solution.py:305
  60.2 16.0 %collective-permute-start.5 = (bf16[2,64,16,128]{3,2,1,0:T(8,128)(2,1)S(1)}, bf16[2,64,16,128]{3,2,1,0:T(8,128)(2,1)S(1)}, u32[]{:S(2)}, u32[]{:S(2)}) collective-permute-start(bf16[2,64,16,128]{3,2,1,0:T(8,128)(2,1)S(1)} %get-tuple-element.16.refs_0_), channel_id=1, source_target_pairs={{0,8},{8,16},{16,24},{24,0},{1,9},{9,17},{17,25},{25,1},{2,10},{10... | collective-permute-start | bytes 1572872 | tf_op jit(solution)/shard_map/ppermute | solution.py:305
  60.2 27.3 %collective-permute-start.3 = (bf16[2,64,16,128]{3,2,1,0:T(8,128)(2,1)S(1)}, bf16[2,64,16,128]{3,2,1,0:T(8,128)(2,1)S(1)}, u32[]{:S(2)}, u32[]{:S(2)}) collective-permute-start(bf16[2,64,16,128]{3,2,1,0:T(8,128)(2,1)S(1)} %get-tuple-element.14.refs_1_), channel_id=1, source_target_pairs={{0,8},{8,16},{16,24},{24,0},{1,9},{9,17},{17,25},{25,1},{2,10},{10... | collective-permute-start | bytes 1572872 | tf_op jit(solution)/shard_map/ppermute | solution.py:305
  60.7 26.7 %collective-permute-start.4 = (bf16[2,64,16,128]{3,2,1,0:T(8,128)(2,1)S(1)}, bf16[2,64,16,128]{3,2,1,0:T(8,128)(2,1)S(1)}, u32[]{:S(2)}, u32[]{:S(2)}) collective-permute-start(bf16[2,64,16,128]{3,2,1,0:T(8,128)(2,1)S(1)} %get-tuple-element.16.refs_0_), channel_id=1, source_target_pairs={{0,24},{8,0},{16,8},{24,16},{1,25},{9,1},{17,9},{25,17},{2,26},{10... | collective-permute-start | bytes 1572872 | tf_op jit(solution)/shard_map/ppermute | solution.py:305
  63.4 34.7 %all-to-all-start.1 = ((bf16[8,8,2,16,256]{4,3,2,1,0:T(8,128)(2,1)}), bf16[8,8,2,16,256]{4,3,2,1,0:T(8,128)(2,1)}, u32[]{:S(2)}, u32[]{:S(2)}) async-start(bf16[8,8,2,16,256]{4,3,2,1,0:T(8,128)(2,1)} %filter_transform.3), calls=%async_computation.1 | async-start | bytes 2097152 | tf_op jit(solution)/shard_map/all_to_all | solution.py:357
  67.7 76.5 %all-gather.3.cloned.1.call-start = ((), (), s32[]{:S(2)}) async-start(), calls=%async_computation.2 | async-start | bytes 4718592 | tf_op jit(solution)/shard_map/all_gather | solution.py:322
  72.5 15.0 %copy-start.14 = (bf16[2,64,16,128]{3,2,1,0:T(8,128)(2,1)}, bf16[2,64,16,128]{3,2,1,0:T(8,128)(2,1)S(1)}, u32[]{:S(2)}) copy-start(bf16[2,64,16,128]{3,2,1,0:T(8,128)(2,1)S(1)} %collective-permute-done.1.refs_2_) | copy-start | bytes 1572868
  72.5 21.5 %collective-permute-start.2 = (bf16[2,64,16,128]{3,2,1,0:T(8,128)(2,1)S(1)}, bf16[2,64,16,128]{3,2,1,0:T(8,128)(2,1)S(1)}, u32[]{:S(2)}, u32[]{:S(2)}) collective-permute-start(bf16[2,64,16,128]{3,2,1,0:T(8,128)(2,1)S(1)} %collective-permute-done.1.refs_2_), channel_id=1, source_target_pairs={{0,24},{8,0},{16,8},{24,16},{1,25},{9,1},{17,9},{25,17},{2,26},{10... | collective-permute-start | bytes 1572872 | tf_op jit(solution)/shard_map/ppermute | solution.py:305
  76.2 11.2 %copy-start.17 = (bf16[2,64,16,128]{3,2,1,0:T(8,128)(2,1)}, bf16[2,64,16,128]{3,2,1,0:T(8,128)(2,1)S(1)}, u32[]{:S(2)}) copy-start(bf16[2,64,16,128]{3,2,1,0:T(8,128)(2,1)S(1)} %collective-permute-done.5.refs_1_.refs_3_) | copy-start | bytes 1572868
  76.2 21.3 %collective-permute-start.6 = (bf16[2,64,16,128]{3,2,1,0:T(8,128)(2,1)S(1)}, bf16[2,64,16,128]{3,2,1,0:T(8,128)(2,1)}, u32[]{:S(2)}, u32[]{:S(2)}) collective-permute-start(bf16[2,64,16,128]{3,2,1,0:T(8,128)(2,1)S(1)} %collective-permute-done.5.refs_1_.refs_3_), channel_id=1, source_target_pairs={{0,8},{8,16},{16,24},{24,0},{1,9},{9,17},{17,25},{25,1},{2,10},{10... | collective-permute-start | bytes 1572872 | tf_op jit(solution)/shard_map/ppermute | solution.py:305
  87.4 0.8 copy-start.15
  88.3 0.8 copy-start.18
  89.7 8.5 %copy-start.6 = (f32[8,128]{1,0:T(8,128)S(1)}, f32[8,128]{1,0:T(8,128)}, u32[]{:S(2)}) copy-start(f32[8,128]{1,0:T(8,128)} %hold.2.refs_0_) | copy-start | bytes 12292
  94.0 3.5 %copy-start.16 = (bf16[2,64,16,128]{3,2,1,0:T(8,128)(2,1)}, bf16[2,64,16,128]{3,2,1,0:T(8,128)(2,1)S(1)}, u32[]{:S(2)}) copy-start(bf16[2,64,16,128]{3,2,1,0:T(8,128)(2,1)S(1)} %collective-permute-done.2.refs_1_.refs_3_) | copy-start | bytes 1572868
  98.1 0.7 copy-start.7
  101.0 43.2 %copy-start = (bf16[2,64,16,128]{3,2,1,0:T(8,128)(2,1)}, bf16[2,64,16,128]{3,2,1,0:T(8,128)(2,1)S(1)}, u32[]{:S(2)}) copy-start(bf16[2,64,16,128]{3,2,1,0:T(8,128)(2,1)S(1)} %get-tuple-element.19) | copy-start | bytes 1572868
  101.0 43.2 %copy-start.4 = (bf16[2,64,16,128]{3,2,1,0:T(8,128)(2,1)}, bf16[2,64,16,128]{3,2,1,0:T(8,128)(2,1)S(1)}, u32[]{:S(2)}) copy-start(bf16[2,64,16,128]{3,2,1,0:T(8,128)(2,1)S(1)} %get-tuple-element.20.refs_4_) | copy-start | bytes 1572868
  101.0 55.8 %copy-start.2 = (bf16[2,64,16,128]{3,2,1,0:T(8,128)(2,1)}, bf16[2,64,16,128]{3,2,1,0:T(8,128)(2,1)S(1)}, u32[]{:S(2)}) copy-start(bf16[2,64,16,128]{3,2,1,0:T(8,128)(2,1)S(1)} %get-tuple-element.17.refs_5_) | copy-start | bytes 1572868
  101.1 15.0 %collective-permute-start.7 = (bf16[2,64,16,128]{3,2,1,0:T(8,128)(2,1)S(1)}, bf16[2,64,16,128]{3,2,1,0:T(8,128)(2,1)}, u32[]{:S(2)}, u32[]{:S(2)}) collective-permute-start(bf16[2,64,16,128]{3,2,1,0:T(8,128)(2,1)S(1)} %get-tuple-element.17.refs_5_), channel_id=1, source_target_pairs={{0,24},{8,0},{16,8},{24,16},{1,25},{9,1},{17,9},{25,17},{2,26},{10... | collective-permute-start | bytes 1572872 | tf_op jit(solution)/shard_map/ppermute | solution.py:305
  102.2 14.5 %collective-permute-start.18 = (bf16[2,64,16,128]{3,2,1,0:T(8,128)(2,1)S(1)}, bf16[2,64,16,128]{3,2,1,0:T(8,128)(2,1)S(1)}, u32[]{:S(2)}, u32[]{:S(2)}) collective-permute-start(bf16[2,64,16,128]{3,2,1,0:T(8,128)(2,1)S(1)} %get-tuple-element.20.refs_4_), channel_id=1, source_target_pairs={{0,8},{8,16},{16,24},{24,0},{1,9},{9,17},{17,25},{25,1},{2,10},{10... | collective-permute-start | bytes 1572872 | tf_op jit(solution)/shard_map/ppermute | solution.py:305
  103.2 21.9 %collective-permute-start.17 = (bf16[2,64,16,128]{3,2,1,0:T(8,128)(2,1)S(1)}, bf16[2,64,16,128]{3,2,1,0:T(8,128)(2,1)S(1)}, u32[]{:S(2)}, u32[]{:S(2)}) collective-permute-start(bf16[2,64,16,128]{3,2,1,0:T(8,128)(2,1)S(1)} %get-tuple-element.20.refs_4_), channel_id=1, source_target_pairs={{0,24},{8,0},{16,8},{24,16},{1,25},{9,1},{17,9},{25,17},{2,26},{10... | collective-permute-start | bytes 1572872 | tf_op jit(solution)/shard_map/ppermute | solution.py:305
  105.4 20.5 %collective-permute-start.15 = (bf16[2,64,16,128]{3,2,1,0:T(8,128)(2,1)S(1)}, bf16[2,64,16,128]{3,2,1,0:T(8,128)(2,1)S(1)}, u32[]{:S(2)}, u32[]{:S(2)}) collective-permute-start(bf16[2,64,16,128]{3,2,1,0:T(8,128)(2,1)S(1)} %get-tuple-element.19), channel_id=1, source_target_pairs={{0,64},{64,128},{128,192},{192,0},{1,65},{65,129},{129,193},{193,1... | collective-permute-start | bytes 1572872 | tf_op jit(solution)/shard_map/ppermute | solution.py:305
  106.9 19.0 %collective-permute-start.13 = (bf16[2,64,16,128]{3,2,1,0:T(8,128)(2,1)S(1)}, bf16[2,64,16,128]{3,2,1,0:T(8,128)(2,1)S(1)}, u32[]{:S(2)}, u32[]{:S(2)}) collective-permute-start(bf16[2,64,16,128]{3,2,1,0:T(8,128)(2,1)S(1)} %get-tuple-element.19), channel_id=1, source_target_pairs={{0,128},{64,192},{128,0},{192,64},{1,129},{65,193},{129,1},{193,65... | collective-permute-start | bytes 1572872 | tf_op jit(solution)/shard_map/ppermute | solution.py:305
  116.1 15.5 %collective-permute-start.11 = (bf16[2,64,16,128]{3,2,1,0:T(8,128)(2,1)S(1)}, bf16[2,64,16,128]{3,2,1,0:T(8,128)(2,1)S(1)}, u32[]{:S(2)}, u32[]{:S(2)}) collective-permute-start(bf16[2,64,16,128]{3,2,1,0:T(8,128)(2,1)S(1)} %get-tuple-element.19), channel_id=1, source_target_pairs={{0,192},{64,0},{128,64},{192,128},{1,193},{65,1},{129,65},{193,129... | collective-permute-start | bytes 1572872 | tf_op jit(solution)/shard_map/ppermute | solution.py:305
  116.7 25.9 %copy-start.19 = (bf16[2,64,16,128]{3,2,1,0:T(8,128)(2,1)}, bf16[2,64,16,128]{3,2,1,0:T(8,128)(2,1)S(1)}, u32[]{:S(2)}) copy-start(bf16[2,64,16,128]{3,2,1,0:T(8,128)(2,1)S(1)} %collective-permute-done.18.refs_7_) | copy-start | bytes 1572868
  116.7 14.9 %collective-permute-start.10 = (bf16[2,64,16,128]{3,2,1,0:T(8,128)(2,1)S(1)}, bf16[2,64,16,128]{3,2,1,0:T(8,128)(2,1)S(1)}, u32[]{:S(2)}, u32[]{:S(2)}) collective-permute-start(bf16[2,64,16,128]{3,2,1,0:T(8,128)(2,1)S(1)} %get-tuple-element.19), channel_id=1, source_target_pairs={{0,32},{32,0},{1,33},{33,1},{2,34},{34,2},{3,35},{35,3},{4,36},{36... | collective-permute-start | bytes 1572872 | tf_op jit(solution)/shard_map/ppermute | solution.py:305
  125.1 0.8 copy-start.20
  125.1 15.3 %collective-permute-start.19 = (bf16[2,64,16,128]{3,2,1,0:T(8,128)(2,1)S(1)}, bf16[2,64,16,128]{3,2,1,0:T(8,128)(2,1)S(1)}, u32[]{:S(2)}, u32[]{:S(2)}) collective-permute-start(bf16[2,64,16,128]{3,2,1,0:T(8,128)(2,1)S(1)} %collective-permute-done.18.refs_7_), channel_id=1, source_target_pairs={{0,8},{8,16},{16,24},{24,0},{1,9},{9,17},{17,25},{25,1},{2,10},{10... | collective-permute-start | bytes 1572872 | tf_op jit(solution)/shard_map/ppermute | solution.py:305
  125.9 18.3 %copy-start.8 = (bf16[2,64,16,128]{3,2,1,0:T(8,128)(2,1)}, bf16[2,64,16,128]{3,2,1,0:T(8,128)(2,1)S(1)}, u32[]{:S(2)}) copy-start(bf16[2,64,16,128]{3,2,1,0:T(8,128)(2,1)S(1)} %collective-permute-done.15) | copy-start | bytes 1572868
  125.9 16.7 %collective-permute-start.16 = (bf16[2,64,16,128]{3,2,1,0:T(8,128)(2,1)S(1)}, bf16[2,64,16,128]{3,2,1,0:T(8,128)(2,1)S(1)}, u32[]{:S(2)}, u32[]{:S(2)}) collective-permute-start(bf16[2,64,16,128]{3,2,1,0:T(8,128)(2,1)S(1)} %collective-permute-done.15), channel_id=1, source_target_pairs={{0,32},{32,0},{1,33},{33,1},{2,34},{34,2},{3,35},{35,3},{4,36},{36... | collective-permute-start | bytes 1572872 | tf_op jit(solution)/shard_map/ppermute | solution.py:305
  125.9 18.3 %copy-start.9 = (bf16[2,64,16,128]{3,2,1,0:T(8,128)(2,1)}, bf16[2,64,16,128]{3,2,1,0:T(8,128)(2,1)S(1)}, u32[]{:S(2)}) copy-start(bf16[2,64,16,128]{3,2,1,0:T(8,128)(2,1)S(1)} %collective-permute-done.13) | copy-start | bytes 1572868
  125.9 16.7 %collective-permute-start.14 = (bf16[2,64,16,128]{3,2,1,0:T(8,128)(2,1)S(1)}, bf16[2,64,16,128]{3,2,1,0:T(8,128)(2,1)S(1)}, u32[]{:S(2)}, u32[]{:S(2)}) collective-permute-start(bf16[2,64,16,128]{3,2,1,0:T(8,128)(2,1)S(1)} %collective-permute-done.13), channel_id=1, source_target_pairs={{0,32},{32,0},{1,33},{33,1},{2,34},{34,2},{3,35},{35,3},{4,36},{36... | collective-permute-start | bytes 1572872 | tf_op jit(solution)/shard_map/ppermute | solution.py:305
  131.6 12.6 %copy-start.10 = (bf16[2,64,16,128]{3,2,1,0:T(8,128)(2,1)}, bf16[2,64,16,128]{3,2,1,0:T(8,128)(2,1)S(1)}, u32[]{:S(2)}) copy-start(bf16[2,64,16,128]{3,2,1,0:T(8,128)(2,1)S(1)} %collective-permute-done.11) | copy-start | bytes 1572868
  131.6 12.6 %collective-permute-start.12 = (bf16[2,64,16,128]{3,2,1,0:T(8,128)(2,1)S(1)}, bf16[2,64,16,128]{3,2,1,0:T(8,128)(2,1)}, u32[]{:S(2)}, u32[]{:S(2)}) collective-permute-start(bf16[2,64,16,128]{3,2,1,0:T(8,128)(2,1)S(1)} %collective-permute-done.11), channel_id=1, source_target_pairs={{0,32},{32,0},{1,33},{33,1},{2,34},{34,2},{3,35},{35,3},{4,36},{36... | collective-permute-start | bytes 1572872 | tf_op jit(solution)/shard_map/ppermute | solution.py:305
  131.6 11.0 %copy-start.11 = (bf16[2,64,16,128]{3,2,1,0:T(8,128)(2,1)}, bf16[2,64,16,128]{3,2,1,0:T(8,128)(2,1)S(1)}, u32[]{:S(2)}) copy-start(bf16[2,64,16,128]{3,2,1,0:T(8,128)(2,1)S(1)} %collective-permute-done.10) | copy-start | bytes 1572868
  131.6 25.2 %collective-permute-start.9 = (bf16[2,64,16,128]{3,2,1,0:T(8,128)(2,1)S(1)}, bf16[2,64,16,128]{3,2,1,0:T(8,128)(2,1)}, u32[]{:S(2)}, u32[]{:S(2)}) collective-permute-start(bf16[2,64,16,128]{3,2,1,0:T(8,128)(2,1)S(1)} %get-tuple-element.17.refs_5_), channel_id=1, source_target_pairs={{0,8},{8,16},{16,24},{24,0},{1,9},{9,17},{17,25},{25,1},{2,10},{10... | collective-permute-start | bytes 1572872 | tf_op jit(solution)/shard_map/ppermute | solution.py:305
  140.3 2.3 %copy-start.21 = (bf16[2,64,16,128]{3,2,1,0:T(8,128)(2,1)}, bf16[2,64,16,128]{3,2,1,0:T(8,128)(2,1)S(1)}, u32[]{:S(2)}) copy-start(bf16[2,64,16,128]{3,2,1,0:T(8,128)(2,1)S(1)} %collective-permute-done.19.refs_6_) | copy-start | bytes 1572868
  140.3 16.5 %collective-permute-start.8 = (bf16[2,64,16,128]{3,2,1,0:T(8,128)(2,1)}, bf16[2,64,16,128]{3,2,1,0:T(8,128)(2,1)}, u32[]{:S(2)}, u32[]{:S(2)}) collective-permute-start(bf16[2,64,16,128]{3,2,1,0:T(8,128)(2,1)} %collective-permute-done.7.refs_6_), channel_id=1, source_target_pairs={{0,24},{8,0},{16,8},{24,16},{1,25},{9,1},{17,9},{25,17},{2,26},{10... | collective-permute-start | bytes 1572872 | tf_op jit(solution)/shard_map/ppermute | solution.py:305
  142.6 0.8 copy-start.12
  143.4 0.8 copy-start.13
Sparse Core Ops, SparseCore 0:
  70.4 33.9 all-gather.2

commit v3 on v2

--- a/solution.py
+++ b/solution.py
@@ -95,17 +95,19 @@
         imag = (both[:, 1, :, :width] - both[:, 0, :, width:]) * scale
         for part, value in enumerate((real, imag)):
             value = value.astype(jnp.bfloat16)
-            for z in range(2):
-                outs[0][z * BANDS + k, :, part] = value
+            for half, out in enumerate(outs):
+                cols = slice(half * LANES, (half + 1) * LANES) if late else slice(None)
+                for z in range(2):
+                    out[z * BANDS + k, :, part] = value[:, :, cols]
 
 
 def filter_transform(late, place, prototype, table, *frames):
     vmem = pl.BlockSpec(memory_space=pltpu.VMEM)
     hbm = pl.BlockSpec(memory_space=pl.ANY)
-    shapes = [(2 * BANDS, INPUTS, 2, HALF, 2 * LANES)]
+    shapes = [(2 * BANDS, INPUTS, 2, HALF, LANES if late else 2 * LANES)] * (1 + late)
     held = [(INPUTS, HALF, 16, LANES)] + [(INPUTS, TAPS - 1, 16, LANES)] * 2
     held = held if late else [(INPUTS, 2 * HALF, 16, LANES)]
-    (blocks,) = pl.pallas_call(
+    return pl.pallas_call(
         functools.partial(filter_transform_kernel, late),
         out_shape=[jax.ShapeDtypeStruct(shape, jnp.bfloat16) for shape in shapes],
         in_specs=[pl.BlockSpec(memory_space=pltpu.SMEM)] + [hbm] * len(frames) + [vmem, hbm],
@@ -125,21 +127,21 @@
         ),
         name="filter_transform",
     )(place, *frames, prototype, table)
-    return blocks
 
 
 def turn_kernel(place_ref, recv_ref, *refs):
-    outs, own_ref, rows = refs[-4:-2], refs[-2], refs[-1]
+    halves = recv_ref.shape[-1] // LANES
+    outs, own_ref, rows = refs[-2 - halves : -2], refs[-2], refs[-1]
     for z in range(2):
         for a in range(INPUTS):
-            for g in range(2):
+            for g in range(halves):
                 cols = slice(g * LANES, (g + 1) * LANES)
                 pieces = [recv_ref[z * BANDS + k, a, c, :, cols] for c in range(2) for k in range(BANDS)]
                 block = jnp.concatenate(pieces, 0).astype(jnp.float32).T
                 for h in range(2):
                     start = (g * 2 + z) * PAIRS * 16 + h * INPUTS + a
                     rows[pl.ds(start, PAIRS, 16), :] = block[h * PAIRS : (h + 1) * PAIRS]
-    for g in range(2):
+    for g in range(halves):
         for z in range(2):
 
             def one(n, carry):
@@ -153,14 +155,15 @@
 
 def turn(place, recv, *tokens):
     vmem = pl.BlockSpec(memory_space=pltpu.VMEM)
-    shapes = [(2, PAIRS, 16, LANES)] * 3
+    halves = recv.shape[-1] // LANES
+    shapes = [(2, PAIRS, 16, LANES)] * halves + [(halves, PAIRS, 16, LANES)]
     return pl.pallas_call(
         turn_kernel,
         out_shape=[jax.ShapeDtypeStruct(shape, jnp.bfloat16) for shape in shapes],
         in_specs=[pl.BlockSpec(memory_space=pltpu.SMEM), vmem]
         + [pl.BlockSpec(memory_space=pl.ANY)] * len(tokens),
         out_specs=[vmem] * len(shapes),
-        scratch_shapes=[pltpu.VMEM((4 * PAIRS * 16, LANES), jnp.float32)],
+        scratch_shapes=[pltpu.VMEM((2 * halves * PAIRS * 16, LANES), jnp.float32)],
         compiler_params=pltpu.CompilerParams(vmem_limit_bytes=32 << 20),
         cost_estimate=pl.CostEstimate(flops=1 << 20, bytes_accessed=4 << 20, transcendentals=0),
         name="turn",
@@ -278,26 +281,10 @@
         input_output_aliases=aliases,
         compiler_params=pltpu.CompilerParams(vmem_limit_bytes=VMEM_LIMIT),
         cost_estimate=pl.CostEstimate(
-            flops=2 * 64 * 128 * 256 * 128, bytes_accessed=12 << 20, transcendentals=0
+            flops=1 << 33, bytes_accessed=12 << 20, transcendentals=0
         ),
         name="correlate",
     )(place, *arrays, *extra)
-
-
-def hold_kernel(*refs):
-    refs[-1][...] = jnp.zeros_like(refs[-1])
-
-
-def hold(*values):
-    return pl.pallas_call(
-        hold_kernel,
-        out_shape=jax.ShapeDtypeStruct((8, LANES), jnp.float32),
-        in_specs=[pl.BlockSpec(memory_space=pl.ANY)] * len(values),
-        out_specs=pl.BlockSpec(memory_space=pltpu.VMEM),
-        compiler_params=pltpu.CompilerParams(vmem_limit_bytes=60 << 20),
-        cost_estimate=pl.CostEstimate(flops=FAR, bytes_accessed=1 << 20, transcendentals=0),
-        name="hold",
-    )(*values)
 
 
 def ring(value, axis, step):
@@ -348,18 +335,23 @@
     exchange = functools.partial(
         lax.all_to_all, axis_name=("zh", "zl"), split_axis=0, concat_axis=0, tiled=True
     )
-    recv, late = lax.optimization_barrier((exchange(early), late))
+    recv, *late = lax.optimization_barrier((exchange(early[0]), *late))
     *halves, own = turn(place, recv)
     right0 = gather_x(own)
     first = [along_y(value, step) for value, step in zip(halves, (1, -1))]
-    near = [value for _, above, _, below in first for value in (above, below)]
-    tokens = hold(*near), hold(first[0][2], first[1][2])
-    *halves, own = turn(place, exchange(late), *tokens)
-    right1 = across_x(own)
-    second = [along_y(value, step) for value, step in zip(halves, (1, -1))]
+    recv, last = lax.optimization_barrier((exchange(late[0]), late[1]))
+
+    value, own = turn(place, recv)
+    second = [along_y(value, -1)]
+    right1 = [across_x(own)]
+
+    value, own = turn(place, exchange(last))
+    second.append(along_y(value, 1))
+    right1.append(across_x(own))
     out = None
     for half in range(2):
-        out = correlate(half, spectra, place, (first[half], second[half]), (right0, right1), out)
+        lefts, rights = (first[half], second[half]), (right0, right1[half])
+        out = correlate(half, spectra, place, lefts, rights, out)
     return out
 
 

time: 177 us -> 168 us (0.949)
  waiting for transfers between devices: 74.4 us -> 58.9 us
  starting transfers between devices: 35.6 us -> 47.2 us
  local copies, waits for them, and re-layouts: 7.24 us -> 3.24 us
    ppermute x19 -> x26, waiting for transfers between devices: 53.4 us -> 27.1 us  [ring(): lax.ppermute(value, axis, [(i, (i + step) % count) for i in range(count)])]
    all_to_all x2 -> x3, waiting for transfers between devices: 20.2 us -> 31.7 us  [the longest x1 20.2 us: shards(): recv, *late = lax.optimization_barrier((exchange(early[0]), *late))]
    ppermute x19 -> x26, starting transfers between devices: 20.4 us -> 29.2 us  [ring(): lax.ppermute(value, axis, [(i, (i + step) % count) for i in range(count)])]
    unnamed x46 -> x28, local copies, waits for them, and re-layouts: 5.51 us -> 1.51 us
    all_to_all x2 -> x3, starting transfers between devices: 13.9 us -> 16.7 us  [the longest x1 9.66 us: shards(): recv, *late = lax.optimization_barrier((exchange(early[0]), *late))]
    pallas_call x2 -> x3, Pallas kernels: 4.54 us -> 4.29 us  [turn(): pl.pallas_call(turn_kernel, out_shape=[jax.ShapeDtypeStruct(shape, jnp.bf...]
  transfers between devices with their start and end apart: 23 -> 31, of which waited for: 9 -> 10; matrix products, arithmetic and copies ran while one was open for 0% -> 0% of each run, Pallas kernels for 17% -> 17%
where the time goes in v3:
time: 168 us; the launch traced here: 167 us
  waiting for transfers between devices  58.9 us (35%)
  starting transfers between devices  47.2 us (28%)
  Pallas kernels  43.9 us (26%)
  between operations  13.7 us (8%)
  local copies, waits for them, and re-layouts  3.24 us (2%)
    ppermute x26, starting transfers between devices, ring(): lax.ppermute(value, axis, [(i, (i + step) % count) for i in range(count)])  29.2 us
    ppermute x26, waiting for transfers between devices, ring(): lax.ppermute(value, axis, [(i, (i + step) % count) for i in range(count)])  27.1 us
    pallas_call x2, Pallas kernels, correlate(): pl.pallas_call(kernel, out_shape=jax.ShapeDtypeStruct((64, 1, 64, 2, 256)...  25.2 us
    all_to_all x1, waiting for transfers between devices, shards(): recv, *late = lax.optimization_barrier((exchange(early[0]), *late))  20.2 us
    pallas_call x2, Pallas kernels, filter_transform(): pl.pallas_call(functools.partial(filter_transform_kernel, late), out_shap...  14.5 us
    all_to_all x1, waiting for transfers between devices, shards(): recv, last = lax.optimization_barrier((exchange(late[0]), late[1]))  11.5 us
    all_to_all x1, starting transfers between devices, shards(): recv, *late = lax.optimization_barrier((exchange(early[0]), *late))  9.66 us
    pallas_call x3, Pallas kernels, turn(): pl.pallas_call(turn_kernel, out_shape=[jax.ShapeDtypeStruct(shape, jnp.bf...  4.29 us
  transfers between devices with their start and end apart: 31, of which 10 were waited for; matrix products, arithmetic and copies ran while one was open for 0% of the time, Pallas kernels for 17%

profile of v3, /device:TPU:2, one launch (start us, length us, event | category | flops | bytes accessed | tf_op | source)
XLA Modules:
  0.0 167.0 jit_solution(2085058532394242372)
XLA Ops:
  6.5 1.1 slice.4
  7.6 1.3 collective-permute-start
  8.9 0.7 stack.47.refs_0_.place_ref
  9.6 7.1 %filter_transform.2 = bf16[8,8,2,16,256]{4,3,2,1,0:T(8,128)(2,1)} custom-call(s32[11]{0:T(128)} %stack.47.refs_0_.place_ref, bf16[8,32,16,128]{3,2,1,0:T(8,128)(2,1)} %bitcast.41, f32[16,1024]{1,0:T(8,128)} %refs_4_.1, bf16[4,1024,512]{2,1,0:T(8,128)(2,1)} %constant.38.clone.refs_3_.refs_5_), custom_call_target="tpu_custom_call" | custom-call | flops 2147483648 | bytes 8388608 | tf_op jit(solution)/shard_map/filter_transform/pallas_call | solution.py:110
  16.7 9.7 %all-to-all-start = ((bf16[8,8,2,16,256]{4,3,2,1,0:T(8,128)(2,1)}), bf16[8,8,2,16,256]{4,3,2,1,0:T(8,128)(2,1)S(1)}, u32[]{:S(2)}, u32[]{:S(2)}) async-start(bf16[8,8,2,16,256]{4,3,2,1,0:T(8,128)(2,1)} %filter_transform.2), calls=%async_computation | async-start | bytes 2097152 | tf_op jit(solution)/shard_map/all_to_all | solution.py:338
  26.4 0.0 all-gather.3.cloned.1.call-start
  26.4 0.8 copy-done.10
  27.2 7.4 %filter_transform.3 = (bf16[8,8,2,16,128]{4,3,2,1,0:T(8,128)(2,1)}, bf16[8,8,2,16,128]{4,3,2,1,0:T(8,128)(2,1)}) custom-call(s32[11]{0:T(128)} %stack.47.refs_0_.place_ref, bf16[8,32,16,128]{3,2,1,0:T(8,128)(2,1)} %bitcast.42, bf16[8,15,16,128]{3,2,1,0:T(8,128)(2,1)} %copy-done.10, bf16[8,15,16,128]{3,2,1,0:T(8,128)(2,1)} %bitcast.45, f32[16,1024]{1,0:T(8,128)} %refs_4_.1, ...), custom_call_target="tpu_custom_call" | custom-call | flops 137438953472 | bytes 8388608 | tf_op jit(solution)/shard_map/filter_transform/pallas_call | solution.py:110
  34.6 20.2 %all-to-all-done.recv_ref = bf16[8,8,2,16,256]{4,3,2,1,0:T(8,128)(2,1)S(1)} async-done(((bf16[8,8,2,16,256]{4,3,2,1,0:T(8,128)(2,1)}), bf16[8,8,2,16,256]{4,3,2,1,0:T(8,128)(2,1)S(1)}, u32[]{:S(2)}, u32[]{:S(2)}) %all-to-all-start) | async-done | bytes 1048608 | tf_op jit(solution)/shard_map/all_to_all | solution.py:338
  54.8 2.3 %turn.3 = (bf16[2,64,16,128]{3,2,1,0:T(8,128)(2,1)S(1)}, bf16[2,64,16,128]{3,2,1,0:T(8,128)(2,1)S(1)}, bf16[2,64,16,128]{3,2,1,0:T(8,128)(2,1)}) custom-call(s32[11]{0:T(128)S(1)} %copy-done, bf16[8,8,2,16,256]{4,3,2,1,0:T(8,128)(2,1)S(1)} %all-to-all-done.recv_ref), custom_call_target="tpu_custom_call" | custom-call | flops 1048576 | bytes 4194304 | tf_op jit(solution)/shard_map/turn/pallas_call | solution.py:160
  57.2 3.5 %all-to-all-start.1 = ((bf16[8,8,2,16,128]{4,3,2,1,0:T(8,128)(2,1)}), bf16[8,8,2,16,128]{4,3,2,1,0:T(8,128)(2,1)S(1)}, u32[]{:S(2)}, u32[]{:S(2)}) async-start(bf16[8,8,2,16,128]{4,3,2,1,0:T(8,128)(2,1)} %get-tuple-element.23), calls=%async_computation.1 | async-start | bytes 1048576 | tf_op jit(solution)/shard_map/all_to_all | solution.py:342
  60.7 3.1 %collective-permute-start.1 = (bf16[2,64,16,128]{3,2,1,0:T(8,128)(2,1)S(1)}, bf16[2,64,16,128]{3,2,1,0:T(8,128)(2,1)}, u32[]{:S(2)}, u32[]{:S(2)}) collective-permute-start(bf16[2,64,16,128]{3,2,1,0:T(8,128)(2,1)S(1)} %get-tuple-element.22.refs_1_), channel_id=1, source_target_pairs={{0,24},{8,0},{16,8},{24,16},{1,25},{9,1},{17,9},{25,17},{2,26},{10... | collective-permute-start | bytes 1572872 | tf_op jit(solution)/shard_map/ppermute | solution.py:292
  63.8 0.6 collective-permute-start.3
  64.4 2.7 %collective-permute-start.14 = (bf16[2,64,16,128]{3,2,1,0:T(8,128)(2,1)S(1)}, bf16[2,64,16,128]{3,2,1,0:T(8,128)(2,1)}, u32[]{:S(2)}, u32[]{:S(2)}) collective-permute-start(bf16[2,64,16,128]{3,2,1,0:T(8,128)(2,1)S(1)} %get-tuple-element.29.refs_0_), channel_id=1, source_target_pairs={{0,24},{8,0},{16,8},{24,16},{1,25},{9,1},{17,9},{25,17},{2,26},{10... | collective-permute-start | bytes 1572872 | tf_op jit(solution)/shard_map/ppermute | solution.py:292
  67.1 11.5 %all-to-all-done.1.recv_ref = bf16[8,8,2,16,128]{4,3,2,1,0:T(8,128)(2,1)S(1)} async-done(((bf16[8,8,2,16,128]{4,3,2,1,0:T(8,128)(2,1)}), bf16[8,8,2,16,128]{4,3,2,1,0:T(8,128)(2,1)S(1)}, u32[]{:S(2)}, u32[]{:S(2)}) %all-to-all-start.1) | async-done | bytes 524320 | tf_op jit(solution)/shard_map/all_to_all | solution.py:342
  78.6 3.5 %all-to-all-start.2 = ((bf16[8,8,2,16,128]{4,3,2,1,0:T(8,128)(2,1)}), bf16[8,8,2,16,128]{4,3,2,1,0:T(8,128)(2,1)S(1)}, u32[]{:S(2)}, u32[]{:S(2)}) async-start(bf16[8,8,2,16,128]{4,3,2,1,0:T(8,128)(2,1)} %get-tuple-element.25), calls=%async_computation.2 | async-start | bytes 1048576 | tf_op jit(solution)/shard_map/all_to_all | solution.py:348
  82.1 3.1 %collective-permute-start.2 = (bf16[2,64,16,128]{3,2,1,0:T(8,128)(2,1)}, bf16[2,64,16,128]{3,2,1,0:T(8,128)(2,1)S(1)}, u32[]{:S(2)}, u32[]{:S(2)}) collective-permute-start(bf16[2,64,16,128]{3,2,1,0:T(8,128)(2,1)} %collective-permute-done.1.refs_2_), channel_id=1, source_target_pairs={{0,24},{8,0},{16,8},{24,16},{1,25},{9,1},{17,9},{25,17},{2,26},{10... | collective-permute-start | bytes 1572872 | tf_op jit(solution)/shard_map/ppermute | solution.py:292
  85.2 1.0 turn.5
  86.2 3.3 %collective-permute-start.17 = (bf16[2,64,16,128]{3,2,1,0:T(8,128)(2,1)S(1)}, bf16[2,64,16,128]{3,2,1,0:T(8,128)(2,1)}, u32[]{:S(2)}, u32[]{:S(2)}) collective-permute-start(bf16[2,64,16,128]{3,2,1,0:T(8,128)(2,1)S(1)} %get-tuple-element.31.refs_4_), channel_id=1, source_target_pairs={{0,24},{8,0},{16,8},{24,16},{1,25},{9,1},{17,9},{25,17},{2,26},{10... | collective-permute-start | bytes 1572872 | tf_op jit(solution)/shard_map/ppermute | solution.py:292
  89.5 1.2 collective-permute-done.3.refs_4_
  90.7 1.5 collective-permute-start.25
  92.2 1.1 collective-permute-start.23
  93.3 5.2 %collective-permute-done.2.refs_3_ = bf16[2,64,16,128]{3,2,1,0:T(8,128)(2,1)S(1)} collective-permute-done((bf16[2,64,16,128]{3,2,1,0:T(8,128)(2,1)}, bf16[2,64,16,128]{3,2,1,0:T(8,128)(2,1)S(1)}, u32[]{:S(2)}, u32[]{:S(2)}) %collective-permute-start.2) | collective-permute-done | bytes 524320 | tf_op jit(solution)/shard_map/ppermute | solution.py:292
  98.5 0.5 collective-permute-start.21
  99.1 2.0 %collective-permute-done.16.refs_2_ = bf16[2,64,16,128]{3,2,1,0:T(8,128)(2,1)S(1)} collective-permute-done((bf16[2,64,16,128]{3,2,1,0:T(8,128)(2,1)}, bf16[2,64,16,128]{3,2,1,0:T(8,128)(2,1)S(1)}, u32[]{:S(2)}, u32[]{:S(2)}) %collective-permute-start.16) | collective-permute-done | bytes 524320 | tf_op jit(solution)/shard_map/ppermute | solution.py:292
  101.0 0.1 collective-permute-start.19
  101.1 7.7 %collective-permute-done.17.refs_5_ = bf16[2,64,16,128]{3,2,1,0:T(8,128)(2,1)} collective-permute-done((bf16[2,64,16,128]{3,2,1,0:T(8,128)(2,1)S(1)}, bf16[2,64,16,128]{3,2,1,0:T(8,128)(2,1)}, u32[]{:S(2)}, u32[]{:S(2)}) %collective-permute-start.17) | collective-permute-done | bytes 524320 | tf_op jit(solution)/shard_map/ppermute | solution.py:292
  108.9 3.8 %collective-permute-start.18 = (bf16[2,64,16,128]{3,2,1,0:T(8,128)(2,1)}, bf16[2,64,16,128]{3,2,1,0:T(8,128)(2,1)}, u32[]{:S(2)}, u32[]{:S(2)}) collective-permute-start(bf16[2,64,16,128]{3,2,1,0:T(8,128)(2,1)} %collective-permute-done.17.refs_5_), channel_id=1, source_target_pairs={{0,24},{8,0},{16,8},{24,16},{1,25},{9,1},{17,9},{25,17},{2,26},{10... | collective-permute-start | bytes 1572872 | tf_op jit(solution)/shard_map/ppermute | solution.py:292
  112.7 0.5 collective-permute-start.24
  113.2 0.2 collective-permute-start.22
  113.4 0.5 copy-done.12
  113.9 1.0 turn.4
  114.9 0.1 collective-permute-start.5
  115.0 1.6 collective-permute-start.12
  116.6 1.1 collective-permute-start.10
  117.7 2.2 %collective-permute-start.8 = (bf16[1,64,16,128]{3,2,1,0:T(8,128)(2,1)S(1)}, bf16[1,64,16,128]{3,2,1,0:T(8,128)(2,1)}, u32[]{:S(2)}, u32[]{:S(2)}) collective-permute-start(bf16[1,64,16,128]{3,2,1,0:T(8,128)(2,1)S(1)} %get-tuple-element.28), channel_id=1, source_target_pairs={{0,192},{64,0},{128,64},{192,128},{1,193},{65,1},{129,65},{193,129... | collective-permute-start | bytes 786440 | tf_op jit(solution)/shard_map/ppermute | solution.py:292
  119.8 3.8 %collective-permute-done.18.refs_6_ = bf16[2,64,16,128]{3,2,1,0:T(8,128)(2,1)} collective-permute-done((bf16[2,64,16,128]{3,2,1,0:T(8,128)(2,1)}, bf16[2,64,16,128]{3,2,1,0:T(8,128)(2,1)}, u32[]{:S(2)}, u32[]{:S(2)}) %collective-permute-start.18) | collective-permute-done | bytes 524320 | tf_op jit(solution)/shard_map/ppermute | solution.py:292
  123.6 0.7 collective-permute-done.12
  124.3 3.2 %collective-permute-start.4 = (bf16[2,64,16,128]{3,2,1,0:T(8,128)(2,1)S(1)}, bf16[2,64,16,128]{3,2,1,0:T(8,128)(2,1)}, u32[]{:S(2)}, u32[]{:S(2)}) collective-permute-start(bf16[2,64,16,128]{3,2,1,0:T(8,128)(2,1)S(1)} %get-tuple-element.26.refs_5_), channel_id=1, source_target_pairs={{0,24},{8,0},{16,8},{24,16},{1,25},{9,1},{17,9},{25,17},{2,26},{10... | collective-permute-start | bytes 1572872 | tf_op jit(solution)/shard_map/ppermute | solution.py:292
  127.5 0.0 collective-permute-start.13
  127.5 3.7 %collective-permute-done.8 = bf16[1,64,16,128]{3,2,1,0:T(8,128)(2,1)} collective-permute-done((bf16[1,64,16,128]{3,2,1,0:T(8,128)(2,1)S(1)}, bf16[1,64,16,128]{3,2,1,0:T(8,128)(2,1)}, u32[]{:S(2)}, u32[]{:S(2)}) %collective-permute-start.8) | collective-permute-done | bytes 262176 | tf_op jit(solution)/shard_map/ppermute | solution.py:292
  131.2 0.5 collective-permute-start.9
  131.7 0.2 copy-done.13
  131.9 0.1 collective-permute-start.6
  132.0 0.0 all-gather.3.cloned.1.call-done
  132.1 12.6 %correlate.2.refs_18_ = f32[64,1,64,2,256]{4,3,2,1,0:T(2,128)} custom-call(s32[11]{0:T(128)} %stack.47.refs_0_.place_ref, bf16[2,64,16,128]{3,2,1,0:T(8,128)(2,1)} %copy-done.2, bf16[2,64,16,128]{3,2,1,0:T(8,128)(2,1)} %collective-permute-done.14.refs_1_, bf16[2,64,16,128]{3,2,1,0:T(8,128)(2,1)} %copy-done.8, ...), custom_call_target="tpu_custom_call" | custom-call | flops 8589934592 | bytes 12582912 | tf_op jit(solution)/shard_map/correlate/pallas_call | solution.py:267
  144.8 2.8 %collective-permute-done.6.refs_7_ = bf16[2,64,16,128]{3,2,1,0:T(8,128)(2,1)} collective-permute-done((bf16[2,64,16,128]{3,2,1,0:T(8,128)(2,1)S(1)}, bf16[2,64,16,128]{3,2,1,0:T(8,128)(2,1)}, u32[]{:S(2)}, u32[]{:S(2)}) %collective-permute-start.6) | collective-permute-done | bytes 524320 | tf_op jit(solution)/shard_map/ppermute | solution.py:292
  147.6 12.6 %correlate.3 = f32[64,1,64,2,256]{4,3,2,1,0:T(2,128)} custom-call(s32[11]{0:T(128)} %stack.47.refs_0_.place_ref, bf16[2,64,16,128]{3,2,1,0:T(8,128)(2,1)} %copy-done.1, bf16[2,64,16,128]{3,2,1,0:T(8,128)(2,1)} %collective-permute-done.1.refs_2_, bf16[2,64,16,128]{3,2,1,0:T(8,128)(2,1)} %copy-done.7, ...), custom_call_target="tpu_custom_call", output_to_operand_aliasing={{}: (18, {})} | custom-call | flops 8589934592 | bytes 12582912 | tf_op jit(solution)/shard_map/correlate/pallas_call | solution.py:267
  (52 shorter events, 0.1 us)
Async XLA Ops:
  7.6 18.8 %collective-permute-start = (bf16[8,15,16,128]{3,2,1,0:T(8,128)(2,1)S(1)}, bf16[8,15,16,128]{3,2,1,0:T(8,128)(2,1)S(1)}, u32[]{:S(2)}, u32[]{:S(2)}) collective-permute-start(bf16[8,15,16,128]{3,2,1,0:T(8,128)(2,1)S(1)} %slice.4), channel_id=1, source_target_pairs={{1,0},{2,1},{3,2},{5,4},{6,5},{7,6},{9,8},{10,9},{11,10},{13,12},{... | collective-permute-start | bytes 1474568 | tf_op jit(solution)/shard_map/ppermute | solution.py:323
  16.7 38.1 %all-to-all-start = ((bf16[8,8,2,16,256]{4,3,2,1,0:T(8,128)(2,1)}), bf16[8,8,2,16,256]{4,3,2,1,0:T(8,128)(2,1)S(1)}, u32[]{:S(2)}, u32[]{:S(2)}) async-start(bf16[8,8,2,16,256]{4,3,2,1,0:T(8,128)(2,1)} %filter_transform.2), calls=%async_computation | async-start | bytes 2097152 | tf_op jit(solution)/shard_map/all_to_all | solution.py:338
  26.4 105.7 %all-gather.3.cloned.1.call-start = ((), (), s32[]{:S(2)}) async-start(), calls=%async_computation.3 | async-start | bytes 4718592 | tf_op jit(solution)/shard_map/all_gather | solution.py:309
  26.4 0.8 copy-start.10
  27.2 27.6 %copy-start = (s32[11]{0:T(128)S(1)}, s32[11]{0:T(128)}, u32[]{:S(2)}) copy-start(s32[11]{0:T(128)} %stack.47.refs_0_.place_ref) | copy-start | bytes 136
  57.1 74.9 %copy-start.2 = (bf16[2,64,16,128]{3,2,1,0:T(8,128)(2,1)}, bf16[2,64,16,128]{3,2,1,0:T(8,128)(2,1)S(1)}, u32[]{:S(2)}) copy-start(bf16[2,64,16,128]{3,2,1,0:T(8,128)(2,1)S(1)} %get-tuple-element.29.refs_0_) | copy-start | bytes 1572868
  57.2 87.5 %copy-start.1 = (bf16[2,64,16,128]{3,2,1,0:T(8,128)(2,1)}, bf16[2,64,16,128]{3,2,1,0:T(8,128)(2,1)S(1)}, u32[]{:S(2)}) copy-start(bf16[2,64,16,128]{3,2,1,0:T(8,128)(2,1)S(1)} %get-tuple-element.22.refs_1_) | copy-start | bytes 1572868
  57.2 21.4 %all-to-all-start.1 = ((bf16[8,8,2,16,128]{4,3,2,1,0:T(8,128)(2,1)}), bf16[8,8,2,16,128]{4,3,2,1,0:T(8,128)(2,1)S(1)}, u32[]{:S(2)}, u32[]{:S(2)}) async-start(bf16[8,8,2,16,128]{4,3,2,1,0:T(8,128)(2,1)} %get-tuple-element.23), calls=%async_computation.1 | async-start | bytes 1048576 | tf_op jit(solution)/shard_map/all_to_all | solution.py:342
  60.7 21.4 %collective-permute-start.1 = (bf16[2,64,16,128]{3,2,1,0:T(8,128)(2,1)S(1)}, bf16[2,64,16,128]{3,2,1,0:T(8,128)(2,1)}, u32[]{:S(2)}, u32[]{:S(2)}) collective-permute-start(bf16[2,64,16,128]{3,2,1,0:T(8,128)(2,1)S(1)} %get-tuple-element.22.refs_1_), channel_id=1, source_target_pairs={{0,24},{8,0},{16,8},{24,16},{1,25},{9,1},{17,9},{25,17},{2,26},{10... | collective-permute-start | bytes 1572872 | tf_op jit(solution)/shard_map/ppermute | solution.py:292
  63.8 21.4 %collective-permute-start.15 = (bf16[2,64,16,128]{3,2,1,0:T(8,128)(2,1)S(1)}, bf16[2,64,16,128]{3,2,1,0:T(8,128)(2,1)}, u32[]{:S(2)}, u32[]{:S(2)}) collective-permute-start(bf16[2,64,16,128]{3,2,1,0:T(8,128)(2,1)S(1)} %get-tuple-element.29.refs_0_), channel_id=1, source_target_pairs={{0,8},{8,16},{16,24},{24,0},{1,9},{9,17},{17,25},{25,1},{2,10},{10... | collective-permute-start | bytes 1572872 | tf_op jit(solution)/shard_map/ppermute | solution.py:292
  63.8 26.9 %collective-permute-start.3 = (bf16[2,64,16,128]{3,2,1,0:T(8,128)(2,1)S(1)}, bf16[2,64,16,128]{3,2,1,0:T(8,128)(2,1)}, u32[]{:S(2)}, u32[]{:S(2)}) collective-permute-start(bf16[2,64,16,128]{3,2,1,0:T(8,128)(2,1)S(1)} %get-tuple-element.22.refs_1_), channel_id=1, source_target_pairs={{0,8},{8,16},{16,24},{24,0},{1,9},{9,17},{17,25},{25,1},{2,10},{10... | collective-permute-start | bytes 1572872 | tf_op jit(solution)/shard_map/ppermute | solution.py:292
  64.4 27.8 %collective-permute-start.14 = (bf16[2,64,16,128]{3,2,1,0:T(8,128)(2,1)S(1)}, bf16[2,64,16,128]{3,2,1,0:T(8,128)(2,1)}, u32[]{:S(2)}, u32[]{:S(2)}) collective-permute-start(bf16[2,64,16,128]{3,2,1,0:T(8,128)(2,1)S(1)} %get-tuple-element.29.refs_0_), channel_id=1, source_target_pairs={{0,24},{8,0},{16,8},{24,16},{1,25},{9,1},{17,9},{25,17},{2,26},{10... | collective-permute-start | bytes 1572872 | tf_op jit(solution)/shard_map/ppermute | solution.py:292
  78.6 35.3 %all-to-all-start.2 = ((bf16[8,8,2,16,128]{4,3,2,1,0:T(8,128)(2,1)}), bf16[8,8,2,16,128]{4,3,2,1,0:T(8,128)(2,1)S(1)}, u32[]{:S(2)}, u32[]{:S(2)}) async-start(bf16[8,8,2,16,128]{4,3,2,1,0:T(8,128)(2,1)} %get-tuple-element.25), calls=%async_computation.2 | async-start | bytes 1048576 | tf_op jit(solution)/shard_map/all_to_all | solution.py:348
  82.1 16.5 %collective-permute-start.2 = (bf16[2,64,16,128]{3,2,1,0:T(8,128)(2,1)}, bf16[2,64,16,128]{3,2,1,0:T(8,128)(2,1)S(1)}, u32[]{:S(2)}, u32[]{:S(2)}) collective-permute-start(bf16[2,64,16,128]{3,2,1,0:T(8,128)(2,1)} %collective-permute-done.1.refs_2_), channel_id=1, source_target_pairs={{0,24},{8,0},{16,8},{24,16},{1,25},{9,1},{17,9},{25,17},{2,26},{10... | collective-permute-start | bytes 1572872 | tf_op jit(solution)/shard_map/ppermute | solution.py:292
  85.2 15.9 %collective-permute-start.16 = (bf16[2,64,16,128]{3,2,1,0:T(8,128)(2,1)}, bf16[2,64,16,128]{3,2,1,0:T(8,128)(2,1)S(1)}, u32[]{:S(2)}, u32[]{:S(2)}) collective-permute-start(bf16[2,64,16,128]{3,2,1,0:T(8,128)(2,1)} %collective-permute-done.15.refs_3_), channel_id=1, source_target_pairs={{0,8},{8,16},{16,24},{24,0},{1,9},{9,17},{17,25},{25,1},{2,10},{10... | collective-permute-start | bytes 1572872 | tf_op jit(solution)/shard_map/ppermute | solution.py:292
  86.2 45.9 %copy-start.3 = (bf16[2,64,16,128]{3,2,1,0:T(8,128)(2,1)}, bf16[2,64,16,128]{3,2,1,0:T(8,128)(2,1)S(1)}, u32[]{:S(2)}) copy-start(bf16[2,64,16,128]{3,2,1,0:T(8,128)(2,1)S(1)} %get-tuple-element.31.refs_4_) | copy-start | bytes 1572868
  86.2 45.9 %copy-start.5 = (bf16[1,64,16,128]{3,2,1,0:T(8,128)(2,1)}, bf16[1,64,16,128]{3,2,1,0:T(8,128)(2,1)S(1)}, u32[]{:S(2)}) copy-start(bf16[1,64,16,128]{3,2,1,0:T(8,128)(2,1)S(1)} %get-tuple-element.32) | copy-start | bytes 786436
  86.2 22.7 %collective-permute-start.17 = (bf16[2,64,16,128]{3,2,1,0:T(8,128)(2,1)S(1)}, bf16[2,64,16,128]{3,2,1,0:T(8,128)(2,1)}, u32[]{:S(2)}, u32[]{:S(2)}) collective-permute-start(bf16[2,64,16,128]{3,2,1,0:T(8,128)(2,1)S(1)} %get-tuple-element.31.refs_4_), channel_id=1, source_target_pairs={{0,24},{8,0},{16,8},{24,16},{1,25},{9,1},{17,9},{25,17},{2,26},{10... | collective-permute-start | bytes 1572872 | tf_op jit(solution)/shard_map/ppermute | solution.py:292
  90.7 10.3 %collective-permute-start.25 = (bf16[1,64,16,128]{3,2,1,0:T(8,128)(2,1)S(1)}, bf16[1,64,16,128]{3,2,1,0:T(8,128)(2,1)S(1)}, u32[]{:S(2)}, u32[]{:S(2)}) collective-permute-start(bf16[1,64,16,128]{3,2,1,0:T(8,128)(2,1)S(1)} %get-tuple-element.32), channel_id=1, source_target_pairs={{0,64},{64,128},{128,192},{192,0},{1,65},{65,129},{129,193},{193,1... | collective-permute-start | bytes 786440 | tf_op jit(solution)/shard_map/ppermute | solution.py:292
  92.2 20.5 %collective-permute-start.23 = (bf16[1,64,16,128]{3,2,1,0:T(8,128)(2,1)S(1)}, bf16[1,64,16,128]{3,2,1,0:T(8,128)(2,1)}, u32[]{:S(2)}, u32[]{:S(2)}) collective-permute-start(bf16[1,64,16,128]{3,2,1,0:T(8,128)(2,1)S(1)} %get-tuple-element.32), channel_id=1, source_target_pairs={{0,128},{64,192},{128,0},{192,64},{1,129},{65,193},{129,1},{193,65... | collective-permute-start | bytes 786440 | tf_op jit(solution)/shard_map/ppermute | solution.py:292
  98.5 14.6 %copy-start.7 = (bf16[2,64,16,128]{3,2,1,0:T(8,128)(2,1)}, bf16[2,64,16,128]{3,2,1,0:T(8,128)(2,1)S(1)}, u32[]{:S(2)}) copy-start(bf16[2,64,16,128]{3,2,1,0:T(8,128)(2,1)S(1)} %collective-permute-done.2.refs_3_) | copy-start | bytes 1572868
  98.5 14.1 %collective-permute-start.21 = (bf16[1,64,16,128]{3,2,1,0:T(8,128)(2,1)S(1)}, bf16[1,64,16,128]{3,2,1,0:T(8,128)(2,1)}, u32[]{:S(2)}, u32[]{:S(2)}) collective-permute-start(bf16[1,64,16,128]{3,2,1,0:T(8,128)(2,1)S(1)} %get-tuple-element.32), channel_id=1, source_target_pairs={{0,192},{64,0},{128,64},{192,128},{1,193},{65,1},{129,65},{193,129... | collective-permute-start | bytes 786440 | tf_op jit(solution)/shard_map/ppermute | solution.py:292
  101.0 12.1 %copy-start.8 = (bf16[2,64,16,128]{3,2,1,0:T(8,128)(2,1)}, bf16[2,64,16,128]{3,2,1,0:T(8,128)(2,1)S(1)}, u32[]{:S(2)}) copy-start(bf16[2,64,16,128]{3,2,1,0:T(8,128)(2,1)S(1)} %collective-permute-done.16.refs_2_) | copy-start | bytes 1572868
  101.0 12.1 %collective-permute-start.20 = (bf16[1,64,16,128]{3,2,1,0:T(8,128)(2,1)S(1)}, bf16[1,64,16,128]{3,2,1,0:T(8,128)(2,1)S(1)}, u32[]{:S(2)}, u32[]{:S(2)}) collective-permute-start(bf16[1,64,16,128]{3,2,1,0:T(8,128)(2,1)S(1)} %get-tuple-element.32), channel_id=1, source_target_pairs={{0,32},{32,0},{1,33},{33,1},{2,34},{34,2},{3,35},{35,3},{4,36},{36... | collective-permute-start | bytes 786440 | tf_op jit(solution)/shard_map/ppermute | solution.py:292
  101.0 31.1 %copy-start.11 = (bf16[1,64,16,128]{3,2,1,0:T(8,128)(2,1)}, bf16[1,64,16,128]{3,2,1,0:T(8,128)(2,1)S(1)}, u32[]{:S(2)}) copy-start(bf16[1,64,16,128]{3,2,1,0:T(8,128)(2,1)S(1)} %collective-permute-done.25) | copy-start | bytes 786436
  101.0 16.6 %collective-permute-start.19 = (bf16[2,64,16,128]{3,2,1,0:T(8,128)(2,1)S(1)}, bf16[2,64,16,128]{3,2,1,0:T(8,128)(2,1)}, u32[]{:S(2)}, u32[]{:S(2)}) collective-permute-start(bf16[2,64,16,128]{3,2,1,0:T(8,128)(2,1)S(1)} %get-tuple-element.31.refs_4_), channel_id=1, source_target_pairs={{0,8},{8,16},{16,24},{24,0},{1,9},{9,17},{17,25},{25,1},{2,10},{10... | collective-permute-start | bytes 1572872 | tf_op jit(solution)/shard_map/ppermute | solution.py:292
  108.9 14.8 %collective-permute-start.18 = (bf16[2,64,16,128]{3,2,1,0:T(8,128)(2,1)}, bf16[2,64,16,128]{3,2,1,0:T(8,128)(2,1)}, u32[]{:S(2)}, u32[]{:S(2)}) collective-permute-start(bf16[2,64,16,128]{3,2,1,0:T(8,128)(2,1)} %collective-permute-done.17.refs_5_), channel_id=1, source_target_pairs={{0,24},{8,0},{16,8},{24,16},{1,25},{9,1},{17,9},{25,17},{2,26},{10... | collective-permute-start | bytes 1572872 | tf_op jit(solution)/shard_map/ppermute | solution.py:292
  112.7 2.2 %collective-permute-start.26 = (bf16[1,64,16,128]{3,2,1,0:T(8,128)(2,1)S(1)}, bf16[1,64,16,128]{3,2,1,0:T(8,128)(2,1)}, u32[]{:S(2)}, u32[]{:S(2)}) collective-permute-start(bf16[1,64,16,128]{3,2,1,0:T(8,128)(2,1)S(1)} %collective-permute-done.25), channel_id=1, source_target_pairs={{0,32},{32,0},{1,33},{33,1},{2,34},{34,2},{3,35},{35,3},{4,36},{36... | collective-permute-start | bytes 786440 | tf_op jit(solution)/shard_map/ppermute | solution.py:292
  112.7 2.3 %collective-permute-start.24 = (bf16[1,64,16,128]{3,2,1,0:T(8,128)(2,1)}, bf16[1,64,16,128]{3,2,1,0:T(8,128)(2,1)}, u32[]{:S(2)}, u32[]{:S(2)}) collective-permute-start(bf16[1,64,16,128]{3,2,1,0:T(8,128)(2,1)} %collective-permute-done.23), channel_id=1, source_target_pairs={{0,32},{32,0},{1,33},{33,1},{2,34},{34,2},{3,35},{35,3},{4,36},{36... | collective-permute-start | bytes 786440 | tf_op jit(solution)/shard_map/ppermute | solution.py:292
  113.2 0.7 copy-start.12
  113.2 3.4 %collective-permute-start.22 = (bf16[1,64,16,128]{3,2,1,0:T(8,128)(2,1)}, bf16[1,64,16,128]{3,2,1,0:T(8,128)(2,1)}, u32[]{:S(2)}, u32[]{:S(2)}) collective-permute-start(bf16[1,64,16,128]{3,2,1,0:T(8,128)(2,1)} %collective-permute-done.21), channel_id=1, source_target_pairs={{0,32},{32,0},{1,33},{33,1},{2,34},{34,2},{3,35},{35,3},{4,36},{36... | collective-permute-start | bytes 786440 | tf_op jit(solution)/shard_map/ppermute | solution.py:292
  114.9 29.8 %copy-start.4 = (bf16[2,64,16,128]{3,2,1,0:T(8,128)(2,1)}, bf16[2,64,16,128]{3,2,1,0:T(8,128)(2,1)S(1)}, u32[]{:S(2)}) copy-start(bf16[2,64,16,128]{3,2,1,0:T(8,128)(2,1)S(1)} %get-tuple-element.26.refs_5_) | copy-start | bytes 1572868
  114.9 29.8 %copy-start.6 = (bf16[1,64,16,128]{3,2,1,0:T(8,128)(2,1)}, bf16[1,64,16,128]{3,2,1,0:T(8,128)(2,1)S(1)}, u32[]{:S(2)}) copy-start(bf16[1,64,16,128]{3,2,1,0:T(8,128)(2,1)S(1)} %get-tuple-element.28) | copy-start | bytes 786436
  114.9 16.8 %collective-permute-start.5 = (bf16[2,64,16,128]{3,2,1,0:T(8,128)(2,1)S(1)}, bf16[2,64,16,128]{3,2,1,0:T(8,128)(2,1)S(1)}, u32[]{:S(2)}, u32[]{:S(2)}) collective-permute-start(bf16[2,64,16,128]{3,2,1,0:T(8,128)(2,1)S(1)} %get-tuple-element.26.refs_5_), channel_id=1, source_target_pairs={{0,8},{8,16},{16,24},{24,0},{1,9},{9,17},{17,25},{25,1},{2,10},{10... | collective-permute-start | bytes 1572872 | tf_op jit(solution)/shard_map/ppermute | solution.py:292
  115.0 9.3 %collective-permute-start.12 = (bf16[1,64,16,128]{3,2,1,0:T(8,128)(2,1)S(1)}, bf16[1,64,16,128]{3,2,1,0:T(8,128)(2,1)}, u32[]{:S(2)}, u32[]{:S(2)}) collective-permute-start(bf16[1,64,16,128]{3,2,1,0:T(8,128)(2,1)S(1)} %get-tuple-element.28), channel_id=1, source_target_pairs={{0,64},{64,128},{128,192},{192,0},{1,65},{65,129},{129,193},{193,1... | collective-permute-start | bytes 786440 | tf_op jit(solution)/shard_map/ppermute | solution.py:292
  116.6 11.0 %collective-permute-start.10 = (bf16[1,64,16,128]{3,2,1,0:T(8,128)(2,1)S(1)}, bf16[1,64,16,128]{3,2,1,0:T(8,128)(2,1)}, u32[]{:S(2)}, u32[]{:S(2)}) collective-permute-start(bf16[1,64,16,128]{3,2,1,0:T(8,128)(2,1)S(1)} %get-tuple-element.28), channel_id=1, source_target_pairs={{0,128},{64,192},{128,0},{192,64},{1,129},{65,193},{129,1},{193,65... | collective-permute-start | bytes 786440 | tf_op jit(solution)/shard_map/ppermute | solution.py:292
  117.7 13.5 %collective-permute-start.8 = (bf16[1,64,16,128]{3,2,1,0:T(8,128)(2,1)S(1)}, bf16[1,64,16,128]{3,2,1,0:T(8,128)(2,1)}, u32[]{:S(2)}, u32[]{:S(2)}) collective-permute-start(bf16[1,64,16,128]{3,2,1,0:T(8,128)(2,1)S(1)} %get-tuple-element.28), channel_id=1, source_target_pairs={{0,192},{64,0},{128,64},{192,128},{1,193},{65,1},{129,65},{193,129... | collective-permute-start | bytes 786440 | tf_op jit(solution)/shard_map/ppermute | solution.py:292
  123.6 7.6 %collective-permute-start.7 = (bf16[1,64,16,128]{3,2,1,0:T(8,128)(2,1)S(1)}, bf16[1,64,16,128]{3,2,1,0:T(8,128)(2,1)S(1)}, u32[]{:S(2)}, u32[]{:S(2)}) collective-permute-start(bf16[1,64,16,128]{3,2,1,0:T(8,128)(2,1)S(1)} %get-tuple-element.28), channel_id=1, source_target_pairs={{0,32},{32,0},{1,33},{33,1},{2,34},{34,2},{3,35},{35,3},{4,36},{36... | collective-permute-start | bytes 786440 | tf_op jit(solution)/shard_map/ppermute | solution.py:292
  124.3 20.4 %collective-permute-start.4 = (bf16[2,64,16,128]{3,2,1,0:T(8,128)(2,1)S(1)}, bf16[2,64,16,128]{3,2,1,0:T(8,128)(2,1)}, u32[]{:S(2)}, u32[]{:S(2)}) collective-permute-start(bf16[2,64,16,128]{3,2,1,0:T(8,128)(2,1)S(1)} %get-tuple-element.26.refs_5_), channel_id=1, source_target_pairs={{0,24},{8,0},{16,8},{24,16},{1,25},{9,1},{17,9},{25,17},{2,26},{10... | collective-permute-start | bytes 1572872 | tf_op jit(solution)/shard_map/ppermute | solution.py:292
  127.5 17.2 %collective-permute-start.13 = (bf16[1,64,16,128]{3,2,1,0:T(8,128)(2,1)}, bf16[1,64,16,128]{3,2,1,0:T(8,128)(2,1)}, u32[]{:S(2)}, u32[]{:S(2)}) collective-permute-start(bf16[1,64,16,128]{3,2,1,0:T(8,128)(2,1)} %collective-permute-done.12), channel_id=1, source_target_pairs={{0,32},{32,0},{1,33},{33,1},{2,34},{34,2},{3,35},{35,3},{4,36},{36... | collective-permute-start | bytes 786440 | tf_op jit(solution)/shard_map/ppermute | solution.py:292
  131.2 13.6 %collective-permute-start.11 = (bf16[1,64,16,128]{3,2,1,0:T(8,128)(2,1)}, bf16[1,64,16,128]{3,2,1,0:T(8,128)(2,1)}, u32[]{:S(2)}, u32[]{:S(2)}) collective-permute-start(bf16[1,64,16,128]{3,2,1,0:T(8,128)(2,1)} %collective-permute-done.10), channel_id=1, source_target_pairs={{0,32},{32,0},{1,33},{33,1},{2,34},{34,2},{3,35},{35,3},{4,36},{36... | collective-permute-start | bytes 786440 | tf_op jit(solution)/shard_map/ppermute | solution.py:292
  131.2 0.7 copy-start.13
  131.2 13.6 %collective-permute-start.9 = (bf16[1,64,16,128]{3,2,1,0:T(8,128)(2,1)}, bf16[1,64,16,128]{3,2,1,0:T(8,128)(2,1)}, u32[]{:S(2)}, u32[]{:S(2)}) collective-permute-start(bf16[1,64,16,128]{3,2,1,0:T(8,128)(2,1)} %collective-permute-done.8), channel_id=1, source_target_pairs={{0,32},{32,0},{1,33},{33,1},{2,34},{34,2},{3,35},{35,3},{4,36},{36... | collective-permute-start | bytes 786440 | tf_op jit(solution)/shard_map/ppermute | solution.py:292
  131.9 12.8 %copy-start.9 = (bf16[2,64,16,128]{3,2,1,0:T(8,128)(2,1)}, bf16[2,64,16,128]{3,2,1,0:T(8,128)(2,1)S(1)}, u32[]{:S(2)}) copy-start(bf16[2,64,16,128]{3,2,1,0:T(8,128)(2,1)S(1)} %collective-permute-done.5.refs_8_) | copy-start | bytes 1572868
  131.9 15.7 %collective-permute-start.6 = (bf16[2,64,16,128]{3,2,1,0:T(8,128)(2,1)S(1)}, bf16[2,64,16,128]{3,2,1,0:T(8,128)(2,1)}, u32[]{:S(2)}, u32[]{:S(2)}) collective-permute-start(bf16[2,64,16,128]{3,2,1,0:T(8,128)(2,1)S(1)} %collective-permute-done.5.refs_8_), channel_id=1, source_target_pairs={{0,8},{8,16},{16,24},{24,0},{1,9},{9,17},{17,25},{25,1},{2,10},{10... | collective-permute-start | bytes 1572872 | tf_op jit(solution)/shard_map/ppermute | solution.py:292
Sparse Core Ops, SparseCore 0:
  57.3 29.9 all-gather.2

commit v4 on v3

--- a/solution.py
+++ b/solution.py
@@ -179,7 +179,7 @@
     step = pl.program_id(0)
     count = PAIRS // STEPS
     lane = lax.broadcasted_iota(jnp.int32, (1, LANES), 1)
-    sign = jnp.where(lane < LANES // 2, -1.0, 1.0)
+    sign = jnp.where(lane < LANES // 2, 1.0, -1.0)
     first = (lane % 16) < 8
 
     def multiply(n, carry):
@@ -192,30 +192,31 @@
         lhs, plain = (
             [jnp.concatenate(found[kind, late], 0) for late in range(2)] for kind in range(2)
         )
-        lhs = jnp.concatenate(lhs, 1)
         turned = [
             (pltpu.roll(p.astype(jnp.float32), LANES // 2, 1) * sign).astype(jnp.bfloat16)
-            for p in plain
+            for p in lhs
         ]
-        rhs = jnp.concatenate([jnp.concatenate(plain, 1), jnp.concatenate(turned, 1)], 0)
+        lhs = jnp.concatenate([jnp.concatenate(lhs, 1), jnp.concatenate(turned, 1)], 0)
         value = lax.dot_general(
-            lhs, rhs, (((1,), (1,)), ((), ())), preferred_element_type=jnp.float32
+            lhs,
+            jnp.concatenate(plain, 1),
+            (((1,), (1,)), ((), ())),
+            preferred_element_type=jnp.float32,
         )
-        value = value.reshape(8, 2, 8, 2 * LANES)
+        value = value.reshape(2, 8, 2, 8, LANES)
         base = (step * count + n) * 64
         for part in range(2):
-            cols = slice(part * LANES, (part + 1) * LANES)
-            kept = jnp.where(first[None], value[:, 0, :, cols], value[:, 1, :, cols])
+            kept = jnp.where(first[None], value[part, :, 0], value[part, :, 1])
             outer[part, pl.ds(pl.multiple_of(base, 64), 64), :] = kept.reshape(64, LANES)
         return carry
 
     @pl.when(step < STEPS)
     def _():
-        lax.fori_loop(0, count, multiply, 0, unroll=16)
+        lax.fori_loop(0, count, multiply, 0, unroll=32)
 
     low = lane < LANES // 2
 
-    def write(i, carry):
+    def write(i):
         place = lax.rem(step - STEPS - place_ref[1] + 4, 4) * 16
         for part in range(2):
             cols = [outer[part, pl.ds(place + z * 8 + i, PAIRS, 64), :] for z in range(2)]
@@ -226,15 +227,15 @@
                 two = block[r * 16 + 8 : r * 16 + 16]
                 near = jnp.where(low, one, pltpu.roll(two, PAIRS, 1))
                 other = jnp.where(low, pltpu.roll(one, PAIRS, 1), two)
-                mixed[0, pl.ds(start, 8, 2), :] = near
-                mixed[1, pl.ds(start, 8, 2), :] = other
+                mixed[i % 2, 0, pl.ds(start, 8, 2), :] = near
+                mixed[i % 2, 1, pl.ds(start, 8, 2), :] = other
         for z in range(2):
-            out_ref[i + z * 8, 0] = mixed[z].reshape(64, 2, LANES)
-        return carry
+            out_ref[i + z * 8, 0] = mixed[i % 2, z].reshape(64, 2, LANES)
 
     @pl.when(step >= STEPS)
     def _():
-        lax.fori_loop(0, 8, write, 0, unroll=4)
+        for i in range(8):
+            write(i)
 
 
 def correlate(half, spectra, place, lefts, rights, previous):
@@ -276,7 +277,7 @@
         ),
         scratch_shapes=[
             pltpu.VMEM((2, PAIRS * 64, LANES), jnp.float32),
-            pltpu.VMEM((2, LANES, LANES), jnp.float32),
+            pltpu.VMEM((2, 2, LANES, LANES), jnp.float32),
         ],
         input_output_aliases=aliases,
         compiler_params=pltpu.CompilerParams(vmem_limit_bytes=VMEM_LIMIT),

time: 168 us -> 167 us (level)
  Pallas kernels: 43.9 us -> 41.7 us
    pallas_call x2, Pallas kernels: 25.2 us -> 23 us  [correlate(): pl.pallas_call(kernel, out_shape=jax.ShapeDtypeStruct((64, 1, 64, 2, 256)...]
where the time goes in v4:
time: 167 us; the launch traced here: 166 us
  waiting for transfers between devices  60 us (36%)
  starting transfers between devices  47.2 us (28%)
  Pallas kernels  41.7 us (25%)
  between operations  13.7 us (8%)
  local copies, waits for them, and re-layouts  3.24 us (2%)
    ppermute x26, starting transfers between devices, ring(): lax.ppermute(value, axis, [(i, (i + step) % count) for i in range(count)])  29.2 us
    ppermute x26, waiting for transfers between devices, ring(): lax.ppermute(value, axis, [(i, (i + step) % count) for i in range(count)])  28.2 us
    pallas_call x2, Pallas kernels, correlate(): pl.pallas_call(kernel, out_shape=jax.ShapeDtypeStruct((64, 1, 64, 2, 256)...  23 us
    all_to_all x1, waiting for transfers between devices, shards(): recv, *late = lax.optimization_barrier((exchange(early[0]), *late))  20.2 us
    pallas_call x2, Pallas kernels, filter_transform(): pl.pallas_call(functools.partial(filter_transform_kernel, late), out_shap...  14.5 us
    all_to_all x1, waiting for transfers between devices, shards(): recv, last = lax.optimization_barrier((exchange(late[0]), late[1]))  11.5 us
    all_to_all x1, starting transfers between devices, shards(): recv, *late = lax.optimization_barrier((exchange(early[0]), *late))  9.66 us
    pallas_call x3, Pallas kernels, turn(): pl.pallas_call(turn_kernel, out_shape=[jax.ShapeDtypeStruct(shape, jnp.bf...  4.29 us
  transfers between devices with their start and end apart: 31, of which 10 were waited for; matrix products, arithmetic and copies ran while one was open for 0% of the time, Pallas kernels for 17%

profile of v4, /device:TPU:2, one launch (start us, length us, event | category | flops | bytes accessed | tf_op | source)
XLA Modules:
  0.0 165.9 jit_solution(5819809393972773874)
XLA Ops:
  6.5 1.1 slice.4
  7.6 1.3 collective-permute-start
  8.9 0.7 stack.47.refs_0_.place_ref
  9.6 7.1 %filter_transform.2 = bf16[8,8,2,16,256]{4,3,2,1,0:T(8,128)(2,1)} custom-call(s32[11]{0:T(128)} %stack.47.refs_0_.place_ref, bf16[8,32,16,128]{3,2,1,0:T(8,128)(2,1)} %bitcast.41, f32[16,1024]{1,0:T(8,128)} %refs_4_.1, bf16[4,1024,512]{2,1,0:T(8,128)(2,1)} %constant.38.clone.refs_3_.refs_5_), custom_call_target="tpu_custom_call" | custom-call | flops 2147483648 | bytes 8388608 | tf_op jit(solution)/shard_map/filter_transform/pallas_call | solution.py:110
  16.7 9.7 %all-to-all-start = ((bf16[8,8,2,16,256]{4,3,2,1,0:T(8,128)(2,1)}), bf16[8,8,2,16,256]{4,3,2,1,0:T(8,128)(2,1)S(1)}, u32[]{:S(2)}, u32[]{:S(2)}) async-start(bf16[8,8,2,16,256]{4,3,2,1,0:T(8,128)(2,1)} %filter_transform.2), calls=%async_computation | async-start | bytes 2097152 | tf_op jit(solution)/shard_map/all_to_all | solution.py:339
  26.4 0.0 all-gather.3.cloned.1.call-start
  26.4 0.8 copy-done.10
  27.2 7.4 %filter_transform.3 = (bf16[8,8,2,16,128]{4,3,2,1,0:T(8,128)(2,1)}, bf16[8,8,2,16,128]{4,3,2,1,0:T(8,128)(2,1)}) custom-call(s32[11]{0:T(128)} %stack.47.refs_0_.place_ref, bf16[8,32,16,128]{3,2,1,0:T(8,128)(2,1)} %bitcast.42, bf16[8,15,16,128]{3,2,1,0:T(8,128)(2,1)} %copy-done.10, bf16[8,15,16,128]{3,2,1,0:T(8,128)(2,1)} %bitcast.45, f32[16,1024]{1,0:T(8,128)} %refs_4_.1, ...), custom_call_target="tpu_custom_call" | custom-call | flops 137438953472 | bytes 8388608 | tf_op jit(solution)/shard_map/filter_transform/pallas_call | solution.py:110
  34.6 20.2 %all-to-all-done.recv_ref = bf16[8,8,2,16,256]{4,3,2,1,0:T(8,128)(2,1)S(1)} async-done(((bf16[8,8,2,16,256]{4,3,2,1,0:T(8,128)(2,1)}), bf16[8,8,2,16,256]{4,3,2,1,0:T(8,128)(2,1)S(1)}, u32[]{:S(2)}, u32[]{:S(2)}) %all-to-all-start) | async-done | bytes 1048608 | tf_op jit(solution)/shard_map/all_to_all | solution.py:339
  54.8 2.3 %turn.3 = (bf16[2,64,16,128]{3,2,1,0:T(8,128)(2,1)S(1)}, bf16[2,64,16,128]{3,2,1,0:T(8,128)(2,1)S(1)}, bf16[2,64,16,128]{3,2,1,0:T(8,128)(2,1)}) custom-call(s32[11]{0:T(128)S(1)} %copy-done, bf16[8,8,2,16,256]{4,3,2,1,0:T(8,128)(2,1)S(1)} %all-to-all-done.recv_ref), custom_call_target="tpu_custom_call" | custom-call | flops 1048576 | bytes 4194304 | tf_op jit(solution)/shard_map/turn/pallas_call | solution.py:160
  57.2 3.5 %all-to-all-start.1 = ((bf16[8,8,2,16,128]{4,3,2,1,0:T(8,128)(2,1)}), bf16[8,8,2,16,128]{4,3,2,1,0:T(8,128)(2,1)S(1)}, u32[]{:S(2)}, u32[]{:S(2)}) async-start(bf16[8,8,2,16,128]{4,3,2,1,0:T(8,128)(2,1)} %get-tuple-element.23), calls=%async_computation.1 | async-start | bytes 1048576 | tf_op jit(solution)/shard_map/all_to_all | solution.py:343
  60.7 3.1 %collective-permute-start.1 = (bf16[2,64,16,128]{3,2,1,0:T(8,128)(2,1)S(1)}, bf16[2,64,16,128]{3,2,1,0:T(8,128)(2,1)}, u32[]{:S(2)}, u32[]{:S(2)}) collective-permute-start(bf16[2,64,16,128]{3,2,1,0:T(8,128)(2,1)S(1)} %get-tuple-element.22.refs_1_), channel_id=1, source_target_pairs={{0,24},{8,0},{16,8},{24,16},{1,25},{9,1},{17,9},{25,17},{2,26},{10... | collective-permute-start | bytes 1572872 | tf_op jit(solution)/shard_map/ppermute | solution.py:293
  63.8 0.6 collective-permute-start.3
  64.4 2.7 %collective-permute-start.14 = (bf16[2,64,16,128]{3,2,1,0:T(8,128)(2,1)S(1)}, bf16[2,64,16,128]{3,2,1,0:T(8,128)(2,1)}, u32[]{:S(2)}, u32[]{:S(2)}) collective-permute-start(bf16[2,64,16,128]{3,2,1,0:T(8,128)(2,1)S(1)} %get-tuple-element.29.refs_0_), channel_id=1, source_target_pairs={{0,24},{8,0},{16,8},{24,16},{1,25},{9,1},{17,9},{25,17},{2,26},{10... | collective-permute-start | bytes 1572872 | tf_op jit(solution)/shard_map/ppermute | solution.py:293
  67.1 11.5 %all-to-all-done.1.recv_ref = bf16[8,8,2,16,128]{4,3,2,1,0:T(8,128)(2,1)S(1)} async-done(((bf16[8,8,2,16,128]{4,3,2,1,0:T(8,128)(2,1)}), bf16[8,8,2,16,128]{4,3,2,1,0:T(8,128)(2,1)S(1)}, u32[]{:S(2)}, u32[]{:S(2)}) %all-to-all-start.1) | async-done | bytes 524320 | tf_op jit(solution)/shard_map/all_to_all | solution.py:343
  78.6 3.5 %all-to-all-start.2 = ((bf16[8,8,2,16,128]{4,3,2,1,0:T(8,128)(2,1)}), bf16[8,8,2,16,128]{4,3,2,1,0:T(8,128)(2,1)S(1)}, u32[]{:S(2)}, u32[]{:S(2)}) async-start(bf16[8,8,2,16,128]{4,3,2,1,0:T(8,128)(2,1)} %get-tuple-element.25), calls=%async_computation.2 | async-start | bytes 1048576 | tf_op jit(solution)/shard_map/all_to_all | solution.py:349
  82.1 3.1 %collective-permute-start.2 = (bf16[2,64,16,128]{3,2,1,0:T(8,128)(2,1)}, bf16[2,64,16,128]{3,2,1,0:T(8,128)(2,1)S(1)}, u32[]{:S(2)}, u32[]{:S(2)}) collective-permute-start(bf16[2,64,16,128]{3,2,1,0:T(8,128)(2,1)} %collective-permute-done.1.refs_2_), channel_id=1, source_target_pairs={{0,24},{8,0},{16,8},{24,16},{1,25},{9,1},{17,9},{25,17},{2,26},{10... | collective-permute-start | bytes 1572872 | tf_op jit(solution)/shard_map/ppermute | solution.py:293
  85.2 1.0 turn.5
  86.2 3.3 %collective-permute-start.17 = (bf16[2,64,16,128]{3,2,1,0:T(8,128)(2,1)S(1)}, bf16[2,64,16,128]{3,2,1,0:T(8,128)(2,1)}, u32[]{:S(2)}, u32[]{:S(2)}) collective-permute-start(bf16[2,64,16,128]{3,2,1,0:T(8,128)(2,1)S(1)} %get-tuple-element.31.refs_4_), channel_id=1, source_target_pairs={{0,24},{8,0},{16,8},{24,16},{1,25},{9,1},{17,9},{25,17},{2,26},{10... | collective-permute-start | bytes 1572872 | tf_op jit(solution)/shard_map/ppermute | solution.py:293
  89.5 1.2 collective-permute-done.3.refs_4_
  90.7 1.5 collective-permute-start.25
  92.2 1.1 collective-permute-start.23
  93.3 5.2 %collective-permute-done.2.refs_3_ = bf16[2,64,16,128]{3,2,1,0:T(8,128)(2,1)S(1)} collective-permute-done((bf16[2,64,16,128]{3,2,1,0:T(8,128)(2,1)}, bf16[2,64,16,128]{3,2,1,0:T(8,128)(2,1)S(1)}, u32[]{:S(2)}, u32[]{:S(2)}) %collective-permute-start.2) | collective-permute-done | bytes 524320 | tf_op jit(solution)/shard_map/ppermute | solution.py:293
  98.5 0.5 collective-permute-start.21
  99.1 2.0 %collective-permute-done.16.refs_2_ = bf16[2,64,16,128]{3,2,1,0:T(8,128)(2,1)S(1)} collective-permute-done((bf16[2,64,16,128]{3,2,1,0:T(8,128)(2,1)}, bf16[2,64,16,128]{3,2,1,0:T(8,128)(2,1)S(1)}, u32[]{:S(2)}, u32[]{:S(2)}) %collective-permute-start.16) | collective-permute-done | bytes 524320 | tf_op jit(solution)/shard_map/ppermute | solution.py:293
  101.0 0.1 collective-permute-start.19
  101.1 7.7 %collective-permute-done.17.refs_5_ = bf16[2,64,16,128]{3,2,1,0:T(8,128)(2,1)} collective-permute-done((bf16[2,64,16,128]{3,2,1,0:T(8,128)(2,1)S(1)}, bf16[2,64,16,128]{3,2,1,0:T(8,128)(2,1)}, u32[]{:S(2)}, u32[]{:S(2)}) %collective-permute-start.17) | collective-permute-done | bytes 524320 | tf_op jit(solution)/shard_map/ppermute | solution.py:293
  108.9 3.8 %collective-permute-start.18 = (bf16[2,64,16,128]{3,2,1,0:T(8,128)(2,1)}, bf16[2,64,16,128]{3,2,1,0:T(8,128)(2,1)}, u32[]{:S(2)}, u32[]{:S(2)}) collective-permute-start(bf16[2,64,16,128]{3,2,1,0:T(8,128)(2,1)} %collective-permute-done.17.refs_5_), channel_id=1, source_target_pairs={{0,24},{8,0},{16,8},{24,16},{1,25},{9,1},{17,9},{25,17},{2,26},{10... | collective-permute-start | bytes 1572872 | tf_op jit(solution)/shard_map/ppermute | solution.py:293
  112.7 0.5 collective-permute-start.24
  113.2 0.2 collective-permute-start.22
  113.4 0.5 copy-done.12
  113.9 1.0 turn.4
  114.9 0.1 collective-permute-start.5
  115.0 1.6 collective-permute-start.12
  116.6 1.1 collective-permute-start.10
  117.7 2.2 %collective-permute-start.8 = (bf16[1,64,16,128]{3,2,1,0:T(8,128)(2,1)S(1)}, bf16[1,64,16,128]{3,2,1,0:T(8,128)(2,1)}, u32[]{:S(2)}, u32[]{:S(2)}) collective-permute-start(bf16[1,64,16,128]{3,2,1,0:T(8,128)(2,1)S(1)} %get-tuple-element.28), channel_id=1, source_target_pairs={{0,192},{64,0},{128,64},{192,128},{1,193},{65,1},{129,65},{193,129... | collective-permute-start | bytes 786440 | tf_op jit(solution)/shard_map/ppermute | solution.py:293
  119.8 3.8 %collective-permute-done.18.refs_6_ = bf16[2,64,16,128]{3,2,1,0:T(8,128)(2,1)} collective-permute-done((bf16[2,64,16,128]{3,2,1,0:T(8,128)(2,1)}, bf16[2,64,16,128]{3,2,1,0:T(8,128)(2,1)}, u32[]{:S(2)}, u32[]{:S(2)}) %collective-permute-start.18) | collective-permute-done | bytes 524320 | tf_op jit(solution)/shard_map/ppermute | solution.py:293
  123.6 0.7 collective-permute-done.12
  124.3 3.2 %collective-permute-start.4 = (bf16[2,64,16,128]{3,2,1,0:T(8,128)(2,1)S(1)}, bf16[2,64,16,128]{3,2,1,0:T(8,128)(2,1)}, u32[]{:S(2)}, u32[]{:S(2)}) collective-permute-start(bf16[2,64,16,128]{3,2,1,0:T(8,128)(2,1)S(1)} %get-tuple-element.26.refs_5_), channel_id=1, source_target_pairs={{0,24},{8,0},{16,8},{24,16},{1,25},{9,1},{17,9},{25,17},{2,26},{10... | collective-permute-start | bytes 1572872 | tf_op jit(solution)/shard_map/ppermute | solution.py:293
  127.5 0.0 collective-permute-start.13
  127.5 3.7 %collective-permute-done.8 = bf16[1,64,16,128]{3,2,1,0:T(8,128)(2,1)} collective-permute-done((bf16[1,64,16,128]{3,2,1,0:T(8,128)(2,1)S(1)}, bf16[1,64,16,128]{3,2,1,0:T(8,128)(2,1)}, u32[]{:S(2)}, u32[]{:S(2)}) %collective-permute-start.8) | collective-permute-done | bytes 262176 | tf_op jit(solution)/shard_map/ppermute | solution.py:293
  131.2 0.5 collective-permute-start.9
  131.7 0.2 copy-done.13
  131.9 0.1 collective-permute-start.6
  132.0 0.0 all-gather.3.cloned.1.call-done
  132.1 11.5 %correlate.2.refs_18_ = f32[64,1,64,2,256]{4,3,2,1,0:T(2,128)} custom-call(s32[11]{0:T(128)} %stack.47.refs_0_.place_ref, bf16[2,64,16,128]{3,2,1,0:T(8,128)(2,1)} %copy-done.2, bf16[2,64,16,128]{3,2,1,0:T(8,128)(2,1)} %collective-permute-done.14.refs_1_, bf16[2,64,16,128]{3,2,1,0:T(8,128)(2,1)} %copy-done.8, ...), custom_call_target="tpu_custom_call" | custom-call | flops 8589934592 | bytes 12582912 | tf_op jit(solution)/shard_map/correlate/pallas_call | solution.py:268
  143.7 3.9 %collective-permute-done.6.refs_7_ = bf16[2,64,16,128]{3,2,1,0:T(8,128)(2,1)} collective-permute-done((bf16[2,64,16,128]{3,2,1,0:T(8,128)(2,1)S(1)}, bf16[2,64,16,128]{3,2,1,0:T(8,128)(2,1)}, u32[]{:S(2)}, u32[]{:S(2)}) %collective-permute-start.6) | collective-permute-done | bytes 524320 | tf_op jit(solution)/shard_map/ppermute | solution.py:293
  147.6 11.5 %correlate.3 = f32[64,1,64,2,256]{4,3,2,1,0:T(2,128)} custom-call(s32[11]{0:T(128)} %stack.47.refs_0_.place_ref, bf16[2,64,16,128]{3,2,1,0:T(8,128)(2,1)} %copy-done.1, bf16[2,64,16,128]{3,2,1,0:T(8,128)(2,1)} %collective-permute-done.1.refs_2_, bf16[2,64,16,128]{3,2,1,0:T(8,128)(2,1)} %copy-done.7, ...), custom_call_target="tpu_custom_call", output_to_operand_aliasing={{}: (18, {})} | custom-call | flops 8589934592 | bytes 12582912 | tf_op jit(solution)/shard_map/correlate/pallas_call | solution.py:268
  (52 shorter events, 0.1 us)
Async XLA Ops:
  7.6 18.8 %collective-permute-start = (bf16[8,15,16,128]{3,2,1,0:T(8,128)(2,1)S(1)}, bf16[8,15,16,128]{3,2,1,0:T(8,128)(2,1)S(1)}, u32[]{:S(2)}, u32[]{:S(2)}) collective-permute-start(bf16[8,15,16,128]{3,2,1,0:T(8,128)(2,1)S(1)} %slice.4), channel_id=1, source_target_pairs={{1,0},{2,1},{3,2},{5,4},{6,5},{7,6},{9,8},{10,9},{11,10},{13,12},{... | collective-permute-start | bytes 1474568 | tf_op jit(solution)/shard_map/ppermute | solution.py:324
  16.7 38.1 %all-to-all-start = ((bf16[8,8,2,16,256]{4,3,2,1,0:T(8,128)(2,1)}), bf16[8,8,2,16,256]{4,3,2,1,0:T(8,128)(2,1)S(1)}, u32[]{:S(2)}, u32[]{:S(2)}) async-start(bf16[8,8,2,16,256]{4,3,2,1,0:T(8,128)(2,1)} %filter_transform.2), calls=%async_computation | async-start | bytes 2097152 | tf_op jit(solution)/shard_map/all_to_all | solution.py:339
  26.4 105.7 %all-gather.3.cloned.1.call-start = ((), (), s32[]{:S(2)}) async-start(), calls=%async_computation.3 | async-start | bytes 4718592 | tf_op jit(solution)/shard_map/all_gather | solution.py:310
  26.4 0.8 copy-start.10
  27.2 27.6 %copy-start = (s32[11]{0:T(128)S(1)}, s32[11]{0:T(128)}, u32[]{:S(2)}) copy-start(s32[11]{0:T(128)} %stack.47.refs_0_.place_ref) | copy-start | bytes 136
  57.1 74.9 %copy-start.2 = (bf16[2,64,16,128]{3,2,1,0:T(8,128)(2,1)}, bf16[2,64,16,128]{3,2,1,0:T(8,128)(2,1)S(1)}, u32[]{:S(2)}) copy-start(bf16[2,64,16,128]{3,2,1,0:T(8,128)(2,1)S(1)} %get-tuple-element.29.refs_0_) | copy-start | bytes 1572868
  57.2 86.4 %copy-start.1 = (bf16[2,64,16,128]{3,2,1,0:T(8,128)(2,1)}, bf16[2,64,16,128]{3,2,1,0:T(8,128)(2,1)S(1)}, u32[]{:S(2)}) copy-start(bf16[2,64,16,128]{3,2,1,0:T(8,128)(2,1)S(1)} %get-tuple-element.22.refs_1_) | copy-start | bytes 1572868
  57.2 21.4 %all-to-all-start.1 = ((bf16[8,8,2,16,128]{4,3,2,1,0:T(8,128)(2,1)}), bf16[8,8,2,16,128]{4,3,2,1,0:T(8,128)(2,1)S(1)}, u32[]{:S(2)}, u32[]{:S(2)}) async-start(bf16[8,8,2,16,128]{4,3,2,1,0:T(8,128)(2,1)} %get-tuple-element.23), calls=%async_computation.1 | async-start | bytes 1048576 | tf_op jit(solution)/shard_map/all_to_all | solution.py:343
  60.7 21.4 %collective-permute-start.1 = (bf16[2,64,16,128]{3,2,1,0:T(8,128)(2,1)S(1)}, bf16[2,64,16,128]{3,2,1,0:T(8,128)(2,1)}, u32[]{:S(2)}, u32[]{:S(2)}) collective-permute-start(bf16[2,64,16,128]{3,2,1,0:T(8,128)(2,1)S(1)} %get-tuple-element.22.refs_1_), channel_id=1, source_target_pairs={{0,24},{8,0},{16,8},{24,16},{1,25},{9,1},{17,9},{25,17},{2,26},{10... | collective-permute-start | bytes 1572872 | tf_op jit(solution)/shard_map/ppermute | solution.py:293
  63.8 21.4 %collective-permute-start.15 = (bf16[2,64,16,128]{3,2,1,0:T(8,128)(2,1)S(1)}, bf16[2,64,16,128]{3,2,1,0:T(8,128)(2,1)}, u32[]{:S(2)}, u32[]{:S(2)}) collective-permute-start(bf16[2,64,16,128]{3,2,1,0:T(8,128)(2,1)S(1)} %get-tuple-element.29.refs_0_), channel_id=1, source_target_pairs={{0,8},{8,16},{16,24},{24,0},{1,9},{9,17},{17,25},{25,1},{2,10},{10... | collective-permute-start | bytes 1572872 | tf_op jit(solution)/shard_map/ppermute | solution.py:293
  63.8 26.9 %collective-permute-start.3 = (bf16[2,64,16,128]{3,2,1,0:T(8,128)(2,1)S(1)}, bf16[2,64,16,128]{3,2,1,0:T(8,128)(2,1)}, u32[]{:S(2)}, u32[]{:S(2)}) collective-permute-start(bf16[2,64,16,128]{3,2,1,0:T(8,128)(2,1)S(1)} %get-tuple-element.22.refs_1_), channel_id=1, source_target_pairs={{0,8},{8,16},{16,24},{24,0},{1,9},{9,17},{17,25},{25,1},{2,10},{10... | collective-permute-start | bytes 1572872 | tf_op jit(solution)/shard_map/ppermute | solution.py:293
  64.4 27.8 %collective-permute-start.14 = (bf16[2,64,16,128]{3,2,1,0:T(8,128)(2,1)S(1)}, bf16[2,64,16,128]{3,2,1,0:T(8,128)(2,1)}, u32[]{:S(2)}, u32[]{:S(2)}) collective-permute-start(bf16[2,64,16,128]{3,2,1,0:T(8,128)(2,1)S(1)} %get-tuple-element.29.refs_0_), channel_id=1, source_target_pairs={{0,24},{8,0},{16,8},{24,16},{1,25},{9,1},{17,9},{25,17},{2,26},{10... | collective-permute-start | bytes 1572872 | tf_op jit(solution)/shard_map/ppermute | solution.py:293
  78.6 35.3 %all-to-all-start.2 = ((bf16[8,8,2,16,128]{4,3,2,1,0:T(8,128)(2,1)}), bf16[8,8,2,16,128]{4,3,2,1,0:T(8,128)(2,1)S(1)}, u32[]{:S(2)}, u32[]{:S(2)}) async-start(bf16[8,8,2,16,128]{4,3,2,1,0:T(8,128)(2,1)} %get-tuple-element.25), calls=%async_computation.2 | async-start | bytes 1048576 | tf_op jit(solution)/shard_map/all_to_all | solution.py:349
  82.1 16.5 %collective-permute-start.2 = (bf16[2,64,16,128]{3,2,1,0:T(8,128)(2,1)}, bf16[2,64,16,128]{3,2,1,0:T(8,128)(2,1)S(1)}, u32[]{:S(2)}, u32[]{:S(2)}) collective-permute-start(bf16[2,64,16,128]{3,2,1,0:T(8,128)(2,1)} %collective-permute-done.1.refs_2_), channel_id=1, source_target_pairs={{0,24},{8,0},{16,8},{24,16},{1,25},{9,1},{17,9},{25,17},{2,26},{10... | collective-permute-start | bytes 1572872 | tf_op jit(solution)/shard_map/ppermute | solution.py:293
  85.2 15.9 %collective-permute-start.16 = (bf16[2,64,16,128]{3,2,1,0:T(8,128)(2,1)}, bf16[2,64,16,128]{3,2,1,0:T(8,128)(2,1)S(1)}, u32[]{:S(2)}, u32[]{:S(2)}) collective-permute-start(bf16[2,64,16,128]{3,2,1,0:T(8,128)(2,1)} %collective-permute-done.15.refs_3_), channel_id=1, source_target_pairs={{0,8},{8,16},{16,24},{24,0},{1,9},{9,17},{17,25},{25,1},{2,10},{10... | collective-permute-start | bytes 1572872 | tf_op jit(solution)/shard_map/ppermute | solution.py:293
  86.2 45.9 %copy-start.3 = (bf16[2,64,16,128]{3,2,1,0:T(8,128)(2,1)}, bf16[2,64,16,128]{3,2,1,0:T(8,128)(2,1)S(1)}, u32[]{:S(2)}) copy-start(bf16[2,64,16,128]{3,2,1,0:T(8,128)(2,1)S(1)} %get-tuple-element.31.refs_4_) | copy-start | bytes 1572868
  86.2 45.9 %copy-start.5 = (bf16[1,64,16,128]{3,2,1,0:T(8,128)(2,1)}, bf16[1,64,16,128]{3,2,1,0:T(8,128)(2,1)S(1)}, u32[]{:S(2)}) copy-start(bf16[1,64,16,128]{3,2,1,0:T(8,128)(2,1)S(1)} %get-tuple-element.32) | copy-start | bytes 786436
  86.2 22.7 %collective-permute-start.17 = (bf16[2,64,16,128]{3,2,1,0:T(8,128)(2,1)S(1)}, bf16[2,64,16,128]{3,2,1,0:T(8,128)(2,1)}, u32[]{:S(2)}, u32[]{:S(2)}) collective-permute-start(bf16[2,64,16,128]{3,2,1,0:T(8,128)(2,1)S(1)} %get-tuple-element.31.refs_4_), channel_id=1, source_target_pairs={{0,24},{8,0},{16,8},{24,16},{1,25},{9,1},{17,9},{25,17},{2,26},{10... | collective-permute-start | bytes 1572872 | tf_op jit(solution)/shard_map/ppermute | solution.py:293
  90.7 10.3 %collective-permute-start.25 = (bf16[1,64,16,128]{3,2,1,0:T(8,128)(2,1)S(1)}, bf16[1,64,16,128]{3,2,1,0:T(8,128)(2,1)S(1)}, u32[]{:S(2)}, u32[]{:S(2)}) collective-permute-start(bf16[1,64,16,128]{3,2,1,0:T(8,128)(2,1)S(1)} %get-tuple-element.32), channel_id=1, source_target_pairs={{0,64},{64,128},{128,192},{192,0},{1,65},{65,129},{129,193},{193,1... | collective-permute-start | bytes 786440 | tf_op jit(solution)/shard_map/ppermute | solution.py:293
  92.2 20.5 %collective-permute-start.23 = (bf16[1,64,16,128]{3,2,1,0:T(8,128)(2,1)S(1)}, bf16[1,64,16,128]{3,2,1,0:T(8,128)(2,1)}, u32[]{:S(2)}, u32[]{:S(2)}) collective-permute-start(bf16[1,64,16,128]{3,2,1,0:T(8,128)(2,1)S(1)} %get-tuple-element.32), channel_id=1, source_target_pairs={{0,128},{64,192},{128,0},{192,64},{1,129},{65,193},{129,1},{193,65... | collective-permute-start | bytes 786440 | tf_op jit(solution)/shard_map/ppermute | solution.py:293
  98.5 14.6 %copy-start.7 = (bf16[2,64,16,128]{3,2,1,0:T(8,128)(2,1)}, bf16[2,64,16,128]{3,2,1,0:T(8,128)(2,1)S(1)}, u32[]{:S(2)}) copy-start(bf16[2,64,16,128]{3,2,1,0:T(8,128)(2,1)S(1)} %collective-permute-done.2.refs_3_) | copy-start | bytes 1572868
  98.5 14.1 %collective-permute-start.21 = (bf16[1,64,16,128]{3,2,1,0:T(8,128)(2,1)S(1)}, bf16[1,64,16,128]{3,2,1,0:T(8,128)(2,1)}, u32[]{:S(2)}, u32[]{:S(2)}) collective-permute-start(bf16[1,64,16,128]{3,2,1,0:T(8,128)(2,1)S(1)} %get-tuple-element.32), channel_id=1, source_target_pairs={{0,192},{64,0},{128,64},{192,128},{1,193},{65,1},{129,65},{193,129... | collective-permute-start | bytes 786440 | tf_op jit(solution)/shard_map/ppermute | solution.py:293
  101.0 12.1 %copy-start.8 = (bf16[2,64,16,128]{3,2,1,0:T(8,128)(2,1)}, bf16[2,64,16,128]{3,2,1,0:T(8,128)(2,1)S(1)}, u32[]{:S(2)}) copy-start(bf16[2,64,16,128]{3,2,1,0:T(8,128)(2,1)S(1)} %collective-permute-done.16.refs_2_) | copy-start | bytes 1572868
  101.0 12.1 %collective-permute-start.20 = (bf16[1,64,16,128]{3,2,1,0:T(8,128)(2,1)S(1)}, bf16[1,64,16,128]{3,2,1,0:T(8,128)(2,1)S(1)}, u32[]{:S(2)}, u32[]{:S(2)}) collective-permute-start(bf16[1,64,16,128]{3,2,1,0:T(8,128)(2,1)S(1)} %get-tuple-element.32), channel_id=1, source_target_pairs={{0,32},{32,0},{1,33},{33,1},{2,34},{34,2},{3,35},{35,3},{4,36},{36... | collective-permute-start | bytes 786440 | tf_op jit(solution)/shard_map/ppermute | solution.py:293
  101.0 31.1 %copy-start.11 = (bf16[1,64,16,128]{3,2,1,0:T(8,128)(2,1)}, bf16[1,64,16,128]{3,2,1,0:T(8,128)(2,1)S(1)}, u32[]{:S(2)}) copy-start(bf16[1,64,16,128]{3,2,1,0:T(8,128)(2,1)S(1)} %collective-permute-done.25) | copy-start | bytes 786436
  101.0 16.6 %collective-permute-start.19 = (bf16[2,64,16,128]{3,2,1,0:T(8,128)(2,1)S(1)}, bf16[2,64,16,128]{3,2,1,0:T(8,128)(2,1)}, u32[]{:S(2)}, u32[]{:S(2)}) collective-permute-start(bf16[2,64,16,128]{3,2,1,0:T(8,128)(2,1)S(1)} %get-tuple-element.31.refs_4_), channel_id=1, source_target_pairs={{0,8},{8,16},{16,24},{24,0},{1,9},{9,17},{17,25},{25,1},{2,10},{10... | collective-permute-start | bytes 1572872 | tf_op jit(solution)/shard_map/ppermute | solution.py:293
  108.9 14.8 %collective-permute-start.18 = (bf16[2,64,16,128]{3,2,1,0:T(8,128)(2,1)}, bf16[2,64,16,128]{3,2,1,0:T(8,128)(2,1)}, u32[]{:S(2)}, u32[]{:S(2)}) collective-permute-start(bf16[2,64,16,128]{3,2,1,0:T(8,128)(2,1)} %collective-permute-done.17.refs_5_), channel_id=1, source_target_pairs={{0,24},{8,0},{16,8},{24,16},{1,25},{9,1},{17,9},{25,17},{2,26},{10... | collective-permute-start | bytes 1572872 | tf_op jit(solution)/shard_map/ppermute | solution.py:293
  112.7 2.2 %collective-permute-start.26 = (bf16[1,64,16,128]{3,2,1,0:T(8,128)(2,1)S(1)}, bf16[1,64,16,128]{3,2,1,0:T(8,128)(2,1)}, u32[]{:S(2)}, u32[]{:S(2)}) collective-permute-start(bf16[1,64,16,128]{3,2,1,0:T(8,128)(2,1)S(1)} %collective-permute-done.25), channel_id=1, source_target_pairs={{0,32},{32,0},{1,33},{33,1},{2,34},{34,2},{3,35},{35,3},{4,36},{36... | collective-permute-start | bytes 786440 | tf_op jit(solution)/shard_map/ppermute | solution.py:293
  112.7 2.3 %collective-permute-start.24 = (bf16[1,64,16,128]{3,2,1,0:T(8,128)(2,1)}, bf16[1,64,16,128]{3,2,1,0:T(8,128)(2,1)}, u32[]{:S(2)}, u32[]{:S(2)}) collective-permute-start(bf16[1,64,16,128]{3,2,1,0:T(8,128)(2,1)} %collective-permute-done.23), channel_id=1, source_target_pairs={{0,32},{32,0},{1,33},{33,1},{2,34},{34,2},{3,35},{35,3},{4,36},{36... | collective-permute-start | bytes 786440 | tf_op jit(solution)/shard_map/ppermute | solution.py:293
  113.2 0.7 copy-start.12
  113.2 3.4 %collective-permute-start.22 = (bf16[1,64,16,128]{3,2,1,0:T(8,128)(2,1)}, bf16[1,64,16,128]{3,2,1,0:T(8,128)(2,1)}, u32[]{:S(2)}, u32[]{:S(2)}) collective-permute-start(bf16[1,64,16,128]{3,2,1,0:T(8,128)(2,1)} %collective-permute-done.21), channel_id=1, source_target_pairs={{0,32},{32,0},{1,33},{33,1},{2,34},{34,2},{3,35},{35,3},{4,36},{36... | collective-permute-start | bytes 786440 | tf_op jit(solution)/shard_map/ppermute | solution.py:293
  114.9 28.7 %copy-start.4 = (bf16[2,64,16,128]{3,2,1,0:T(8,128)(2,1)}, bf16[2,64,16,128]{3,2,1,0:T(8,128)(2,1)S(1)}, u32[]{:S(2)}) copy-start(bf16[2,64,16,128]{3,2,1,0:T(8,128)(2,1)S(1)} %get-tuple-element.26.refs_5_) | copy-start | bytes 1572868
  114.9 28.7 %copy-start.6 = (bf16[1,64,16,128]{3,2,1,0:T(8,128)(2,1)}, bf16[1,64,16,128]{3,2,1,0:T(8,128)(2,1)S(1)}, u32[]{:S(2)}) copy-start(bf16[1,64,16,128]{3,2,1,0:T(8,128)(2,1)S(1)} %get-tuple-element.28) | copy-start | bytes 786436
  114.9 16.8 %collective-permute-start.5 = (bf16[2,64,16,128]{3,2,1,0:T(8,128)(2,1)S(1)}, bf16[2,64,16,128]{3,2,1,0:T(8,128)(2,1)S(1)}, u32[]{:S(2)}, u32[]{:S(2)}) collective-permute-start(bf16[2,64,16,128]{3,2,1,0:T(8,128)(2,1)S(1)} %get-tuple-element.26.refs_5_), channel_id=1, source_target_pairs={{0,8},{8,16},{16,24},{24,0},{1,9},{9,17},{17,25},{25,1},{2,10},{10... | collective-permute-start | bytes 1572872 | tf_op jit(solution)/shard_map/ppermute | solution.py:293
  115.0 9.3 %collective-permute-start.12 = (bf16[1,64,16,128]{3,2,1,0:T(8,128)(2,1)S(1)}, bf16[1,64,16,128]{3,2,1,0:T(8,128)(2,1)}, u32[]{:S(2)}, u32[]{:S(2)}) collective-permute-start(bf16[1,64,16,128]{3,2,1,0:T(8,128)(2,1)S(1)} %get-tuple-element.28), channel_id=1, source_target_pairs={{0,64},{64,128},{128,192},{192,0},{1,65},{65,129},{129,193},{193,1... | collective-permute-start | bytes 786440 | tf_op jit(solution)/shard_map/ppermute | solution.py:293
  116.6 11.0 %collective-permute-start.10 = (bf16[1,64,16,128]{3,2,1,0:T(8,128)(2,1)S(1)}, bf16[1,64,16,128]{3,2,1,0:T(8,128)(2,1)}, u32[]{:S(2)}, u32[]{:S(2)}) collective-permute-start(bf16[1,64,16,128]{3,2,1,0:T(8,128)(2,1)S(1)} %get-tuple-element.28), channel_id=1, source_target_pairs={{0,128},{64,192},{128,0},{192,64},{1,129},{65,193},{129,1},{193,65... | collective-permute-start | bytes 786440 | tf_op jit(solution)/shard_map/ppermute | solution.py:293
  117.7 13.5 %collective-permute-start.8 = (bf16[1,64,16,128]{3,2,1,0:T(8,128)(2,1)S(1)}, bf16[1,64,16,128]{3,2,1,0:T(8,128)(2,1)}, u32[]{:S(2)}, u32[]{:S(2)}) collective-permute-start(bf16[1,64,16,128]{3,2,1,0:T(8,128)(2,1)S(1)} %get-tuple-element.28), channel_id=1, source_target_pairs={{0,192},{64,0},{128,64},{192,128},{1,193},{65,1},{129,65},{193,129... | collective-permute-start | bytes 786440 | tf_op jit(solution)/shard_map/ppermute | solution.py:293
  123.6 7.6 %collective-permute-start.7 = (bf16[1,64,16,128]{3,2,1,0:T(8,128)(2,1)S(1)}, bf16[1,64,16,128]{3,2,1,0:T(8,128)(2,1)S(1)}, u32[]{:S(2)}, u32[]{:S(2)}) collective-permute-start(bf16[1,64,16,128]{3,2,1,0:T(8,128)(2,1)S(1)} %get-tuple-element.28), channel_id=1, source_target_pairs={{0,32},{32,0},{1,33},{33,1},{2,34},{34,2},{3,35},{35,3},{4,36},{36... | collective-permute-start | bytes 786440 | tf_op jit(solution)/shard_map/ppermute | solution.py:293
  124.3 19.3 %collective-permute-start.4 = (bf16[2,64,16,128]{3,2,1,0:T(8,128)(2,1)S(1)}, bf16[2,64,16,128]{3,2,1,0:T(8,128)(2,1)}, u32[]{:S(2)}, u32[]{:S(2)}) collective-permute-start(bf16[2,64,16,128]{3,2,1,0:T(8,128)(2,1)S(1)} %get-tuple-element.26.refs_5_), channel_id=1, source_target_pairs={{0,24},{8,0},{16,8},{24,16},{1,25},{9,1},{17,9},{25,17},{2,26},{10... | collective-permute-start | bytes 1572872 | tf_op jit(solution)/shard_map/ppermute | solution.py:293
  127.5 16.1 %collective-permute-start.13 = (bf16[1,64,16,128]{3,2,1,0:T(8,128)(2,1)}, bf16[1,64,16,128]{3,2,1,0:T(8,128)(2,1)}, u32[]{:S(2)}, u32[]{:S(2)}) collective-permute-start(bf16[1,64,16,128]{3,2,1,0:T(8,128)(2,1)} %collective-permute-done.12), channel_id=1, source_target_pairs={{0,32},{32,0},{1,33},{33,1},{2,34},{34,2},{3,35},{35,3},{4,36},{36... | collective-permute-start | bytes 786440 | tf_op jit(solution)/shard_map/ppermute | solution.py:293
  131.2 12.5 %collective-permute-start.11 = (bf16[1,64,16,128]{3,2,1,0:T(8,128)(2,1)}, bf16[1,64,16,128]{3,2,1,0:T(8,128)(2,1)}, u32[]{:S(2)}, u32[]{:S(2)}) collective-permute-start(bf16[1,64,16,128]{3,2,1,0:T(8,128)(2,1)} %collective-permute-done.10), channel_id=1, source_target_pairs={{0,32},{32,0},{1,33},{33,1},{2,34},{34,2},{3,35},{35,3},{4,36},{36... | collective-permute-start | bytes 786440 | tf_op jit(solution)/shard_map/ppermute | solution.py:293
  131.2 0.7 copy-start.13
  131.2 12.5 %collective-permute-start.9 = (bf16[1,64,16,128]{3,2,1,0:T(8,128)(2,1)}, bf16[1,64,16,128]{3,2,1,0:T(8,128)(2,1)}, u32[]{:S(2)}, u32[]{:S(2)}) collective-permute-start(bf16[1,64,16,128]{3,2,1,0:T(8,128)(2,1)} %collective-permute-done.8), channel_id=1, source_target_pairs={{0,32},{32,0},{1,33},{33,1},{2,34},{34,2},{3,35},{35,3},{4,36},{36... | collective-permute-start | bytes 786440 | tf_op jit(solution)/shard_map/ppermute | solution.py:293
  131.9 11.7 %copy-start.9 = (bf16[2,64,16,128]{3,2,1,0:T(8,128)(2,1)}, bf16[2,64,16,128]{3,2,1,0:T(8,128)(2,1)S(1)}, u32[]{:S(2)}) copy-start(bf16[2,64,16,128]{3,2,1,0:T(8,128)(2,1)S(1)} %collective-permute-done.5.refs_8_) | copy-start | bytes 1572868
  131.9 15.7 %collective-permute-start.6 = (bf16[2,64,16,128]{3,2,1,0:T(8,128)(2,1)S(1)}, bf16[2,64,16,128]{3,2,1,0:T(8,128)(2,1)}, u32[]{:S(2)}, u32[]{:S(2)}) collective-permute-start(bf16[2,64,16,128]{3,2,1,0:T(8,128)(2,1)S(1)} %collective-permute-done.5.refs_8_), channel_id=1, source_target_pairs={{0,8},{8,16},{16,24},{24,0},{1,9},{9,17},{17,25},{25,1},{2,10},{10... | collective-permute-start | bytes 1572872 | tf_op jit(solution)/shard_map/ppermute | solution.py:293
Sparse Core Ops, SparseCore 0:
  57.3 29.9 all-gather.2
